TPU v7x, 32 devices: a whole 2x2x4 slice. The times are simulated.
32 devices in a mesh: dp: 8 (over y, x, core), mp: 4 (over z).
Axes of the slice: x: 2, y: 2, z: 4, core: 2. Of those that a mesh axis runs over, the one named last changes fastest.
Arguments:
- tokens: bfloat16 [2048, 24, 512], P('mp', 'dp'), may hold values from -6 to 6
- pair_ids: int32 [24], P('dp'), may hold values from 0 to 15
- lengths: int32 [24], P('dp'), may hold values from 256 to 2048, as said below
- pair_embed: float32 [16, 512], replicated, may hold values from -3 to 3
- qkv_weight: bfloat16 [512, 1536], P(None, 'mp'), may hold values from -0.25 to 0.25
- q_bias: bfloat16 [512], P('mp'), may hold values from -1.796875 to 1.796875
- v_bias: bfloat16 [512], P('mp'), may hold values from -0.29882812 to 0.29882812
- out_weight: bfloat16 [512, 512], P('mp'), may hold values from -3 to 3
- out_bias: float32 [512], replicated, may hold values from -1.8 to 1.8
- ffn_in_weight: bfloat16 [512, 2048], replicated, may hold values from -0.25 to 0.25
- ffn_in_bias: float32 [2048], replicated, may hold values from -3 to 3
- ffn_out_weight: bfloat16 [2048, 512], replicated, may hold values from -0.125 to 0.125
- ffn_out_bias: float32 [512], replicated, may hold values from -1.8 to 1.8
- cotangent: bfloat16 [2048, 24, 512], P('mp', 'dp'), may hold values from -6 to 6
Outputs:
- out: bfloat16 [2048, 24, 512], P('mp', 'dp')
- tokens_grad: float32 [2048, 24, 512], P('mp', 'dp')
- pair_embed_grad: float32 [16, 512], replicated
- qkv_weight_grad: float32 [512, 1536], P(None, 'mp')
- q_bias_grad: float32 [512], P('mp')
- v_bias_grad: float32 [512], P('mp')
- out_weight_grad: float32 [512, 512], P('mp')
- out_bias_grad: float32 [512], replicated
- ffn_in_weight_grad: float32 [512, 2048], replicated
- ffn_in_bias_grad: float32 [2048], replicated
- ffn_out_weight_grad: float32 [2048, 512], replicated
- ffn_out_bias_grad: float32 [512], replicated
Inputs may be any that keep to these rules, and one draw needn't show every extreme that they name: `lengths`: in every group of 3 consecutive sequences one, drawn from the seed, has exactly 2048 tokens; positions at or after a sequence's length are padding.
All inputs are finite; a program needn't handle non-finite values.
Results may differ from a plain program's by a relative error of at most 0.018.
The roundings to bfloat16 on the way count: a program that leaves them out, or rounds other values in their place, can miss the bound.
Values may be sent and summed in bfloat16 or wider, within the bound.
A program may use at most 256 MiB of HBM per device.

v0:
```python
import jax
import jax.numpy as jnp
from jax import lax
from jax.sharding import PartitionSpec as P

HD = 64


HIGHEST = lax.Precision.HIGHEST
NEGATIVE = -1e30


def contract_rows(left_side, right_side):
    return lax.dot_general(
        left_side, right_side, (((0, 1), (0, 1)), ((), ())), preferred_element_type=jnp.float32
    )


def against_rows(grad_rows, weight):
    return lax.dot_general(
        grad_rows, weight, (((2,), (1,)), ((), ())), preferred_element_type=jnp.float32
    )


def add_bias(projected, query_part, value_part):
    count = query_part.shape[0] // HD
    blank_part = jnp.zeros((count, HD), jnp.float32)
    bias_all = jnp.stack(
        [
            query_part.reshape(count, HD).astype(jnp.float32),
            blank_part,
            value_part.reshape(count, HD).astype(jnp.float32),
        ],
        axis=1,
    )
    shaped = projected.reshape(projected.shape[0], projected.shape[1], count, 3, HD) + bias_all
    return shaped.reshape(projected.shape[0], projected.shape[1], count * 3 * HD).astype(
        jnp.bfloat16
    )


def bias_sums(grad_packed):
    totals = jnp.sum(grad_packed.astype(jnp.float32), axis=(0, 1)).reshape(-1, 3, HD)
    return (totals[:, 0].reshape(-1), totals[:, 2].reshape(-1))


def split_heads(packed):
    length, seqs = (packed.shape[0], packed.shape[1])
    count = packed.shape[2] // (3 * HD)
    ordered = jnp.transpose(packed.reshape(length, seqs, count, 3, HD), (3, 1, 2, 0, 4))
    return (ordered[0], ordered[1], ordered[2])


def attend_forward(queries, keys_all, values_all, seq_length):
    length = queries.shape[0]
    block_rows = min(512, length)
    scale = HD ** (-0.5)
    is_valid = lax.iota(jnp.int32, length) < seq_length

    def forward_block(query_block):
        scores = (
            lax.dot_general(
                query_block, keys_all, (((1,), (1,)), ((), ())), preferred_element_type=jnp.float32
            )
            * scale
        )
        scores = jnp.where(is_valid[None, :], scores, NEGATIVE)
        highest = jnp.max(scores, axis=-1, keepdims=True)
        exponent = jnp.exp(scores - highest)
        total_mass = jnp.sum(exponent, axis=-1, keepdims=True)
        probs = (exponent / total_mass).astype(jnp.bfloat16)
        attended = jnp.dot(probs, values_all, preferred_element_type=jnp.float32)
        return (attended, (highest + jnp.log(total_mass))[:, 0])

    attended, log_total = lax.map(
        forward_block, queries.reshape(length // block_rows, block_rows, HD)
    )
    return (attended.reshape(length, HD), log_total.reshape(length))


def attend_backward(queries, keys_all, values_all, grad_out, log_total, seq_length):
    length = queries.shape[0]
    block_rows = min(512, length)
    scale = HD ** (-0.5)
    is_valid = lax.iota(jnp.int32, length) < seq_length

    def backward_block(carry, block_items):
        query_block, grad_block, total_block = block_items
        scores = (
            lax.dot_general(
                query_block, keys_all, (((1,), (1,)), ((), ())), preferred_element_type=jnp.float32
            )
            * scale
        )
        scores = jnp.where(is_valid[None, :], scores, NEGATIVE)
        probs = jnp.exp(scores - total_block[:, None])
        prob_grad = lax.dot_general(
            grad_block, values_all, (((1,), (1,)), ((), ())), preferred_element_type=jnp.float32
        )
        inner = jnp.sum(probs * prob_grad, axis=-1, keepdims=True)
        score_grad = (probs * (prob_grad - inner)).astype(jnp.bfloat16)
        query_grad = jnp.dot(score_grad, keys_all, preferred_element_type=jnp.float32) * scale
        key_grad = (
            carry[0]
            + lax.dot_general(
                score_grad,
                query_block,
                (((0,), (0,)), ((), ())),
                preferred_element_type=jnp.float32,
            )
            * scale
        )
        value_grad = carry[1] + lax.dot_general(
            probs.astype(jnp.bfloat16),
            grad_block,
            (((0,), (0,)), ((), ())),
            preferred_element_type=jnp.float32,
        )
        return ((key_grad, value_grad), query_grad)

    blocks = length // block_rows
    initial = (jnp.zeros((length, HD), jnp.float32), jnp.zeros((length, HD), jnp.float32))
    (key_grad, value_grad), query_grad = lax.scan(
        backward_block,
        initial,
        (
            queries.reshape(blocks, block_rows, HD),
            grad_out.reshape(blocks, block_rows, HD),
            log_total.reshape(blocks, block_rows),
        ),
    )
    return (query_grad.reshape(length, HD), key_grad, value_grad)


def body(
    tokens,
    pair_ids,
    lengths,
    pair_embed,
    qkv_weight,
    q_bias,
    v_bias,
    out_weight,
    out_bias,
    ffn_in_weight,
    ffn_in_bias,
    ffn_out_weight,
    ffn_out_bias,
    cotangent,
):
    local_rows, seqs, width = tokens.shape
    pairs = pair_embed.shape[0]
    select = (pair_ids[:, None] == lax.iota(jnp.int32, pairs)[None, :]).astype(jnp.float32)
    embed_rows = jnp.dot(select, pair_embed, precision=HIGHEST)
    embedded = tokens.astype(jnp.float32) + embed_rows[None]
    embedded_low = embedded.astype(jnp.bfloat16)
    gathered = lax.all_gather(embedded_low, "mp", axis=0, tiled=True)
    qkv_heads = add_bias(
        jnp.dot(gathered, qkv_weight, preferred_element_type=jnp.float32), q_bias, v_bias
    )
    length = qkv_heads.shape[0]
    heads_dev = qkv_heads.shape[2] // (3 * HD)
    queries, keys_all, values_all = split_heads(qkv_heads)
    run_forward = jax.vmap(jax.vmap(attend_forward, in_axes=(0, 0, 0, None)), in_axes=(0, 0, 0, 0))
    attended, log_total = run_forward(queries, keys_all, values_all, lengths)
    attended_low = (
        jnp.transpose(attended, (2, 0, 1, 3))
        .reshape(length, seqs, heads_dev * HD)
        .astype(jnp.bfloat16)
    )
    rows_part = attended_low
    branch_out = lax.psum_scatter(
        jnp.dot(rows_part, out_weight, preferred_element_type=jnp.float32),
        "mp",
        scatter_dimension=0,
        tiled=True,
    )
    mixed = embedded + (branch_out + out_bias)
    mixed_low = mixed.astype(jnp.bfloat16)
    pre_act = jnp.dot(mixed_low, ffn_in_weight, preferred_element_type=jnp.float32) + ffn_in_bias
    act_low = jax.nn.gelu(pre_act).astype(jnp.bfloat16)
    result = (
        mixed
        + (jnp.dot(act_low, ffn_out_weight, preferred_element_type=jnp.float32) + ffn_out_bias)
    ).astype(jnp.bfloat16)
    ffn_out_grad = contract_rows(act_low, cotangent)
    ffn_out_bias_grad = jnp.sum(cotangent.astype(jnp.float32), axis=(0, 1))
    act_grad = against_rows(cotangent, ffn_out_weight)
    gelu_pull = jax.vjp(jax.nn.gelu, pre_act)[1]
    pre_grad = gelu_pull(act_grad)[0].astype(jnp.bfloat16)
    ffn_in_bias_grad = jnp.sum(pre_grad.astype(jnp.float32), axis=(0, 1))
    ffn_in_grad = contract_rows(mixed_low, pre_grad)
    mixed_grad = (cotangent.astype(jnp.float32) + against_rows(pre_grad, ffn_in_weight)).astype(
        jnp.bfloat16
    )
    out_bias_grad = jnp.sum(mixed_grad.astype(jnp.float32), axis=(0, 1))
    mixed_grad_all = lax.all_gather(mixed_grad, "mp", axis=0, tiled=True)
    out_grad = contract_rows(attended_low, mixed_grad_all)
    attended_grad = against_rows(mixed_grad_all, out_weight).astype(jnp.bfloat16)
    grad_heads = jnp.transpose(attended_grad.reshape(length, seqs, heads_dev, HD), (1, 2, 0, 3))
    run_backward = jax.vmap(
        jax.vmap(attend_backward, in_axes=(0, 0, 0, 0, 0, None)), in_axes=(0, 0, 0, 0, 0, 0)
    )
    query_grad, key_grad, value_grad = run_backward(
        queries, keys_all, values_all, grad_heads, log_total, lengths
    )
    stacked = jnp.stack([query_grad, key_grad, value_grad], axis=0)
    qkv_grad = (
        jnp.transpose(stacked, (3, 1, 2, 0, 4))
        .reshape(length, seqs, heads_dev * 3 * HD)
        .astype(jnp.bfloat16)
    )
    q_bias_grad, v_bias_grad = bias_sums(qkv_grad)
    qkv_full_grad = contract_rows(gathered, qkv_grad)
    rows_part = qkv_grad
    input_part = lax.psum_scatter(
        against_rows(rows_part, qkv_weight).astype(jnp.bfloat16),
        "mp",
        scatter_dimension=0,
        tiled=True,
    ).astype(jnp.float32)
    tokens_grad = mixed_grad.astype(jnp.float32) + input_part
    seq_sums = jnp.sum(tokens_grad, axis=0)
    table_grad = lax.dot_general(select, seq_sums, (((0,), (0,)), ((), ())), precision=HIGHEST)
    qkv_sum, q_bias_sum, v_bias_sum, out_sum = (
        lax.psum(qkv_full_grad.astype(jnp.bfloat16), "dp").astype(jnp.float32),
        lax.psum(q_bias_grad.astype(jnp.bfloat16), "dp").astype(jnp.float32),
        lax.psum(v_bias_grad.astype(jnp.bfloat16), "dp").astype(jnp.float32),
        lax.psum(out_grad.astype(jnp.bfloat16), "dp").astype(jnp.float32),
    )
    ffn_in_sum, ffn_in_bias_sum, ffn_out_sum, ffn_out_bias_sum, out_bias_sum, table_sum = lax.psum(
        (ffn_in_grad, ffn_in_bias_grad, ffn_out_grad, ffn_out_bias_grad, out_bias_grad, table_grad),
        ("dp", "mp"),
    )
    return (
        result,
        tokens_grad,
        table_sum,
        qkv_sum,
        q_bias_sum,
        v_bias_sum,
        out_sum,
        out_bias_sum,
        ffn_in_sum,
        ffn_in_bias_sum,
        ffn_out_sum,
        ffn_out_bias_sum,
    )


def solution(mesh):
    return jax.shard_map(
        body,
        mesh=mesh,
        in_specs=(
            P("mp", "dp", None),
            P("dp"),
            P("dp"),
            P(),
            P(None, "mp"),
            P("mp"),
            P("mp"),
            P("mp", None),
            P(),
            P(),
            P(),
            P(),
            P(),
            P("mp", "dp", None),
        ),
        out_specs=(
            P("mp", "dp", None),
            P("mp", "dp", None),
            P(),
            P(None, "mp"),
            P("mp"),
            P("mp"),
            P("mp", None),
            P(),
            P(),
            P(),
            P(),
            P(),
        ),
        check_vma=False,
    )
```

profile of v0, /device:TPU:0, one launch (start us, length us, event | category | flops | bytes accessed | tf_op | source)
XLA Modules:
  0.0 1412.7 jit_solution(5156554275884018065)
XLA Ops:
  12.3 117.7 %all-gather.3.cloned.1.call-done = bf16[2048,3,512]{2,0,1:T(8,128)(2,1)} async-done(((bf16[512,3,512]{2,0,1:T(8,128)(2,1)}), bf16[2048,3,512]{2,0,1:T(8,128)(2,1)}) %all-gather.3.cloned.1.call-update) | async-done | bytes 6291472 | tf_op jit(solution)/shard_map/all_gather | solution.py:157
  146.4 149.2 %while.28 = (s32[]{:T(128)}, bf16[4,3,2,512,64]{3,4,2,1,0:T(8,128)(2,1)}, f32[4,3,2,512]{3,2,1,0:T(2,128)S(1)}, bf16[4,3,2,512,64]{3,4,2,1,0:T(8,128)(2,1)}, bf1...) while((s32[]{:T(128)}, ...), condition=%wide.region_3.4_spmd.clone, body=%wide.region_0.3_spmd.clone.sunk | while | flops 1686113280 | bytes 98822344 | solution.py:75
  183.8 13.4 fusion.116
  221.1 13.4 fusion.116
  258.4 13.4 fusion.116
  305.2 209.8 %reduce-scatter.3.cloned.1.call-done = f32[512,3,512]{2,0,1:T(8,128)} async-done(((f32[2048,3,512]{2,0,1:T(8,128)}), f32[512,3,512]{2,0,1:T(8,128)}) %reduce-scatter.3.cloned.1.call-update) | async-done | bytes 3145744 | tf_op jit(solution)/shard_map/reduce_scatter | solution.py:172
  522.7 13.6 convert_reduce_fusion
  543.9 116.5 %all-gather.5.cloned.1.call-done = bf16[2048,3,512]{2,0,1:T(8,128)(2,1)} async-done(((bf16[512,3,512]{2,0,1:T(8,128)(2,1)}), bf16[2048,3,512]{2,0,1:T(8,128)(2,1)}) %all-gather.5.cloned.1.call-update) | async-done | bytes 6291472 | tf_op jit(solution)/shard_map/all_gather | solution.py:197
  674.5 347.2 %while.29 = (s32[]{:T(128)}, f32[3,2,2048,64]{2,3,1,0:T(8,128)}, f32[3,2,2048,64]{2,3,1,0:T(8,128)}, bf16[4,3,2,512,64]{3,4,2,1,0:T(8,128)(2,1)}, bf16[4,3,2,512...) while((s32[]{:T(128)}, f32[3,2,2048,64]{2,3,1,0:T(8,128)}, ...), condition=%wide.region_7.8_spmd.clone, body=%wide.region_5.7_spmd.clone.sunk | while | flops 4125035520 | bytes 208515248 | solution.py:123
  710.4 17.1 %multiply_reduce_fusion.2 = (f32[3,2,512]{2,1,0:T(2,128)S(1)}, f32[3,2,512,2048]{3,2,1,0:T(8,128)}) fusion(f32[3,2,512,2048]{3,2,1,0:T(8,128)} %fusion.128, f32[3,2,512]{2,1,0:T(2,128)S(1)} %dynamic-slice_bitcast_fusion.2, pred[3,2048]{1,0:T(4,128)(4,1)S(1)} %iota_compare_fusion.8, bf16[3,2,2048,64]{2,3,1,0:T(8,128)(2,1)} %get-tuple-element.400, ...), kind=kOutput, calls=%fused_computation.19.clone.1 | convolution fusion | flops 836760576 | bytes 52328452 | tf_op jit(solution)/shard_map/vmap(vmap())/while/body/eval_jaxpr/dot_general | solution.py:97
  727.5 21.4 %multiply_convert_fusion.5 = bf16[3,2,512,2048]{3,2,1,0:T(8,128)(2,1)} fusion(f32[3,2,512,2048]{3,2,1,0:T(8,128)} %get-tuple-element.342, f32[3,2,512,2048]{3,2,1,0:T(8,128)} %fusion.128, f32[3,2,512]{2,1,0:T(2,128)S(1)} %get-tuple-element.343, f32[3,2,512]{2,1,0:T(2,128)S(1)} %dynamic-slice_bitcast_fusion.2, pred[3,2048]{1,0:T(4,128)(4,1)S(1)} %iota_compare_fusion.8), kind=kLoop, calls=%fused_computation.18.clone.1 | loop fusion | flops 37748736 | bytes 62945280 | tf_op jit(solution)/shard_map/vmap(vmap())/while/body/eval_jaxpr/convert_element_type | solution.py:101
  780.7 13.7 select_add_fusion.5
  794.3 17.1 %multiply_reduce_fusion.2 = (f32[3,2,512]{2,1,0:T(2,128)S(1)}, f32[3,2,512,2048]{3,2,1,0:T(8,128)}) fusion(f32[3,2,512,2048]{3,2,1,0:T(8,128)} %fusion.128, f32[3,2,512]{2,1,0:T(2,128)S(1)} %dynamic-slice_bitcast_fusion.2, pred[3,2048]{1,0:T(4,128)(4,1)S(1)} %iota_compare_fusion.8, bf16[3,2,2048,64]{2,3,1,0:T(8,128)(2,1)} %get-tuple-element.400, ...), kind=kOutput, calls=%fused_computation.19.clone.1 | convolution fusion | flops 836760576 | bytes 52328452 | tf_op jit(solution)/shard_map/vmap(vmap())/while/body/eval_jaxpr/dot_general | solution.py:97
  811.4 21.4 %multiply_convert_fusion.5 = bf16[3,2,512,2048]{3,2,1,0:T(8,128)(2,1)} fusion(f32[3,2,512,2048]{3,2,1,0:T(8,128)} %get-tuple-element.342, f32[3,2,512,2048]{3,2,1,0:T(8,128)} %fusion.128, f32[3,2,512]{2,1,0:T(2,128)S(1)} %get-tuple-element.343, f32[3,2,512]{2,1,0:T(2,128)S(1)} %dynamic-slice_bitcast_fusion.2, pred[3,2048]{1,0:T(4,128)(4,1)S(1)} %iota_compare_fusion.8), kind=kLoop, calls=%fused_computation.18.clone.1 | loop fusion | flops 37748736 | bytes 62945280 | tf_op jit(solution)/shard_map/vmap(vmap())/while/body/eval_jaxpr/convert_element_type | solution.py:101
  865.4 13.7 select_add_fusion.5
  879.1 17.1 %multiply_reduce_fusion.2 = (f32[3,2,512]{2,1,0:T(2,128)S(1)}, f32[3,2,512,2048]{3,2,1,0:T(8,128)}) fusion(f32[3,2,512,2048]{3,2,1,0:T(8,128)} %fusion.128, f32[3,2,512]{2,1,0:T(2,128)S(1)} %dynamic-slice_bitcast_fusion.2, pred[3,2048]{1,0:T(4,128)(4,1)S(1)} %iota_compare_fusion.8, bf16[3,2,2048,64]{2,3,1,0:T(8,128)(2,1)} %get-tuple-element.400, ...), kind=kOutput, calls=%fused_computation.19.clone.1 | convolution fusion | flops 836760576 | bytes 52328452 | tf_op jit(solution)/shard_map/vmap(vmap())/while/body/eval_jaxpr/dot_general | solution.py:97
  896.2 21.4 %multiply_convert_fusion.5 = bf16[3,2,512,2048]{3,2,1,0:T(8,128)(2,1)} fusion(f32[3,2,512,2048]{3,2,1,0:T(8,128)} %get-tuple-element.342, f32[3,2,512,2048]{3,2,1,0:T(8,128)} %fusion.128, f32[3,2,512]{2,1,0:T(2,128)S(1)} %get-tuple-element.343, f32[3,2,512]{2,1,0:T(2,128)S(1)} %dynamic-slice_bitcast_fusion.2, pred[3,2048]{1,0:T(4,128)(4,1)S(1)} %iota_compare_fusion.8), kind=kLoop, calls=%fused_computation.18.clone.1 | loop fusion | flops 37748736 | bytes 62945280 | tf_op jit(solution)/shard_map/vmap(vmap())/while/body/eval_jaxpr/convert_element_type | solution.py:101
  950.2 13.7 select_add_fusion.5
  963.9 17.1 %multiply_reduce_fusion.2 = (f32[3,2,512]{2,1,0:T(2,128)S(1)}, f32[3,2,512,2048]{3,2,1,0:T(8,128)}) fusion(f32[3,2,512,2048]{3,2,1,0:T(8,128)} %fusion.128, f32[3,2,512]{2,1,0:T(2,128)S(1)} %dynamic-slice_bitcast_fusion.2, pred[3,2048]{1,0:T(4,128)(4,1)S(1)} %iota_compare_fusion.8, bf16[3,2,2048,64]{2,3,1,0:T(8,128)(2,1)} %get-tuple-element.400, ...), kind=kOutput, calls=%fused_computation.19.clone.1 | convolution fusion | flops 836760576 | bytes 52328452 | tf_op jit(solution)/shard_map/vmap(vmap())/while/body/eval_jaxpr/dot_general | solution.py:97
  980.9 21.4 %multiply_convert_fusion.5 = bf16[3,2,512,2048]{3,2,1,0:T(8,128)(2,1)} fusion(f32[3,2,512,2048]{3,2,1,0:T(8,128)} %get-tuple-element.342, f32[3,2,512,2048]{3,2,1,0:T(8,128)} %fusion.128, f32[3,2,512]{2,1,0:T(2,128)S(1)} %get-tuple-element.343, f32[3,2,512]{2,1,0:T(2,128)S(1)} %dynamic-slice_bitcast_fusion.2, pred[3,2048]{1,0:T(4,128)(4,1)S(1)} %iota_compare_fusion.8), kind=kLoop, calls=%fused_computation.18.clone.1 | loop fusion | flops 37748736 | bytes 62945280 | tf_op jit(solution)/shard_map/vmap(vmap())/while/body/eval_jaxpr/convert_element_type | solution.py:101
  1083.5 13.8 all-reduce.2
  1101.9 108.6 %reduce-scatter.5.cloned.1.call-done = bf16[512,3,512]{2,0,1:T(8,128)(2,1)} async-done(((bf16[2048,3,512]{2,0,1:T(8,128)(2,1)}), bf16[512,3,512]{2,0,1:T(8,128)(2,1)}) %reduce-scatter.5.cloned.1.call-update) | async-done | bytes 1572880 | tf_op jit(solution)/shard_map/reduce_scatter | solution.py:216
  1215.0 43.6 %all-reduce = (f32[16,512]{1,0:T(8,128)}, f32[512]{0:T(512)}, f32[2048]{0:T(1024)}, f32[512]{0:T(512)}) all-reduce(f32[16,512]{1,0:T(8,128)S(1)} %fusion.67, f32[512]{0:T(512)S(1)} %get-tuple-element.227, f32[2048]{0:T(1024)S(1)} %copy-done.18, f32[512]{0:T(512)S(1)} %convert_reduce_fusion.2), channel_id=1, replica_groups=mesh['dp'=8,'mp'=4] {'dp','mp'}, use_global_device_ids=true, to_apply=%region_10.11 | all-reduce | flops 11264 | bytes 90112 | tf_op jit(solution)/shard_map/psum | solution.py:231
  1258.6 139.9 %all-reduce.7.cloned.1.call-done = (f32[512,2048]{1,0:T(8,128)}, f32[2048,512]{1,0:T(8,128)}) async-done(((f32[512,2048]{1,0:T(8,128)}, f32[2048,512]{1,0:T(8,128)}), (f32[512,2048]{1,0:T(8,128)}, f32[2048,512]{1,0:T(8,128)})) %all-reduce.7.cloned.1.call-update) | async-done | bytes 8388624 | tf_op jit(solution)/shard_map/psum | solution.py:231
  (180 shorter events, 388.5 us)
Async XLA Ops:
  7.2 515.5 %copy-start = (bf16[2048,512]{1,0:T(8,128)(2,1)S(1)}, bf16[2048,512]{1,0:T(8,128)(2,1)}, u32[]{:S(2)}) copy-start(bf16[2048,512]{1,0:T(8,128)(2,1)} %param.29) | copy-start | bytes 6291460
  7.2 122.9 %copy-start.12 = (bf16[512,384]{1,0:T(8,128)(2,1)S(1)}, bf16[512,384]{1,0:T(8,128)(2,1)}, u32[]{:S(2)}) copy-start(bf16[512,384]{1,0:T(8,128)(2,1)} %param.22) | copy-start | bytes 1179652
  7.2 122.8 %all-gather.3.cloned.1.call-start = ((), (), s32[]{:S(2)}) async-start(), calls=%async_computation.2 | async-start | bytes 7864320 | tf_op jit(solution)/shard_map/all_gather | solution.py:157
  11.9 503.1 %reduce-scatter.3.cloned.1.call-start = ((), (), s32[]{:S(2)}) async-start(), calls=%async_computation.3 | async-start | bytes 15728640 | tf_op jit(solution)/shard_map/reduce_scatter | solution.py:172
  146.4 152.0 %copy-start.11 = (bf16[128,512]{1,0:T(8,128)(2,1)S(1)}, bf16[128,512]{1,0:T(8,128)(2,1)}, u32[]{:S(2)}) copy-start(bf16[128,512]{1,0:T(8,128)(2,1)} %param.25) | copy-start | bytes 393220
  159.9 11.3 copy-start.1
  159.9 11.3 copy-start.5
  197.2 11.3 copy-start.1
  197.2 11.3 copy-start.5
  234.6 11.3 copy-start.1
  234.6 11.3 copy-start.5
  271.9 11.3 copy-start.1
  271.9 11.3 copy-start.5
  304.8 210.2 %copy-start.16 = (f32[3,512]{1,0:T(4,128)S(1)}, f32[3,512]{1,0:T(4,128)}, u32[]{:S(2)}) copy-start(f32[3,512]{1,0:T(4,128)} %copy-done.15) | copy-start | bytes 18436
  304.8 210.2 %copy-start.19 = (f32[512]{0:T(512)S(1)}, f32[512]{0:T(512)}, u32[]{:S(2)}) copy-start(f32[512]{0:T(512)} %param.26) | copy-start | bytes 6148
  304.8 355.5 %all-gather.5.cloned.1.call-start = ((), (), s32[]{:S(2)}) async-start(), calls=%async_computation.4 | async-start | bytes 7864320 | tf_op jit(solution)/shard_map/all_gather | solution.py:197
  522.7 13.6 copy-start.28
  543.8 554.5 %all-reduce.9.cloned.1.call-start = ((), (), s32[]{:S(2)}) async-start(), calls=%async_computation.7 | async-start | bytes 1048576 | tf_op jit(solution)/shard_map/psum | solution.py:226
  1029.3 11.7 slice-start
  1045.3 165.3 %reduce-scatter.5.cloned.1.call-start = ((), (), s32[]{:S(2)}) async-start(), calls=%async_computation.5 | async-start | bytes 7864320 | tf_op jit(solution)/shard_map/reduce_scatter | solution.py:216
  1053.1 9.0 copy-start.23
  1053.1 345.4 %all-reduce.7.cloned.1.call-start = ((), (), s32[]{:S(2)}) async-start(), calls=%async_computation.6 | async-start | bytes 16777216 | tf_op jit(solution)/shard_map/psum | solution.py:231
  1083.4 131.4 %copy-start.27 = (s32[3]{0:T(128)S(1)}, s32[3]{0:T(128)}, u32[]{:S(2)}) copy-start(s32[3]{0:T(128)} %param.19) | copy-start | bytes 40
  1083.4 131.7 %copy-start.18 = (f32[2048]{0:T(1024)S(1)}, f32[2048]{0:T(1024)}, u32[]{:S(2)}) copy-start(f32[2048]{0:T(1024)} %get-tuple-element.230) | copy-start | bytes 24580
  (22 other events, 75.0 us)
Sparse Core Ops, SparseCore 0:
  12.0 118.0 all-gather.2
  304.9 210.0 reduce-scatter.2
  543.9 116.3 all-gather.4
  1045.4 52.8 all-reduce.8
  1100.5 109.9 reduce-scatter.4
  1217.9 180.5 all-reduce.6
where the time goes:
time: 1420 us; the launch traced here: 1410 us
  waiting for transfers between devices  693 us (49%)
  matrix products  440 us (31%)
  other arithmetic  152 us (11%)
  blocking collectives  57.4 us (4%)
  local copies, waits for them, and re-layouts  44.4 us (3%)
  between operations  14.9 us (1%)
    reduce_scatter x1, waiting for transfers between devices, body(): lax.psum_scatter(jnp.dot(rows_part, out_weight, preferred_element_type=jn...  210 us
    psum x1, waiting for transfers between devices, body(): lax.psum((ffn_in_grad, ffn_in_bias_grad, ffn_out_grad, ffn_out_bias_grad,...  140 us
    all_gather x1, waiting for transfers between devices, body(): gathered = lax.all_gather(embedded_low, 'mp', axis=0, tiled=True)  118 us
    all_gather x1, waiting for transfers between devices, body(): mixed_grad_all = lax.all_gather(mixed_grad, 'mp', axis=0, tiled=True)  116 us
    reduce_scatter x1, waiting for transfers between devices, body(): lax.psum_scatter(against_rows(rows_part, qkv_weight).astype(jnp.bfloat16)...  109 us
    convert_element_type x4, other arithmetic, backward_block(): score_grad = (probs * (prob_grad - inner)).astype(jnp.bfloat16)  85.5 us
    dot_general x4, matrix products, backward_block(): lax.dot_general(grad_block, values_all, (((1,), (1,)), ((), ())), preferr...  68.3 us
    dot_general x4, matrix products, forward_block(): lax.dot_general(query_block, keys_all, (((1,), (1,)), ((), ())), preferre...  53.7 us
  transfers between devices with their start and end apart: 6, of which 5 were waited for; matrix products, arithmetic and copies ran while one was open for 3% of the time, Pallas kernels for 0%

commit v1 on v0

v1 whole, which is shorter than its diff:
```python
import functools
import math

import jax
import jax.numpy as jnp
from jax import lax
from jax.experimental import pallas as pl
from jax.experimental.pallas import tpu as pltpu
from jax.sharding import PartitionSpec as P

HD = 64
PAIR = 2 * HD
HIGHEST = lax.Precision.HIGHEST
NEGATIVE = -1e30
LOG2E = math.log2(math.e)
F32 = jnp.float32
BF16 = jnp.bfloat16
VMEM_LIMIT = 56 * 1024 * 1024


def nn(a, b):
    return jnp.dot(a, b, preferred_element_type=F32)


def nt(a, b):
    return lax.dot_general(a, b, (((1,), (1,)), ((), ())), preferred_element_type=F32)


def tn(a, b):
    return lax.dot_general(a, b, (((0,), (0,)), ((), ())), preferred_element_type=F32)


def head_lanes(rows, head):
    lane = lax.broadcasted_iota(jnp.int32, (rows, PAIR), 1)
    return (lane >= head * HD) & (lane < (head + 1) * HD)


def one_head(pair_rows, head):
    return jnp.where(head_lanes(pair_rows.shape[0], head), pair_rows, jnp.zeros_like(pair_rows))


def fold8(values, op):
    rows, lanes = values.shape
    return op(values.reshape(rows // 8, 8, lanes), axis=0)


def attend_forward(length_ref, x_all, x_own, weight, q_bias, v_bias,
                   q_out, k_out, v_out, att_out, att_t_out, lse_out, s_all, acc, *, block):
    length = length_ref[0]
    blocks = (length + block - 1) // block
    rows = x_own.shape[0]
    q_pair = ((nn(x_own[...], weight[0, :, :PAIR]) + q_bias[0]).astype(BF16)) * BF16(HD ** -0.5)
    q_out[0] = q_pair
    q_heads = [one_head(q_pair, 0), one_head(q_pair, 1)]

    def score_step(j, tops):
        at = pl.ds(pl.multiple_of(j * block, block), block)
        kv = nn(x_all[at, :], weight[0, :, PAIR:])
        k_blk = kv[:, :PAIR].astype(BF16)
        k_out[0, at, :] = k_blk
        v_out[0, at, :] = (kv[:, PAIR:] + v_bias[0]).astype(BF16)
        keep = (lax.broadcasted_iota(jnp.int32, (block, rows), 0) + j * block) < length
        new = []
        for h in range(2):
            s = nt(k_blk, q_heads[h]) * LOG2E
            s = jnp.where(keep, s, NEGATIVE)
            s_all[h, at, :] = s
            new.append(jnp.maximum(tops[h], fold8(s, jnp.max)))
        return tuple(new)

    start = jnp.full((8, rows), NEGATIVE, F32)
    tops = lax.fori_loop(0, blocks, score_step, (start, start))
    tops = [jnp.max(t, axis=0, keepdims=True) for t in tops]
    acc[...] = jnp.zeros_like(acc)

    def value_step(j, sums):
        at = pl.ds(pl.multiple_of(j * block, block), block)
        v_blk = v_out[0, at, :]
        new = []
        for h in range(2):
            p = jnp.exp2(s_all[h, at, :] - tops[h])
            new.append(sums[h] + fold8(p, jnp.sum))
            acc[h] += tn(v_blk, p.astype(BF16))
        return tuple(new)

    zero = jnp.zeros((8, rows), F32)
    sums = lax.fori_loop(0, blocks, value_step, (zero, zero))
    sums = [jnp.sum(t, axis=0, keepdims=True) for t in sums]
    att_t = jnp.concatenate([acc[h, h * HD:(h + 1) * HD, :] * (1.0 / sums[h]) for h in range(2)], axis=0)
    att_t_out[0] = att_t
    att_out[...] = att_t.T.astype(BF16)
    lse_out[0] = jnp.concatenate(
        [tops[h] + jnp.log2(sums[h]) for h in range(2)] + [jnp.zeros((6, rows), F32)], axis=0)


def attend_backward(length_ref, place_ref, x_all, x_own, weight, q_in, k_in, v_in, att_t, lse, grad_in,
                    x_grad, w_grad, qb_grad, vb_grad, x_acc, kv_grad, dq_acc, *, block):
    length = length_ref[0]
    blocks = (length + block - 1) // block
    rows = x_own.shape[0]
    pair = pl.program_id(0)
    full = x_all.shape[0]
    q_pair = q_in[0]
    grad_pair = grad_in[...]
    q_heads = [one_head(q_pair, h) for h in range(2)]
    g_heads = [one_head(grad_pair, h) for h in range(2)]
    prod = grad_pair.astype(F32).T * att_t[0]
    delta = [jnp.sum(prod[h * HD:(h + 1) * HD], axis=0, keepdims=True) for h in range(2)]
    tops = [lse[0, h:h + 1, :] for h in range(2)]
    dq_acc[...] = jnp.zeros_like(dq_acc)

    @pl.when(pair == 0)
    def _():
        x_acc[...] = jnp.zeros_like(x_acc)

    w_grad[0] = jnp.zeros(w_grad.shape[1:], F32)

    def step(j, vsum):
        at = pl.ds(pl.multiple_of(j * block, block), block)
        k_blk = k_in[0, at, :]
        v_blk = v_in[0, at, :]
        keep = (lax.broadcasted_iota(jnp.int32, (block, rows), 0) + j * block) < length
        dk = jnp.zeros((block, PAIR), F32)
        dv = jnp.zeros((block, PAIR), F32)
        for h in range(2):
            s = nt(k_blk, q_heads[h]) * LOG2E
            p = jnp.where(keep, jnp.exp2(s - tops[h]), 0.0)
            dp = nt(v_blk, g_heads[h])
            ds = (p * (dp - delta[h])).astype(BF16)
            dv += nn(p.astype(BF16), g_heads[h])
            dk += nn(ds, q_heads[h])
            dq_acc[h] += tn(k_blk, ds)
        dv = dv.astype(BF16)
        both = jnp.concatenate([dk.astype(BF16), dv], axis=1)
        x_acc[at, :] += nt(both, weight[0, :, PAIR:])
        w_grad[0, PAIR:, :] += tn(both, x_all[at, :])
        return vsum + fold8(dv.astype(F32), jnp.sum)

    vsum = lax.fori_loop(0, blocks, step, jnp.zeros((8, PAIR), F32))
    vb_grad[0] = jnp.broadcast_to(jnp.sum(vsum, axis=0, keepdims=True), (8, PAIR))
    dq_t = jnp.concatenate([dq_acc[h, h * HD:(h + 1) * HD, :] for h in range(2)], axis=0) * (HD ** -0.5)
    dq = dq_t.T.astype(BF16)
    qb_grad[0] = jnp.broadcast_to(jnp.sum(dq.astype(F32), axis=0, keepdims=True), (8, PAIR))
    mine = pl.ds(pl.multiple_of(place_ref[0] * rows, rows), rows)
    x_acc[mine, :] += nt(dq, weight[0, :, :PAIR])
    w_grad[0, :PAIR, :] += tn(dq, x_own[...])

    @pl.when(pair == pl.num_programs(0) - 1)
    def _():
        x_grad[...] = x_acc[...].astype(BF16)


def feed_forward(tok, row, att, cot, w_out, b_out, w_in, b_in, w_last, b_last,
                 result, mixed_grad, att_grad, g_last, gb_last, g_in, gb_in, g_out, gb_out,
                 *, chunk):
    first = pl.program_id(0) == 0
    rows, width = tok.shape[1], tok.shape[2]
    hidden = w_in.shape[1]

    @pl.when(first)
    def _():
        for ref in (g_last, gb_last, g_in, gb_in, g_out, gb_out):
            ref[...] = jnp.zeros_like(ref)

    cot_rows = cot[0]
    att_rows = att[0]
    mixed = (tok[0].astype(F32) + row[0]) + (nn(att_rows, w_out[...]) + b_out[...])
    mixed_low = mixed.astype(BF16)
    out_sum = mixed + b_last[...]
    back_sum = cot_rows.astype(F32)
    root = math.sqrt(2.0 / math.pi)
    for c in range(hidden // chunk):
        at = slice(c * chunk, (c + 1) * chunk)
        pre = nn(mixed_low, w_in[:, at]) + b_in[:, at]
        square = pre * pre
        th = jnp.tanh(root * pre * (1.0 + 0.044715 * square))
        half = 0.5 * (1.0 + th)
        act = (pre * half).astype(BF16)
        slope = half + (0.5 * root) * pre * (1.0 - th * th) * (1.0 + (3 * 0.044715) * square)
        out_sum += nn(act, w_last[at, :])
        back = (nt(cot_rows, w_last[at, :]) * slope).astype(BF16)
        gb_in[:, at] += jnp.sum(back.astype(F32), axis=0, keepdims=True)
        back_sum += nt(back, w_in[:, at])
        g_last[at, :] += tn(act, cot_rows)
        g_in[:, at] += tn(mixed_low, back)
    result[0] = out_sum.astype(BF16)
    back_low = back_sum.astype(BF16)
    mixed_grad[0] = back_low
    gb_last[...] += jnp.sum(cot_rows.astype(F32), axis=0, keepdims=True)
    gb_out[...] += jnp.sum(back_low.astype(F32), axis=0, keepdims=True)
    g_out[...] += tn(att_rows, back_low)
    att_grad[0] = nt(back_low, w_out[...]).astype(BF16)


def whole(shape):
    return pl.BlockSpec(shape, lambda *_: (0,) * len(shape))


def call_forward(length, x_all, x_own, weight, q_bias, v_bias):
    full, width = x_all.shape
    rows = x_own.shape[0]
    pairs = weight.shape[0]
    block = min(512, full)
    per_pair = lambda *tail: pl.BlockSpec((1,) + tail, lambda p, *_: (p, 0, 0))
    flops = pairs * (2 * full * width * 2 * PAIR + 8 * full * rows * PAIR)
    return pl.pallas_call(
        functools.partial(attend_forward, block=block),
        grid_spec=pltpu.PrefetchScalarGridSpec(
            num_scalar_prefetch=1,
            grid=(pairs,),
            in_specs=[whole((full, width)), whole((rows, width)), per_pair(width, 3 * PAIR),
                      per_pair(1, PAIR), per_pair(1, PAIR)],
            out_specs=[per_pair(rows, PAIR), per_pair(full, PAIR), per_pair(full, PAIR),
                       pl.BlockSpec((rows, PAIR), lambda p, *_: (0, p)), per_pair(PAIR, rows),
                       per_pair(8, rows)],
            scratch_shapes=[pltpu.VMEM((2, full, rows), F32), pltpu.VMEM((2, PAIR, rows), F32)],
        ),
        out_shape=[
            jax.ShapeDtypeStruct((pairs, rows, PAIR), BF16),
            jax.ShapeDtypeStruct((pairs, full, PAIR), BF16),
            jax.ShapeDtypeStruct((pairs, full, PAIR), BF16),
            jax.ShapeDtypeStruct((rows, pairs * PAIR), BF16),
            jax.ShapeDtypeStruct((pairs, PAIR, rows), F32),
            jax.ShapeDtypeStruct((pairs, 8, rows), F32),
        ],
        cost_estimate=pl.CostEstimate(flops=flops * 2, bytes_accessed=16 << 20,
                                      transcendentals=2 * pairs * full * rows),
        compiler_params=pltpu.CompilerParams(vmem_limit_bytes=VMEM_LIMIT),
        name="attend_forward",
    )(length, x_all, x_own, weight, q_bias, v_bias)


def call_backward(length, place, x_all, x_own, weight, q, k, v, att_t, lse, grad):
    full, width = x_all.shape
    rows = x_own.shape[0]
    pairs = weight.shape[0]
    block = min(512, full)
    per_pair = lambda *tail: pl.BlockSpec((1,) + tail, lambda p, *_: (p, 0, 0))
    return pl.pallas_call(
        functools.partial(attend_backward, block=block),
        grid_spec=pltpu.PrefetchScalarGridSpec(
            num_scalar_prefetch=2,
            grid=(pairs,),
            in_specs=[whole((full, width)), whole((rows, width)), per_pair(width, 3 * PAIR),
                      per_pair(rows, PAIR), per_pair(full, PAIR), per_pair(full, PAIR),
                      per_pair(PAIR, rows), per_pair(8, rows),
                      pl.BlockSpec((rows, PAIR), lambda p, *_: (0, p))],
            out_specs=[whole((full, width)), per_pair(3 * PAIR, width), per_pair(8, PAIR), per_pair(8, PAIR)],
            scratch_shapes=[pltpu.VMEM((full, width), F32), pltpu.VMEM((full, 2 * PAIR), BF16),
                            pltpu.VMEM((2, PAIR, rows), F32)],
        ),
        out_shape=[
            jax.ShapeDtypeStruct((full, width), BF16),
            jax.ShapeDtypeStruct((pairs, 3 * PAIR, width), F32),
            jax.ShapeDtypeStruct((pairs, 8, PAIR), F32),
            jax.ShapeDtypeStruct((pairs, 8, PAIR), F32),
        ],
        cost_estimate=pl.CostEstimate(flops=40 * pairs * full * rows * PAIR, bytes_accessed=16 << 20,
                                      transcendentals=2 * pairs * full * rows),
        compiler_params=pltpu.CompilerParams(vmem_limit_bytes=VMEM_LIMIT),
        name="attend_backward",
    )(length, place, x_all, x_own, weight, q, k, v, att_t, lse, grad)


def call_feed(tok, row, att, cot, w_out, b_out, w_in, b_in, w_last, b_last):
    seqs, rows, width = tok.shape
    hidden = w_in.shape[1]
    per_seq = lambda: pl.BlockSpec((1, rows, width), lambda s: (s, 0, 0))
    return pl.pallas_call(
        functools.partial(feed_forward, chunk=512),
        grid=(seqs,),
        in_specs=[per_seq(), pl.BlockSpec((1, 1, width), lambda s: (s, 0, 0)), per_seq(), per_seq(),
                  whole((width, width)), whole((1, width)), whole((width, hidden)), whole((1, hidden)),
                  whole((hidden, width)), whole((1, width))],
        out_specs=[per_seq(), per_seq(), per_seq(), whole((hidden, width)), whole((1, width)),
                   whole((width, hidden)), whole((1, hidden)), whole((width, width)), whole((1, width))],
        out_shape=[
            jax.ShapeDtypeStruct((seqs, rows, width), BF16),
            jax.ShapeDtypeStruct((seqs, rows, width), BF16),
            jax.ShapeDtypeStruct((seqs, rows, width), BF16),
            jax.ShapeDtypeStruct((hidden, width), F32),
            jax.ShapeDtypeStruct((1, width), F32),
            jax.ShapeDtypeStruct((width, hidden), F32),
            jax.ShapeDtypeStruct((1, hidden), F32),
            jax.ShapeDtypeStruct((width, width), F32),
            jax.ShapeDtypeStruct((1, width), F32),
        ],
        cost_estimate=pl.CostEstimate(flops=seqs * rows * width * (12 * hidden + 6 * width) * 2,
                                      bytes_accessed=16 << 20, transcendentals=seqs * rows * hidden),
        compiler_params=pltpu.CompilerParams(vmem_limit_bytes=VMEM_LIMIT),
        name="feed_forward",
    )(tok, row, att, cot, w_out, b_out, w_in, b_in, w_last, b_last)


def body(
    tokens,
    pair_ids,
    lengths,
    pair_embed,
    qkv_weight,
    q_bias,
    v_bias,
    out_weight,
    out_bias,
    ffn_in_weight,
    ffn_in_bias,
    ffn_out_weight,
    ffn_out_bias,
    cotangent,
):
    local_rows, seqs, width = tokens.shape
    table_rows = pair_embed.shape[0]
    place = lax.axis_index("mp").astype(jnp.int32).reshape(1)
    tok = jnp.transpose(tokens, (1, 0, 2))
    cot = jnp.transpose(cotangent, (1, 0, 2))
    select = (pair_ids[:, None] == lax.iota(jnp.int32, table_rows)[None, :]).astype(F32)
    embed_rows = jnp.dot(select, pair_embed, precision=HIGHEST)
    low = [(tok[s].astype(F32) + embed_rows[s][None]).astype(BF16) for s in range(seqs)]
    gather = lambda v: lax.all_gather(v, "mp", axis=0, tiled=True)

    x_all = [gather(low[s]) for s in range(seqs)]
    w_all = gather(qkv_weight.T)
    qb_all = gather(q_bias)
    vb_all = gather(v_bias)
    out_w_all = gather(out_weight)
    pairs = w_all.shape[0] // (3 * PAIR)
    w_pairs = jnp.transpose(
        w_all.reshape(pairs, 2, 3, HD, width), (0, 4, 2, 1, 3)
    ).reshape(pairs, width, 3 * PAIR)
    qb_pairs = qb_all.astype(F32).reshape(pairs, 1, PAIR)
    vb_pairs = vb_all.astype(F32).reshape(pairs, 1, PAIR)

    fwd = [
        call_forward(lengths[s:s + 1], x_all[s], low[s], w_pairs, qb_pairs, vb_pairs)
        for s in range(seqs)
    ]
    att = jnp.stack([f[3] for f in fwd])
    result, mixed_grad, att_grad, g_last, gb_last, g_in, gb_in, g_out, gb_out = call_feed(
        tok, embed_rows[:, None, :], att, cot, out_w_all, out_bias[None], ffn_in_weight,
        ffn_in_bias[None], ffn_out_weight, ffn_out_bias[None])
    g_last_sum, g_in_sum = lax.psum((g_last.astype(BF16), g_in.astype(BF16)), ("dp", "mp"))
    g_out_own = lax.psum(
        lax.psum_scatter(g_out.astype(BF16), "mp", scatter_dimension=0, tiled=True), "dp")

    token_grads, w_grads, qb_grads, vb_grads = [], [], [], []
    for s in range(seqs):
        q, k, v, _, att_t, lse = fwd[s]
        x_grad, w_grad, qb, vb = call_backward(
            lengths[s:s + 1], place, x_all[s], low[s], w_pairs, q, k, v, att_t, lse, att_grad[s])
        own = lax.psum_scatter(x_grad, "mp", scatter_dimension=0, tiled=True)
        token_grads.append(mixed_grad[s].astype(F32) + own.astype(F32))
        w_grads.append(w_grad)
        qb_grads.append(qb[:, 0])
        vb_grads.append(vb[:, 0])

    w_grad = sum(w_grads).astype(BF16).reshape(pairs, 3, 2, HD, width)
    w_grad = jnp.transpose(w_grad, (0, 2, 1, 3, 4)).reshape(pairs * 2 * 3 * HD, width)
    w_grad = lax.psum(lax.psum_scatter(w_grad, "mp", scatter_dimension=0, tiled=True), "dp")
    qkv_sum = w_grad.astype(F32).T
    seq_sums = jnp.stack([jnp.sum(t, axis=0) for t in token_grads])
    table_grad = lax.dot_general(select, seq_sums, (((0,), (0,)), ((), ())), precision=HIGHEST)
    small = jnp.concatenate([
        table_grad.reshape(-1), sum(qb_grads).reshape(-1), sum(vb_grads).reshape(-1),
        gb_out.reshape(-1), gb_in.reshape(-1), gb_last.reshape(-1)])
    small = lax.psum(small, ("dp", "mp"))
    sizes = [table_grad.size, width, width, width, gb_in.size, width]
    parts, at = [], 0
    for size in sizes:
        parts.append(small[at:at + size])
        at += size
    table_sum, qb_sum, vb_sum, out_bias_sum, in_bias_sum, last_bias_sum = parts
    bias_len = q_bias.shape[0]
    qb_own = lax.dynamic_slice_in_dim(qb_sum, place[0] * bias_len, bias_len)
    vb_own = lax.dynamic_slice_in_dim(vb_sum, place[0] * bias_len, bias_len)
    tokens_grad = jnp.transpose(jnp.stack(token_grads), (1, 0, 2))
    return (
        jnp.transpose(result, (1, 0, 2)),
        tokens_grad,
        table_sum.reshape(table_rows, width),
        qkv_sum,
        qb_own,
        vb_own,
        g_out_own.astype(F32),
        out_bias_sum,
        g_in_sum.astype(F32),
        in_bias_sum,
        g_last_sum.astype(F32),
        last_bias_sum,
    )


def solution(mesh):
    return jax.shard_map(
        body,
        mesh=mesh,
        in_specs=(
            P("mp", "dp", None),
            P("dp"),
            P("dp"),
            P(),
            P(None, "mp"),
            P("mp"),
            P("mp"),
            P("mp", None),
            P(),
            P(),
            P(),
            P(),
            P(),
            P("mp", "dp", None),
        ),
        out_specs=(
            P("mp", "dp", None),
            P("mp", "dp", None),
            P(),
            P(None, "mp"),
            P("mp"),
            P("mp"),
            P("mp", None),
            P(),
            P(),
            P(),
            P(),
            P(),
        ),
        check_vma=False,
    )
```

time: 1420 us -> 802 us (0.56)
  matrix products: 440 us -> 1.12 us
  waiting for transfers between devices: 693 us -> 512 us
  Pallas kernels: 0 us -> 152 us
  other arithmetic: 152 us -> 30.5 us
  local copies, waits for them, and re-layouts: 44.4 us -> 13.9 us
  blocking collectives: 57.4 us -> 82.1 us
    dot_general x40 -> x0, matrix products: 439 us -> none  [the longest x4 68.3 us: backward_block(): lax.dot_general(grad_block, values_all, (((1,), (1,)), ((), ())), preferr...]
    pallas_call x0 -> x7, Pallas kernels: none -> 152 us  [the longest x3 70.5 us: call_backward(): pl.pallas_call(functools.partial(attend_backward, block=block), grid_spec...]
    all_gather x2 -> x4, waiting for transfers between devices: 234 us -> 98.3 us  [body(): gather = lambda v: lax.all_gather(v, 'mp', axis=0, tiled=True)]
    reduce_scatter x2 -> x5, waiting for transfers between devices: 318 us -> 215 us  [the longest x3 133 us: body(): own = lax.psum_scatter(x_grad, 'mp', scatter_dimension=0, tiled=True)]
    convert_element_type x10 -> x8, other arithmetic: 96 us -> 21.7 us  [the longest x1 4.28 us: body(): g_in_sum.astype(F32)]
    psum x2, waiting for transfers between devices: 140 us -> 195 us  [the longest x1 145 us: body(): lax.psum((g_last.astype(BF16), g_in.astype(BF16)), ('dp', 'mp'))]
    reduce_sum x7 -> x1, other arithmetic: 55.1 us -> 2.4 us  [body(): seq_sums = jnp.stack([jnp.sum(t, axis=0) for t in token_grads])]
    all_gather x0 -> x3, blocking collectives: none -> 42.1 us  [body(): gather = lambda v: lax.all_gather(v, 'mp', axis=0, tiled=True)]
  transfers between devices with their start and end apart: 6 -> 11, of which waited for: 5 -> 9; matrix products, arithmetic and copies ran while one was open for 3% -> 4% of each run, Pallas kernels for 0% -> 13%
where the time goes in v1:
time: 802 us; the launch traced here: 806 us
  waiting for transfers between devices  512 us (64%)
  Pallas kernels  152 us (19%)
  blocking collectives  82.1 us (10%)
  other arithmetic  30.5 us (4%)
  between operations  14.2 us (2%)
  local copies, waits for them, and re-layouts  13.9 us (2%)
    psum x1, waiting for transfers between devices, body(): lax.psum((g_last.astype(BF16), g_in.astype(BF16)), ('dp', 'mp'))  145 us
    reduce_scatter x3, waiting for transfers between devices, body(): own = lax.psum_scatter(x_grad, 'mp', scatter_dimension=0, tiled=True)  133 us
    all_gather x4, waiting for transfers between devices, body(): gather = lambda v: lax.all_gather(v, 'mp', axis=0, tiled=True)  98.3 us
    reduce_scatter x1, waiting for transfers between devices, body(): lax.psum_scatter(w_grad, 'mp', scatter_dimension=0, tiled=True)  82.6 us
    pallas_call x3, Pallas kernels, call_backward(): pl.pallas_call(functools.partial(attend_backward, block=block), grid_spec...  70.5 us
    psum x1, waiting for transfers between devices, body(): lax.psum(lax.psum_scatter(w_grad, 'mp', scatter_dimension=0, tiled=True),...  49.8 us
    pallas_call x3, Pallas kernels, call_forward(): pl.pallas_call(functools.partial(attend_forward, block=block), grid_spec=...  48.6 us
    all_gather x3, blocking collectives, body(): gather = lambda v: lax.all_gather(v, 'mp', axis=0, tiled=True)  42.1 us
  transfers between devices with their start and end apart: 11, of which 9 were waited for; matrix products, arithmetic and copies ran while one was open for 4% of the time, Pallas kernels for 13%

profile of v1, /device:TPU:0, one launch (start us, length us, event | category | flops | bytes accessed | tf_op | source)
XLA Modules:
  0.0 805.5 jit_solution(13586476342939852799)
XLA Ops:
  10.1 2.6 fusion.2
  14.8 12.6 %all-gather = bf16[4,1,128]{2,1,0:T(2,128)(2,1)S(1)} all-gather(bf16[1,1,128]{2,1,0:T(2,128)(2,1)S(1)} %bitcast.101), channel_id=1, replica_groups=mesh['dp'=8,'mp'=4] {'mp'}, dimensions={0}, use_global_device_ids=true | all-gather | bytes 1280 | tf_op jit(solution)/shard_map/all_gather | solution.py:319
  27.9 7.7 all-gather.1
  36.7 21.9 %all_gather.27.w_out = bf16[512,512]{1,0:T(8,128)(2,1)} all-gather(bf16[128,512]{1,0:T(8,128)(2,1)S(1)} %copy-done.9), channel_id=1, replica_groups=mesh['dp'=8,'mp'=4] {'mp'}, dimensions={0}, use_global_device_ids=true | all-gather | bytes 655360 | tf_op jit(solution)/shard_map/all_gather | solution.py:319
  61.8 43.0 %all-gather.11.cloned.1.call-done.x_all = bf16[2048,512]{1,0:T(8,128)(2,1)} async-done(((bf16[512,512]{1,0:T(8,128)(2,1)}), bf16[2048,512]{1,0:T(8,128)(2,1)}) %all-gather.11.cloned.1.call-update) | async-done | bytes 2097168 | tf_op jit(solution)/shard_map/all_gather | solution.py:319
  104.8 26.8 %attend_forward.4 = (bf16[4,512,128]{2,1,0:T(8,128)(2,1)}, bf16[4,2048,128]{2,1,0:T(8,128)(2,1)}, bf16[4,2048,128]{2,1,0:T(8,128)(2,1)}, bf16[512,512]{1,0:T(8,1...) custom-call(s32[1]{0:T(128)} %get-tuple-element.139.length_ref, ...), custom_call_target="tpu_custom_call" | custom-call | flops 12884901888 | bytes 16777216 | tf_op jit(solution)/shard_map/attend_forward/pallas_call | solution.py:206
  131.6 19.4 %all-gather.13.cloned.1.call-done.x_all = bf16[2048,512]{1,0:T(8,128)(2,1)} async-done(((bf16[512,512]{1,0:T(8,128)(2,1)}), bf16[2048,512]{1,0:T(8,128)(2,1)}) %all-gather.13.cloned.1.call-update) | async-done | bytes 2097168 | tf_op jit(solution)/shard_map/all_gather | solution.py:319
  151.0 10.8 %attend_forward.5 = (bf16[4,512,128]{2,1,0:T(8,128)(2,1)}, bf16[4,2048,128]{2,1,0:T(8,128)(2,1)}, bf16[4,2048,128]{2,1,0:T(8,128)(2,1)}, bf16[512,512]{1,0:T(8,1...) custom-call(s32[1]{0:T(128)} %get-tuple-element.138.length_ref, ...), custom_call_target="tpu_custom_call" | custom-call | flops 12884901888 | bytes 16777216 | tf_op jit(solution)/shard_map/attend_forward/pallas_call | solution.py:206
  161.9 35.9 %all-gather.7.cloned.1.call-done.x_all = bf16[2048,512]{1,0:T(8,128)(2,1)} async-done(((bf16[512,512]{1,0:T(8,128)(2,1)}), bf16[2048,512]{1,0:T(8,128)(2,1)}) %all-gather.7.cloned.1.call-update) | async-done | bytes 2097168 | tf_op jit(solution)/shard_map/all_gather | solution.py:319
  197.8 10.9 %attend_forward.3 = (bf16[4,512,128]{2,1,0:T(8,128)(2,1)}, bf16[4,2048,128]{2,1,0:T(8,128)(2,1)}, bf16[4,2048,128]{2,1,0:T(8,128)(2,1)}, bf16[512,512]{1,0:T(8,1...) custom-call(s32[1]{0:T(128)} %get-tuple-element.137.length_ref, ...), custom_call_target="tpu_custom_call" | custom-call | flops 12884901888 | bytes 16777216 | tf_op jit(solution)/shard_map/attend_forward/pallas_call | solution.py:206
  211.1 32.5 %feed_forward.1 = (bf16[3,512,512]{2,1,0:T(8,128)(2,1)}, bf16[3,512,512]{2,1,0:T(8,128)(2,1)}, bf16[3,512,512]{2,1,0:T(8,128)(2,1)}, f32[2048,512]{1,0:T(8,128)}...) custom-call(bf16[3,512,512]{2,1,0:T(8,128)(2,1)} %bitcast.84, ...), custom_call_target="tpu_custom_call" | custom-call | flops 43486543872 | bytes 16777216 | tf_op jit(solution)/shard_map/feed_forward/pallas_call | solution.py:269
  247.0 38.8 %attend_backward.4 = (bf16[2048,512]{1,0:T(8,128)(2,1)}, f32[4,384,512]{2,1,0:T(8,128)}, f32[4,8,128]{2,1,0:T(8,128)}, f32[4,8,128]{2,1,0:T(8,128)}) custom-call(s32[1]{0:T(128)} %get-tuple-element.139.length_ref, s32[1]{0:T(128)} %bitcast.22.place_ref, bf16[2048,512]{1,0:T(8,128)(2,1)} %all-gather.11.cloned.1.call-done.x_all, ...), custom_call_target="tpu_custom_call" | custom-call | flops 21474836480 | bytes 16777216 | tf_op jit(solution)/shard_map/attend_backward/pallas_call | solution.py:239
  285.9 15.6 %attend_backward.5 = (bf16[2048,512]{1,0:T(8,128)(2,1)}, f32[4,384,512]{2,1,0:T(8,128)}, f32[4,8,128]{2,1,0:T(8,128)}, f32[4,8,128]{2,1,0:T(8,128)}) custom-call(s32[1]{0:T(128)} %get-tuple-element.138.length_ref, s32[1]{0:T(128)} %bitcast.22.place_ref, bf16[2048,512]{1,0:T(8,128)(2,1)} %all-gather.13.cloned.1.call-done.x_all, ...), custom_call_target="tpu_custom_call" | custom-call | flops 21474836480 | bytes 16777216 | tf_op jit(solution)/shard_map/attend_backward/pallas_call | solution.py:239
  301.5 16.1 %attend_backward.3 = (bf16[2048,512]{1,0:T(8,128)(2,1)}, f32[4,384,512]{2,1,0:T(8,128)}, f32[4,8,128]{2,1,0:T(8,128)}, f32[4,8,128]{2,1,0:T(8,128)}) custom-call(s32[1]{0:T(128)} %get-tuple-element.137.length_ref, s32[1]{0:T(128)} %bitcast.22.place_ref, bf16[2048,512]{1,0:T(8,128)(2,1)} %all-gather.7.cloned.1.call-done.x_all, ...), custom_call_target="tpu_custom_call" | custom-call | flops 21474836480 | bytes 16777216 | tf_op jit(solution)/shard_map/attend_backward/pallas_call | solution.py:239
  317.6 2.8 add_convert_fusion
  321.9 4.0 convert_element_type.100
  327.5 82.6 %reduce-scatter.12.cloned.1.call-done = bf16[384,512]{1,0:T(8,128)(2,1)} async-done(((bf16[1536,512]{1,0:T(8,128)(2,1)}), bf16[384,512]{1,0:T(8,128)(2,1)}) %reduce-scatter.12.cloned.1.call-update) | async-done | bytes 393232 | tf_op jit(solution)/shard_map/reduce_scatter | solution.py:358
  413.0 144.9 %all-reduce.5.cloned.1.call-done = (bf16[512,2048]{1,0:T(8,128)(2,1)}, bf16[2048,512]{1,0:T(8,128)(2,1)}) async-done(((bf16[512,2048]{1,0:T(8,128)(2,1)}, bf16[2048,512]{1,0:T(8,128)(2,1)}), (bf16[512,2048]{1,0:T(8,128)(2,1)}, bf16[2048,512]{1,0:T(8,128)(2,1)})) %all-reduce.5.cloned.1.call-update) | async-done | bytes 4194320 | tf_op jit(solution)/shard_map/psum | solution.py:341
  557.9 4.3 convert_element_type.101
  564.8 49.8 %all-reduce.7.cloned.1.call-done = (bf16[512,384]{0,1:T(8,128)(2,1)}, bf16[128,512]{1,0:T(8,128)(2,1)}) async-done(((bf16[512,384]{0,1:T(8,128)(2,1)}, bf16[128,512]{1,0:T(8,128)(2,1)}), (bf16[512,384]{0,1:T(8,128)(2,1)}, bf16[128,512]{1,0:T(8,128)(2,1)})) %all-reduce.7.cloned.1.call-update) | async-done | bytes 524304 | tf_op jit(solution)/shard_map/psum | solution.py:358
  618.3 41.9 %reduce-scatter.10.cloned.1.call-done = bf16[512,512]{1,0:T(8,128)(2,1)} async-done(((bf16[2048,512]{1,0:T(8,128)(2,1)}), bf16[512,512]{1,0:T(8,128)(2,1)}) %reduce-scatter.10.cloned.1.call-update) | async-done | bytes 524304 | tf_op jit(solution)/shard_map/reduce_scatter | solution.py:350
  660.3 45.4 %reduce-scatter.6.cloned.1.call-done = bf16[512,512]{1,0:T(8,128)(2,1)} async-done(((bf16[2048,512]{1,0:T(8,128)(2,1)}), bf16[512,512]{1,0:T(8,128)(2,1)}) %reduce-scatter.6.cloned.1.call-update) | async-done | bytes 524304 | tf_op jit(solution)/shard_map/reduce_scatter | solution.py:350
  705.6 45.6 %reduce-scatter.8.cloned.1.call-done = bf16[512,512]{1,0:T(8,128)(2,1)} async-done(((bf16[2048,512]{1,0:T(8,128)(2,1)}), bf16[512,512]{1,0:T(8,128)(2,1)}) %reduce-scatter.8.cloned.1.call-update) | async-done | bytes 524304 | tf_op jit(solution)/shard_map/reduce_scatter | solution.py:350
  754.0 40.0 %psum.35 = f32[12288]{0:T(1024)S(1)} all-reduce(f32[12288]{0:T(1024)S(1)} %constant_dynamic-update-slice_fusion), channel_id=1, replica_groups=mesh['dp'=8,'mp'=4] {'dp','mp'}, use_global_device_ids=true, to_apply=%region_6.0 | all-reduce | flops 12288 | bytes 98304 | tf_op jit(solution)/shard_map/psum | solution.py:365
  (92 shorter events, 35.5 us)
Async XLA Ops:
  7.2 51.4 %all-gather.9.cloned.1.call-start = ((), (), s32[]{:S(2)}) async-start(), calls=%async_computation.6 | async-start | bytes 1966080 | tf_op jit(solution)/shard_map/all_gather | solution.py:319
  9.2 95.6 %all-gather.11.cloned.1.call-start = ((), (), s32[]{:S(2)}) async-start(), calls=%async_computation.7 | async-start | bytes 2621440 | tf_op jit(solution)/shard_map/all_gather | solution.py:319
  10.1 4.7 copy-start.14
  10.1 17.8 %copy-start.15 = (bf16[128]{0:T(256)(128)(2,1)S(1)}, bf16[128]{0:T(256)(128)(2,1)}, u32[]{:S(2)}) copy-start(bf16[128]{0:T(256)(128)(2,1)} %param.20) | copy-start | bytes 772
  10.1 26.0 %copy-start.11 = (s32[3]{0:T(128)S(1)}, s32[3]{0:T(128)}, u32[]{:S(2)}) copy-start(s32[3]{0:T(128)} %param.16) | copy-start | bytes 40
  10.1 26.6 %copy-start.9 = (bf16[128,512]{1,0:T(8,128)(2,1)S(1)}, bf16[128,512]{1,0:T(8,128)(2,1)}, u32[]{:S(2)}) copy-start(bf16[128,512]{1,0:T(8,128)(2,1)} %param.21) | copy-start | bytes 393220
  12.8 138.2 %all-gather.13.cloned.1.call-start = ((), (), s32[]{:S(2)}) async-start(), calls=%async_computation.8 | async-start | bytes 2621440 | tf_op jit(solution)/shard_map/all_gather | solution.py:319
  13.5 184.2 %all-gather.7.cloned.1.call-start = ((), (), s32[]{:S(2)}) async-start(), calls=%async_computation.5 | async-start | bytes 2621440 | tf_op jit(solution)/shard_map/all_gather | solution.py:319
  14.1 313.4 %reduce-scatter.14.cloned.1.call-start = ((), (), s32[]{:S(2)}) async-start(), calls=%async_computation.13 | async-start | bytes 655360 | tf_op jit(solution)/shard_map/reduce_scatter | solution.py:343
  197.7 10.9 %copy-start.7 = (bf16[512,512]{1,0:T(8,128)(2,1)S(1)}, bf16[512,512]{1,0:T(8,128)(2,1)}, u32[]{:S(2)}) copy-start(bf16[512,512]{1,0:T(8,128)(2,1)} %get-tuple-element.52) | copy-start | bytes 1572868
  197.7 10.9 %copy-start.8 = (bf16[512,512]{1,0:T(8,128)(2,1)S(1)}, bf16[512,512]{1,0:T(8,128)(2,1)}, u32[]{:S(2)}) copy-start(bf16[512,512]{1,0:T(8,128)(2,1)} %get-tuple-element.53) | copy-start | bytes 1572868
  245.8 164.3 %reduce-scatter.12.cloned.1.call-start = ((), (), s32[]{:S(2)}) async-start(), calls=%async_computation.12 | async-start | bytes 1966080 | tf_op jit(solution)/shard_map/reduce_scatter | solution.py:358
  301.4 16.2 %copy-start.3 = (f32[4,384,512]{2,1,0:T(8,128)S(1)}, f32[4,384,512]{2,1,0:T(8,128)}, u32[]{:S(2)}) copy-start(f32[4,384,512]{2,1,0:T(8,128)} %get-tuple-element.85) | copy-start | bytes 9437188
  301.5 16.2 %copy-start.4 = (f32[4,384,512]{2,1,0:T(8,128)S(1)}, f32[4,384,512]{2,1,0:T(8,128)}, u32[]{:S(2)}) copy-start(f32[4,384,512]{2,1,0:T(8,128)} %get-tuple-element.86) | copy-start | bytes 9437188
  321.8 236.1 %all-reduce.5.cloned.1.call-start = ((), (), s32[]{:S(2)}) async-start(), calls=%async_computation.14 | async-start | bytes 8388608 | tf_op jit(solution)/shard_map/psum | solution.py:341
  321.8 4.0 copy-start.2
  327.5 287.2 %all-reduce.7.cloned.1.call-start = ((), (), s32[]{:S(2)}) async-start(), calls=%async_computation.15 | async-start | bytes 1048576 | tf_op jit(solution)/shard_map/psum | solution.py:358
  410.1 250.1 %reduce-scatter.10.cloned.1.call-start = ((), (), s32[]{:S(2)}) async-start(), calls=%async_computation.11 | async-start | bytes 2621440 | tf_op jit(solution)/shard_map/reduce_scatter | solution.py:350
  410.9 294.7 %reduce-scatter.6.cloned.1.call-start = ((), (), s32[]{:S(2)}) async-start(), calls=%async_computation.9 | async-start | bytes 2621440 | tf_op jit(solution)/shard_map/reduce_scatter | solution.py:350
  411.5 339.8 %reduce-scatter.8.cloned.1.call-start = ((), (), s32[]{:S(2)}) async-start(), calls=%async_computation.10 | async-start | bytes 2621440 | tf_op jit(solution)/shard_map/reduce_scatter | solution.py:350
  557.9 4.3 copy-start.5
  751.2 2.8 copy-start.13
  751.2 2.8 copy-start.10
  751.2 2.8 copy-start.12
  (4 other events, 8.8 us)
Sparse Core Ops, SparseCore 0:
  10.2 48.0 all-gather.8
  59.8 44.9 all-gather.10
  106.4 44.5 all-gather.12
  153.0 44.6 all-gather.6
  245.9 36.1 reduce-scatter.13
  321.9 88.1 reduce-scatter.11
  417.0 140.9 all-reduce.4
  561.1 53.5 all-reduce.6
  617.1 43.1 reduce-scatter.9
  662.4 43.1 reduce-scatter.5
  708.0 43.1 reduce-scatter.7

commit v2 on v1

v2 whole, which is shorter than its diff:
```python
import functools
import math

import jax
import jax.numpy as jnp
from jax import lax
from jax.experimental import pallas as pl
from jax.experimental.pallas import tpu as pltpu
from jax.sharding import PartitionSpec as P

HD = 64
PAIR = 2 * HD
HIGHEST = lax.Precision.HIGHEST
NEGATIVE = -1e30
LOG2E = math.log2(math.e)
F32 = jnp.float32
BF16 = jnp.bfloat16
VMEM_LIMIT = 56 * 1024 * 1024


def nn(a, b):
    return jnp.dot(a, b, preferred_element_type=F32)


def nt(a, b):
    return lax.dot_general(a, b, (((1,), (1,)), ((), ())), preferred_element_type=F32)


def tn(a, b):
    return lax.dot_general(a, b, (((0,), (0,)), ((), ())), preferred_element_type=F32)


def head_lanes(rows, head):
    lane = lax.broadcasted_iota(jnp.int32, (rows, PAIR), 1)
    return (lane >= head * HD) & (lane < (head + 1) * HD)


def one_head(pair_rows, head):
    return jnp.where(head_lanes(pair_rows.shape[0], head), pair_rows, jnp.zeros_like(pair_rows))


def fold8(values, op):
    rows, lanes = values.shape
    return op(values.reshape(rows // 8, 8, lanes), axis=0)


def attend_backward(length_ref, place_ref, x_all, x_own, weight, q_in, k_in, v_in, att_t, lse, grad_in,
                    x_grad, w_grad, qb_grad, vb_grad, x_acc, kv_grad, dq_acc, *, block):
    length = length_ref[0]
    blocks = (length + block - 1) // block
    rows = x_own.shape[0]
    pair = pl.program_id(0)
    full = x_all.shape[0]
    q_pair = q_in[0]
    grad_pair = grad_in[...]
    q_heads = [one_head(q_pair, h) for h in range(2)]
    g_heads = [one_head(grad_pair, h) for h in range(2)]
    prod = grad_pair.astype(F32).T * att_t[0]
    delta = [jnp.sum(prod[h * HD:(h + 1) * HD], axis=0, keepdims=True) for h in range(2)]
    tops = [lse[0, h:h + 1, :] for h in range(2)]
    dq_acc[...] = jnp.zeros_like(dq_acc)

    @pl.when(pair == 0)
    def _():
        x_acc[...] = jnp.zeros_like(x_acc)

    w_grad[0] = jnp.zeros(w_grad.shape[1:], F32)

    def step(j, vsum):
        at = pl.ds(pl.multiple_of(j * block, block), block)
        k_blk = k_in[0, at, :]
        v_blk = v_in[0, at, :]
        keep = (lax.broadcasted_iota(jnp.int32, (block, rows), 0) + j * block) < length
        dk = jnp.zeros((block, PAIR), F32)
        dv = jnp.zeros((block, PAIR), F32)
        for h in range(2):
            s = nt(k_blk, q_heads[h]) * LOG2E
            p = jnp.where(keep, jnp.exp2(s - tops[h]), 0.0)
            dp = nt(v_blk, g_heads[h])
            ds = (p * (dp - delta[h])).astype(BF16)
            dv += nn(p.astype(BF16), g_heads[h])
            dk += nn(ds, q_heads[h])
            dq_acc[h] += tn(k_blk, ds)
        dv = dv.astype(BF16)
        both = jnp.concatenate([dk.astype(BF16), dv], axis=1)
        x_acc[at, :] += nn(both, weight[0, PAIR:, :])
        w_grad[0, PAIR:, :] += tn(both, x_all[at, :])
        return vsum + fold8(dv.astype(F32), jnp.sum)

    vsum = lax.fori_loop(0, blocks, step, jnp.zeros((8, PAIR), F32))
    vb_grad[0] = jnp.broadcast_to(jnp.sum(vsum, axis=0, keepdims=True), (8, PAIR))
    dq_t = jnp.concatenate([dq_acc[h, h * HD:(h + 1) * HD, :] for h in range(2)], axis=0) * (HD ** -0.5)
    dq = dq_t.T.astype(BF16)
    qb_grad[0] = jnp.broadcast_to(jnp.sum(dq.astype(F32), axis=0, keepdims=True), (8, PAIR))
    mine = pl.ds(pl.multiple_of(place_ref[0] * rows, rows), rows)
    x_acc[mine, :] += nn(dq, weight[0, :PAIR, :])
    w_grad[0, :PAIR, :] += tn(dq, x_own[...])

    @pl.when(pair == pl.num_programs(0) - 1)
    def _():
        x_grad[...] = x_acc[...].astype(BF16)


def whole(shape):
    return pl.BlockSpec(shape, lambda *_: (0,) * len(shape))


MESH = pl.DeviceIdType.MESH
CONSTANT = pl.Buffered(1)
PIECES = 8


class Relay:
    def __init__(self, place, count, view, send_sem, recv_sem):
        self.place, self.count, self.view = place, count, view
        self.send_sem, self.recv_sem = send_sem, recv_sem

    def copy(self, chunk, downward, step):
        return pltpu.make_async_remote_copy(
            src_ref=self.view(chunk), dst_ref=self.view(chunk),
            send_sem=self.send_sem(downward, step), recv_sem=self.recv_sem(chunk),
            device_id={"mp": self.place - 1 if downward else self.place + 1},
            device_id_type=MESH)

    def each(self, step):
        for downward in (0, 1):
            chunk = self.place + step if downward else self.place - step
            exists = chunk < self.count if downward else chunk >= 0
            onward = self.place >= 1 if downward else self.place + 1 < self.count
            yield downward, chunk, exists, onward

    def advance(self, step):
        for downward, chunk, exists, onward in self.each(step):
            if step:
                @pl.when(exists)
                def _():
                    self.copy(chunk, downward, step).wait_recv()
            if step < self.count - 1:
                @pl.when(exists & onward)
                def _():
                    self.copy(chunk, downward, step).start()

    def drain(self):
        for step in range(self.count - 1):
            for downward, chunk, exists, onward in self.each(step):
                @pl.when(exists & onward)
                def _():
                    self.copy(chunk, downward, step).wait_send()


def greet(place, count, partners):
    barrier = pltpu.get_barrier_semaphore()
    for partner in partners:
        pl.semaphore_signal(barrier, 1, device_id={"dp": partner}, device_id_type=MESH)
    for k in range(1, count):
        pl.semaphore_signal(barrier, 1, device_id={"mp": (place + k) % count}, device_id_type=MESH)


def await_greetings(count, partners):
    pl.semaphore_wait(pltpu.get_barrier_semaphore(), len(partners) + count - 1)


def flip(index, bit):
    return index + bit - 2 * bit * ((index // bit) % 2)


def forward_layer(count, heads_dev, block,
                  lengths, pair_ids, tok, embed, cot, qkv_w, q_bias, v_bias, out_w, b_out,
                  w_in, b_in, w_last, b_last,
                  x_out, w_out, q_out, k_out, v_out, att_t_out, lse_out,
                  result, mixed_grad, att_grad, g_all, g_bias,
                  x_all, w_all, w_o, biases, s_all, acc, att_rows_all, grads, grad_rows,
                  x_send, x_recv, x_copy, w_send, w_recv, plane_send, plane_recv):
    seq, pair = pl.program_id(0), pl.program_id(1)
    seqs, pairs = tok.shape[0], w_out.shape[0]
    rows, width = tok.shape[1], tok.shape[2]
    full = count * rows
    hidden = w_in.shape[1]
    base = heads_dev * 4 * HD
    piece_rows = w_all.shape[1] // PIECES
    place, data_at = lax.axis_index("mp"), lax.axis_index("dp")
    last_step = (seq == seqs - 1) & (pair == pairs - 1)

    def x_relay(s):
        return Relay(
            place, count,
            lambda chunk: x_all.at[s, pl.ds(pl.multiple_of(chunk * rows, rows), rows)],
            lambda downward, step: x_send.at[s, downward * (count - 1) + step],
            lambda chunk: x_recv.at[s, chunk])

    low_bits = [(data_at // bit) % 2 for bit in (4, 2, 1)]
    piece = low_bits[0] + 2 * low_bits[1] + 4 * low_bits[2]

    def w_span(start, size):
        return pl.ds(pl.multiple_of(start * piece_rows, piece_rows), size * piece_rows)

    w_relay = Relay(
        place, count, lambda chunk: w_all.at[chunk, w_span(piece, 1)],
        lambda downward, step: w_send.at[downward * (count - 1) + step],
        lambda chunk: w_recv.at[chunk])
    partners = [flip(data_at, bit) for bit in (4, 2, 1)]
    spans = [w_span(piece, 1), w_span(2 * low_bits[1] + 4 * low_bits[2], 2), w_span(4 * low_bits[2], 4)]

    def plane(stage):
        copies = []
        for k in range(1, count):
            source = (place + k) % count
            copies.append(pltpu.make_async_remote_copy(
                src_ref=w_all.at[source, spans[stage]], dst_ref=w_all.at[source, spans[stage]],
                send_sem=plane_send.at[stage, k - 1], recv_sem=plane_recv.at[stage, k - 1],
                device_id={"dp": partners[stage]}, device_id_type=MESH))
        return copies

    def plane_start(stage):
        for copy in plane(stage):
            copy.start()

    def plane_wait(stage):
        for copy in plane(stage):
            copy.wait()

    @pl.when((seq == 0) & (pair == 0))
    def _():
        greet(place, count, partners)
        turned = qkv_w[...].T
        parts = []
        for j in range(3):
            for h in range(heads_dev):
                parts.append(turned[(h * 3 + j) * HD:(h * 3 + j + 1) * HD])
        w_all[place, 0:heads_dev * 3 * HD, :] = jnp.concatenate(parts, axis=0)
        w_all[place, heads_dev * 3 * HD:base, :] = out_w[...]
        first = lax.broadcasted_iota(jnp.int32, (w_all.shape[1] - base, width), 0)
        w_all[place, base:, :] = jnp.where(
            first == 0, q_bias[...].astype(F32),
            jnp.where(first == 1, v_bias[...].astype(F32), 0.0)).astype(BF16)
        for s in range(seqs):
            row = embed[pl.ds(pair_ids[s], 1), :]
            own = pl.ds(pl.multiple_of(place * rows, rows), rows)
            x_all[s, own, :] = (tok[s].astype(F32) + row).astype(BF16)
        await_greetings(count, partners)
        w_relay.advance(0)
        if count > 2:
            w_relay.advance(1)
        x_relay(0).advance(0)
        for step in range(2 if count > 2 else 1, count):
            w_relay.advance(step)
        plane_start(0)
        plane_wait(0)
        plane_start(1)
        if count > 2:
            x_relay(0).advance(1)
        plane_wait(1)
        plane_start(2)
        for step in range(2, count - 1):
            x_relay(0).advance(step)
        grads[...] = jnp.zeros_like(grads)
        grad_rows[...] = jnp.zeros_like(grad_rows)
        plane_wait(2)
        w_relay.drain()
        total = jnp.zeros((16, width), F32)
        for m in range(count):
            total += w_all[m, base:base + 16, :].astype(F32)
        biases[...] = total
        for p in range(pairs):
            if heads_dev == 2:
                w_out[p] = w_all[p, 0:3 * PAIR, :]
                w_o[p * PAIR:(p + 1) * PAIR, :] = w_all[p, 3 * PAIR:4 * PAIR, :]
            else:
                for half in range(2):
                    for j in range(4):
                        strip = w_all[2 * p + half, j * HD:(j + 1) * HD, :]
                        if j < 3:
                            w_out[p, j * PAIR + half * HD:j * PAIR + (half + 1) * HD, :] = strip
                        else:
                            w_o[p * PAIR + half * HD:p * PAIR + (half + 1) * HD, :] = strip

    def hbm_copy(s):
        return pltpu.make_async_copy(x_all.at[s], x_out.at[s], x_copy.at[s])

    @pl.when(pair == 0)
    def _():
        x_relay(seq).advance(count - 1)

        @pl.when(seq + 1 < seqs)
        def _():
            x_relay(seq + 1).advance(0)
        hbm_copy(seq).start()

    length = lengths[seq]
    lanes = pl.ds(pl.multiple_of(pair * PAIR, PAIR), PAIR)
    own = pl.ds(pl.multiple_of(place * rows, rows), rows)
    q_pair = (nt(x_all[seq, own, :], w_out[pair, 0:PAIR, :]) + biases[0:1, lanes]).astype(BF16)
    q_pair = q_pair * BF16(HD ** -0.5)
    q_out[0, 0] = q_pair
    q_heads = [one_head(q_pair, 0), one_head(q_pair, 1)]
    v_row = biases[1:2, lanes]

    def score_step(j, tops):
        at = pl.ds(pl.multiple_of(j * block, block), block)
        kv = nt(x_all[seq, at, :], w_out[pair, PAIR:3 * PAIR, :])
        k_blk = kv[:, :PAIR].astype(BF16)
        k_out[0, 0, at, :] = k_blk
        v_out[0, 0, at, :] = (kv[:, PAIR:] + v_row).astype(BF16)
        keep = (lax.broadcasted_iota(jnp.int32, (block, rows), 0) + j * block) < length
        new = []
        for h in range(2):
            s = nt(k_blk, q_heads[h]) * LOG2E
            s = jnp.where(keep, s, NEGATIVE)
            s_all[h, at, :] = s
            new.append(jnp.maximum(tops[h], fold8(s, jnp.max)))
        return tuple(new)

    start = jnp.full((8, rows), NEGATIVE, F32)
    tops = lax.fori_loop(0, full // block, score_step, (start, start))
    tops = [jnp.max(t, axis=0, keepdims=True) for t in tops]
    acc[...] = jnp.zeros_like(acc)

    def value_step(j, sums):
        at = pl.ds(pl.multiple_of(j * block, block), block)
        v_blk = v_out[0, 0, at, :]
        new = []
        for h in range(2):
            p = jnp.exp2(s_all[h, at, :] - tops[h])
            new.append(sums[h] + fold8(p, jnp.sum))
            acc[h] += tn(v_blk, p.astype(BF16))
        return tuple(new)

    zero = jnp.zeros((8, rows), F32)
    sums = lax.fori_loop(0, full // block, value_step, (zero, zero))
    sums = [jnp.sum(t, axis=0, keepdims=True) for t in sums]
    att_t = jnp.concatenate([acc[h, h * HD:(h + 1) * HD, :] * (1.0 / sums[h]) for h in range(2)], axis=0)
    att_t_out[0, 0] = att_t
    att_rows_all[:, lanes] = att_t.T.astype(BF16)
    lse_out[0, 0] = jnp.concatenate(
        [tops[h] + jnp.log2(sums[h]) for h in range(2)] + [jnp.zeros((6, rows), F32)], axis=0)

    for step in range(1, count - 1):
        after = max(0, (step * pairs) // (count - 2) - 1)

        @pl.when((pair == after) & (seq + 1 < seqs))
        def _():
            x_relay(seq + 1).advance(step)

    @pl.when(pair == pairs - 1)
    def _():
        cot_rows = cot[0]
        att_rows = att_rows_all[...]
        row = embed[pl.ds(pair_ids[seq], 1), :]
        mixed = (tok[seq].astype(F32) + row) + (nn(att_rows, w_o[...]) + b_out[...])
        mixed_low = mixed.astype(BF16)
        out_sum = mixed + b_last[...]
        back_sum = cot_rows.astype(F32)
        root = math.sqrt(2.0 / math.pi)
        for c in range(hidden // width):
            at = slice(c * width, (c + 1) * width)
            pre = nn(mixed_low, w_in[:, at]) + b_in[:, at]
            square = pre * pre
            th = jnp.tanh(root * pre * (1.0 + 0.044715 * square))
            half = 0.5 * (1.0 + th)
            act = (pre * half).astype(BF16)
            slope = half + (0.5 * root) * pre * (1.0 - th * th) * (1.0 + (3 * 0.044715) * square)
            out_sum += nn(act, w_last[at, :])
            back = (nt(cot_rows, w_last[at, :]) * slope).astype(BF16)
            grad_rows[c:c + 1, :] += jnp.sum(back.astype(F32), axis=0, keepdims=True)
            back_sum += nt(back, w_in[:, at])
            grads[at, :] += tn(act, cot_rows)
            grads[hidden + c * width:hidden + (c + 1) * width, :] += tn(mixed_low, back)
        result[0] = out_sum.astype(BF16)
        back_low = back_sum.astype(BF16)
        mixed_grad[0] = back_low
        at = hidden // width
        grad_rows[at:at + 1, :] += jnp.sum(cot_rows.astype(F32), axis=0, keepdims=True)
        grad_rows[at + 1:at + 2, :] += jnp.sum(back_low.astype(F32), axis=0, keepdims=True)
        grads[2 * hidden:, :] += tn(att_rows, back_low)
        att_grad[0] = nt(back_low, w_o[...]).astype(BF16)

    @pl.when(last_step)
    def _():
        def narrow(j, _):
            at = pl.ds(pl.multiple_of(j * width, width), width)
            g_all[at, :] = grads[at, :].astype(BF16)
            return 0

        lax.fori_loop(0, grads.shape[0] // width, narrow, 0)
        g_bias[...] = grad_rows[...]
        for s in range(seqs):
            x_relay(s).drain()
            hbm_copy(s).wait()


def fixed(shape):
    return pl.BlockSpec(shape, lambda *_: (0,) * len(shape), pipeline_mode=CONSTANT)


def call_layer(count, lengths, pair_ids, tok, embed, cot, qkv_w, q_bias, v_bias, out_w, b_out,
               w_in, b_in, w_last, b_last):
    seqs, rows, width = tok.shape
    hidden = w_in.shape[1]
    heads_dev = qkv_w.shape[1] // (3 * HD)
    full = count * rows
    pairs = width // PAIR
    block = min(512, full)
    w_rows = -(-(heads_dev * 4 * HD + 16) // (16 * PIECES)) * 16 * PIECES
    in_smem = pl.BlockSpec(memory_space=pltpu.SMEM)
    per_seq = lambda: pl.BlockSpec((1, rows, width), lambda s, p: (s, 0, 0))
    per_pair = lambda *tail: pl.BlockSpec((1, 1) + tail, lambda s, p: (s, p, 0, 0))
    shape = jax.ShapeDtypeStruct
    return pl.pallas_call(
        functools.partial(forward_layer, count, heads_dev, block),
        grid=(seqs, pairs),
        in_specs=[in_smem, in_smem, fixed(tok.shape), fixed(embed.shape), per_seq(), fixed(qkv_w.shape),
                  fixed(q_bias.shape), fixed(v_bias.shape), fixed(out_w.shape), fixed(b_out.shape),
                  fixed(w_in.shape), fixed(b_in.shape), fixed(w_last.shape), fixed(b_last.shape)],
        out_specs=[pl.BlockSpec(memory_space=pl.ANY), fixed((pairs, 3 * PAIR, width)),
                   per_pair(rows, PAIR), per_pair(full, PAIR), per_pair(full, PAIR),
                   per_pair(PAIR, rows), per_pair(8, rows),
                   per_seq(), per_seq(), per_seq(), fixed((2 * hidden + width, width)), fixed((8, width))],
        out_shape=[
            shape((seqs, full, width), BF16),
            shape((pairs, 3 * PAIR, width), BF16),
            shape((seqs, pairs, rows, PAIR), BF16),
            shape((seqs, pairs, full, PAIR), BF16),
            shape((seqs, pairs, full, PAIR), BF16),
            shape((seqs, pairs, PAIR, rows), F32),
            shape((seqs, pairs, 8, rows), F32),
            shape((seqs, rows, width), BF16),
            shape((seqs, rows, width), BF16),
            shape((seqs, rows, width), BF16),
            shape((2 * hidden + width, width), BF16),
            shape((8, width), F32),
        ],
        scratch_shapes=[
            pltpu.VMEM((seqs, full, width), BF16),
            pltpu.VMEM((count, w_rows, width), BF16),
            pltpu.VMEM((width, width), BF16),
            pltpu.VMEM((16, width), F32),
            pltpu.VMEM((2, full, rows), F32),
            pltpu.VMEM((2, PAIR, rows), F32),
            pltpu.VMEM((rows, width), BF16),
            pltpu.VMEM((2 * hidden + width, width), F32),
            pltpu.VMEM((8, width), F32),
            pltpu.SemaphoreType.DMA((seqs, 2 * (count - 1))),
            pltpu.SemaphoreType.DMA((seqs, count)),
            pltpu.SemaphoreType.DMA((seqs,)),
            pltpu.SemaphoreType.DMA((2 * (count - 1),)),
            pltpu.SemaphoreType.DMA((count,)),
            pltpu.SemaphoreType.DMA((3, count - 1)),
            pltpu.SemaphoreType.DMA((3, count - 1)),
        ],
        cost_estimate=pl.CostEstimate(flops=120 * 10 ** 9, bytes_accessed=60 << 20,
                                      transcendentals=seqs * pairs * 2 * full * rows),
        compiler_params=pltpu.CompilerParams(
            collective_id=0, has_side_effects=True, vmem_limit_bytes=VMEM_LIMIT),
        name="forward_layer",
    )(lengths, pair_ids, tok, embed, cot, qkv_w, q_bias, v_bias, out_w, b_out, w_in, b_in, w_last, b_last)


def call_backward(length, place, x_all, x_own, weight, q, k, v, att_t, lse, grad):
    full, width = x_all.shape
    rows = x_own.shape[0]
    pairs = weight.shape[0]
    block = min(512, full)
    per_pair = lambda *tail: pl.BlockSpec((1,) + tail, lambda p, *_: (p, 0, 0))
    return pl.pallas_call(
        functools.partial(attend_backward, block=block),
        grid_spec=pltpu.PrefetchScalarGridSpec(
            num_scalar_prefetch=2,
            grid=(pairs,),
            in_specs=[whole((full, width)), whole((rows, width)), per_pair(3 * PAIR, width),
                      per_pair(rows, PAIR), per_pair(full, PAIR), per_pair(full, PAIR),
                      per_pair(PAIR, rows), per_pair(8, rows),
                      pl.BlockSpec((rows, PAIR), lambda p, *_: (0, p))],
            out_specs=[whole((full, width)), per_pair(3 * PAIR, width), per_pair(8, PAIR), per_pair(8, PAIR)],
            scratch_shapes=[pltpu.VMEM((full, width), F32), pltpu.VMEM((full, 2 * PAIR), BF16),
                            pltpu.VMEM((2, PAIR, rows), F32)],
        ),
        out_shape=[
            jax.ShapeDtypeStruct((full, width), BF16),
            jax.ShapeDtypeStruct((pairs, 3 * PAIR, width), F32),
            jax.ShapeDtypeStruct((pairs, 8, PAIR), F32),
            jax.ShapeDtypeStruct((pairs, 8, PAIR), F32),
        ],
        cost_estimate=pl.CostEstimate(flops=40 * pairs * full * rows * PAIR, bytes_accessed=16 << 20,
                                      transcendentals=2 * pairs * full * rows),
        compiler_params=pltpu.CompilerParams(vmem_limit_bytes=VMEM_LIMIT),
        name="attend_backward",
    )(length, place, x_all, x_own, weight, q, k, v, att_t, lse, grad)


def body(
    tokens,
    pair_ids,
    lengths,
    pair_embed,
    qkv_weight,
    q_bias,
    v_bias,
    out_weight,
    out_bias,
    ffn_in_weight,
    ffn_in_bias,
    ffn_out_weight,
    ffn_out_bias,
    cotangent,
):
    local_rows, seqs, width = tokens.shape
    table_rows = pair_embed.shape[0]
    count = lax.axis_size("mp")
    place = lax.axis_index("mp").astype(jnp.int32).reshape(1)
    tok = jnp.transpose(tokens, (1, 0, 2))
    cot = jnp.transpose(cotangent, (1, 0, 2))
    select = (pair_ids[:, None] == lax.iota(jnp.int32, table_rows)[None, :]).astype(F32)
    bias_len = q_bias.shape[0]
    spread = lambda v: lax.dynamic_update_slice(
        jnp.zeros((1, width), BF16), v[None], (0, place[0] * bias_len))
    (x_all, w_pairs, q, k, v, att_t, lse, result, mixed_grad, att_grad, g_all, g_bias) = call_layer(
        count, lengths, pair_ids, tok, pair_embed, cot, qkv_weight, spread(q_bias), spread(v_bias),
        out_weight, out_bias[None], ffn_in_weight, ffn_in_bias[None], ffn_out_weight,
        ffn_out_bias[None])
    hidden = ffn_in_weight.shape[1]
    pairs = w_pairs.shape[0]
    g_sum = lax.psum(g_all, ("dp", "mp"))
    g_last_sum = g_sum[:hidden]
    g_in_sum = jnp.transpose(
        g_sum[hidden:2 * hidden].reshape(hidden // width, width, width), (1, 0, 2)).reshape(width, hidden)
    out_rows = out_weight.shape[0]
    g_out_own = lax.dynamic_slice_in_dim(g_sum, 2 * hidden + place[0] * out_rows, out_rows)
    at = hidden // width
    gb_in, gb_last, gb_out = g_bias[:at].reshape(-1), g_bias[at], g_bias[at + 1]

    token_grads, w_grads, qb_grads, vb_grads = [], [], [], []
    for s in range(seqs):
        x_grad, w_grad, qb, vb = call_backward(
            lengths[s:s + 1], place, x_all[s],
            lax.dynamic_slice_in_dim(x_all[s], place[0] * local_rows, local_rows),
            w_pairs, q[s], k[s], v[s], att_t[s], lse[s], att_grad[s])
        own = lax.psum_scatter(x_grad, "mp", scatter_dimension=0, tiled=True)
        token_grads.append(mixed_grad[s].astype(F32) + own.astype(F32))
        w_grads.append(w_grad)
        qb_grads.append(qb[:, 0])
        vb_grads.append(vb[:, 0])

    w_grad = sum(w_grads).astype(BF16).reshape(pairs, 3, 2, HD, width)
    w_grad = jnp.transpose(w_grad, (0, 2, 1, 3, 4)).reshape(pairs * 2 * 3 * HD, width)
    w_grad = lax.psum(lax.psum_scatter(w_grad, "mp", scatter_dimension=0, tiled=True), "dp")
    qkv_sum = w_grad.astype(F32).T
    seq_sums = jnp.stack([jnp.sum(t, axis=0) for t in token_grads])
    table_grad = lax.dot_general(select, seq_sums, (((0,), (0,)), ((), ())), precision=HIGHEST)
    small = jnp.concatenate([
        table_grad.reshape(-1), sum(qb_grads).reshape(-1), sum(vb_grads).reshape(-1),
        gb_out.reshape(-1), gb_in.reshape(-1), gb_last.reshape(-1)])
    small = lax.psum(small, ("dp", "mp"))
    sizes = [table_grad.size, width, width, width, gb_in.size, width]
    parts, at = [], 0
    for size in sizes:
        parts.append(small[at:at + size])
        at += size
    table_sum, qb_sum, vb_sum, out_bias_sum, in_bias_sum, last_bias_sum = parts
    qb_own = lax.dynamic_slice_in_dim(qb_sum, place[0] * bias_len, bias_len)
    vb_own = lax.dynamic_slice_in_dim(vb_sum, place[0] * bias_len, bias_len)
    tokens_grad = jnp.transpose(jnp.stack(token_grads), (1, 0, 2))
    return (
        jnp.transpose(result, (1, 0, 2)),
        tokens_grad,
        table_sum.reshape(table_rows, width),
        qkv_sum,
        qb_own,
        vb_own,
        g_out_own.astype(F32),
        out_bias_sum,
        g_in_sum.astype(F32),
        in_bias_sum,
        g_last_sum.astype(F32),
        last_bias_sum,
    )


def solution(mesh):
    return jax.shard_map(
        body,
        mesh=mesh,
        in_specs=(
            P("mp", "dp", None),
            P("dp"),
            P("dp"),
            P(),
            P(None, "mp"),
            P("mp"),
            P("mp"),
            P("mp", None),
            P(),
            P(),
            P(),
            P(),
            P(),
            P("mp", "dp", None),
        ),
        out_specs=(
            P("mp", "dp", None),
            P("mp", "dp", None),
            P(),
            P(None, "mp"),
            P("mp"),
            P("mp"),
            P("mp", None),
            P(),
            P(),
            P(),
            P(),
            P(),
        ),
        check_vma=False,
    )
```

time: 802 us -> 666 us (0.83); the launches traced: 806 us -> 661 us
  waiting for transfers between devices: 512 us -> 307 us
  Pallas kernels: 152 us -> 242 us
  blocking collectives: 82.1 us -> 39.7 us
  local copies, waits for them, and re-layouts: 13.9 us -> 41 us
  other arithmetic: 30.5 us -> 15.8 us
    reduce_scatter x3, waiting for transfers between devices: 133 us -> 0.01 us  [body(): own = lax.psum_scatter(x_grad, 'mp', scatter_dimension=0, tiled=True)]
    all_gather x4 -> x0, waiting for transfers between devices: 98.3 us -> none  [body(): gather = lambda v: lax.all_gather(v, 'mp', axis=0, tiled=True)]
    pallas_call x4 -> x1, Pallas kernels: 81.1 us -> 158 us  [call_layer(): pl.pallas_call(functools.partial(forward_layer, count, heads_dev, block),...]
    psum x1, waiting for transfers between devices: 145 us -> 197 us  [body(): g_sum = lax.psum(g_all, ('dp', 'mp'))]
    all_gather x3 -> x0, blocking collectives: 42.1 us -> none  [body(): gather = lambda v: lax.all_gather(v, 'mp', axis=0, tiled=True)]
    reduce_scatter x1, waiting for transfers between devices: 82.6 us -> 61.5 us  [body(): lax.psum_scatter(w_grad, 'mp', scatter_dimension=0, tiled=True)]
    squeeze x0 -> x4, local copies, waits for them, and re-layouts: none -> 15 us  [the longest x1 9.38 us: body(): v[s]]
    convert_element_type x5 -> x0, other arithmetic: 14.7 us -> none  [the longest x1 4.28 us: body(): g_in_sum.astype(F32)]
  transfers between devices with their start and end apart: 11 -> 6, of which waited for: 9 -> 3; matrix products, arithmetic and copies ran while one was open for 4% -> 2% of each run, Pallas kernels for 13% -> 0%
where the time goes in v2:
time: 666 us; the launch traced here: 661 us
  waiting for transfers between devices  307 us (46%)
  Pallas kernels  242 us (36%)
  local copies, waits for them, and re-layouts  41 us (6%)
  blocking collectives  39.7 us (6%)
  other arithmetic  15.8 us (2%)
  between operations  15.4 us (2%)
    psum x1, waiting for transfers between devices, body(): g_sum = lax.psum(g_all, ('dp', 'mp'))  197 us
    pallas_call x1, Pallas kernels, call_layer(): pl.pallas_call(functools.partial(forward_layer, count, heads_dev, block),...  158 us
    pallas_call x3, Pallas kernels, call_backward(): pl.pallas_call(functools.partial(attend_backward, block=block), grid_spec...  84 us
    reduce_scatter x1, waiting for transfers between devices, body(): lax.psum_scatter(w_grad, 'mp', scatter_dimension=0, tiled=True)  61.5 us
    psum x1, waiting for transfers between devices, body(): lax.psum(lax.psum_scatter(w_grad, 'mp', scatter_dimension=0, tiled=True),...  45.7 us
    psum x1, blocking collectives, body(): small = lax.psum(small, ('dp', 'mp'))  39.7 us
  transfers between devices with their start and end apart: 6, of which 3 were waited for; matrix products, arithmetic and copies ran while one was open for 2% of the time, Pallas kernels for 0%

profile of v2, /device:TPU:0, one launch (start us, length us, event | category | flops | bytes accessed | tf_op | source)
XLA Modules:
  0.0 661.2 jit_solution(16816490576478597333)
XLA Ops:
  8.1 1.4 fusion.16
  11.3 157.9 %forward_layer.1 = (bf16[3,2048,512]{2,1,0:T(8,128)(2,1)}, bf16[4,384,512]{2,1,0:T(8,128)(2,1)}, bf16[3,4,512,128]{3,2,1,0:T(8,128)(2,1)}, bf16[3,4,2048,128]{3,...) custom-call(s32[3]{0:T(128)} %lengths.1, ...), custom_call_target="tpu_custom_call" | custom-call | flops 120000004096 | bytes 62914560 | tf_op jit(solution)/shard_map/forward_layer/pallas_call | solution.py:408
  169.2 5.9 fusion.13
  175.1 3.7 slice_bitcast_fusion.8
  178.9 1.2 slice_bitcast_fusion.13
  180.8 1.2 slice_bitcast_fusion.14
  182.7 1.9 dynamic-slice_bitcast_fusion.x_own
  184.6 1.9 dynamic-slice_bitcast_fusion.1.x_own
  187.3 9.4 %slice_bitcast_fusion.4 = (bf16[4,2048,128]{2,1,0:T(8,128)(2,1)}, bf16[4,2048,128]{2,1,0:T(8,128)(2,1)}, bf16[4,2048,128]{2,1,0:T(8,128)(2,1)}, bf16[4,2048,128]...) fusion(bf16[3,4,2048,128]{3,2,1,0:T(8,128)(2,1)} %get-tuple-element.42, ...), kind=kLoop, calls=%fused_computation.8 | loop fusion | bytes 25165824 | tf_op jit(solution)/shard_map/squeeze | solution.py:536
  196.7 15.4 %attend_backward.5 = (bf16[2048,512]{1,0:T(8,128)(2,1)}, f32[4,384,512]{2,1,0:T(8,128)}, f32[4,8,128]{2,1,0:T(8,128)}, f32[4,8,128]{2,1,0:T(8,128)}) custom-call(s32[1]{0:T(128)} %get-tuple-element.111.length_ref, s32[1]{0:T(128)} %bitcast.9.place_ref, bf16[2048,512]{1,0:T(8,128)(2,1)} %get-tuple-element.84.x_all, ...), custom_call_target="tpu_custom_call" | custom-call | flops 21474836480 | bytes 16777216 | tf_op jit(solution)/shard_map/attend_backward/pallas_call | solution.py:464
  212.1 37.8 %attend_backward.4 = (bf16[2048,512]{1,0:T(8,128)(2,1)}, f32[4,384,512]{2,1,0:T(8,128)}, f32[4,8,128]{2,1,0:T(8,128)}, f32[4,8,128]{2,1,0:T(8,128)}) custom-call(s32[1]{0:T(128)} %get-tuple-element.112.length_ref, s32[1]{0:T(128)} %bitcast.9.place_ref, bf16[2048,512]{1,0:T(8,128)(2,1)} %get-tuple-element.83.x_all, ...), custom_call_target="tpu_custom_call" | custom-call | flops 21474836480 | bytes 16777216 | tf_op jit(solution)/shard_map/attend_backward/pallas_call | solution.py:464
  249.9 30.9 %attend_backward.3 = (bf16[2048,512]{1,0:T(8,128)(2,1)}, f32[4,384,512]{2,1,0:T(8,128)}, f32[4,8,128]{2,1,0:T(8,128)}, f32[4,8,128]{2,1,0:T(8,128)}) custom-call(s32[1]{0:T(128)} %get-tuple-element.110.length_ref, s32[1]{0:T(128)} %bitcast.9.place_ref, bf16[2048,512]{1,0:T(8,128)(2,1)} %get-tuple-element.82.x_all, ...), custom_call_target="tpu_custom_call" | custom-call | flops 21474836480 | bytes 16777216 | tf_op jit(solution)/shard_map/attend_backward/pallas_call | solution.py:464
  280.8 2.8 add_convert_fusion
  283.6 1.3 copy.28
  285.5 61.5 %reduce-scatter.11.cloned.1.call-done = bf16[384,512]{1,0:T(8,128)(2,1)} async-done(((bf16[1536,512]{1,0:T(8,128)(2,1)}), bf16[384,512]{1,0:T(8,128)(2,1)}) %reduce-scatter.11.cloned.1.call-update) | async-done | bytes 393232 | tf_op jit(solution)/shard_map/reduce_scatter | solution.py:545
  350.7 197.3 %all-reduce.5.cloned.1.call-done = bf16[4608,512]{1,0:T(8,128)(2,1)} async-done(((bf16[4608,512]{1,0:T(8,128)(2,1)}), bf16[4608,512]{1,0:T(8,128)(2,1)}) %all-reduce.5.cloned.1.call-update) | async-done | bytes 4718608 | tf_op jit(solution)/shard_map/psum | solution.py:522
  547.9 4.9 slice_convert_fusion
  553.5 2.7 copy.31
  556.1 1.6 dynamic-slice_convert_fusion
  557.8 45.7 %all-reduce.3.cloned.1.call-done = bf16[512,384]{0,1:T(8,128)(2,1)} async-done(((bf16[512,384]{0,1:T(8,128)(2,1)}), bf16[512,384]{0,1:T(8,128)(2,1)}) %all-reduce.3.cloned.1.call-update) | async-done | bytes 393232 | tf_op jit(solution)/shard_map/psum | solution.py:545
  603.4 2.0 copy.30
  605.5 2.4 fusion
  608.2 39.7 %psum.21 = f32[12288]{0:T(1024)S(1)} all-reduce(f32[12288]{0:T(1024)S(1)} %constant_dynamic-update-slice_fusion), channel_id=1, replica_groups=mesh['dp'=8,'mp'=4] {'dp','mp'}, use_global_device_ids=true, to_apply=%region_6.0 | all-reduce | flops 12288 | bytes 98304 | tf_op jit(solution)/shard_map/psum | solution.py:552
  651.0 2.0 maximum_bitcast_fusion
  (62 shorter events, 13.4 us)
Async XLA Ops:
  8.0 339.0 %reduce-scatter.11.cloned.1.call-start = ((), (), s32[]{:S(2)}) async-start(), calls=%async_computation.7 | async-start | bytes 1966080 | tf_op jit(solution)/shard_map/reduce_scatter | solution.py:545
  10.1 0.7 copy-start.8
  10.8 0.6 copy-start.7
  175.1 3.7 copy-start.4
  178.9 2.0 copy-start.3
  180.1 2.0 copy-start.5
  249.9 30.9 %copy-start = (f32[4,384,512]{2,1,0:T(8,128)S(1)}, f32[4,384,512]{2,1,0:T(8,128)}, u32[]{:S(2)}) copy-start(f32[4,384,512]{2,1,0:T(8,128)} %get-tuple-element.58) | copy-start | bytes 9437188
  249.9 30.9 %copy-start.1 = (f32[4,384,512]{2,1,0:T(8,128)S(1)}, f32[4,384,512]{2,1,0:T(8,128)}, u32[]{:S(2)}) copy-start(f32[4,384,512]{2,1,0:T(8,128)} %get-tuple-element.57) | copy-start | bytes 9437188
  284.9 263.0 %all-reduce.5.cloned.1.call-start = ((), (), s32[]{:S(2)}) async-start(), calls=%async_computation.9 | async-start | bytes 9437184 | tf_op jit(solution)/shard_map/psum | solution.py:522
  285.5 318.0 %all-reduce.3.cloned.1.call-start = ((), (), s32[]{:S(2)}) async-start(), calls=%async_computation.8 | async-start | bytes 786432 | tf_op jit(solution)/shard_map/psum | solution.py:545
  347.0 258.5 %reduce-scatter.9.cloned.1.call-start = ((), (), s32[]{:S(2)}) async-start(), calls=%async_computation.6 | async-start | bytes 2621440 | tf_op jit(solution)/shard_map/reduce_scatter | solution.py:537
  347.8 257.7 %reduce-scatter.7.cloned.1.call-start = ((), (), s32[]{:S(2)}) async-start(), calls=%async_computation.5 | async-start | bytes 2621440 | tf_op jit(solution)/shard_map/reduce_scatter | solution.py:537
  347.8 1.3 copy-start.6
  348.5 257.0 %reduce-scatter.5.cloned.1.call-start = ((), (), s32[]{:S(2)}) async-start(), calls=%async_computation.4 | async-start | bytes 2621440 | tf_op jit(solution)/shard_map/reduce_scatter | solution.py:537
  605.5 2.4 copy-start.9
  651.0 2.0 copy-start.2
Sparse Core Ops, SparseCore 0:
  285.0 61.9 reduce-scatter.10
  350.2 47.8 reduce-scatter.8
  400.4 45.7 reduce-scatter.6
  448.4 45.2 reduce-scatter.4
Sparse Core Ops, SparseCore 1:
  292.0 255.9 all-reduce.4
  550.9 52.5 all-reduce.2

commit v3 on v2

--- a/solution.py
+++ b/solution.py
@@ -10,7 +10,6 @@
 
 HD = 64
 PAIR = 2 * HD
-HIGHEST = lax.Precision.HIGHEST
 NEGATIVE = -1e30
 LOG2E = math.log2(math.e)
 F32 = jnp.float32
@@ -44,70 +43,10 @@
     return op(values.reshape(rows // 8, 8, lanes), axis=0)
 
 
-def attend_backward(length_ref, place_ref, x_all, x_own, weight, q_in, k_in, v_in, att_t, lse, grad_in,
-                    x_grad, w_grad, qb_grad, vb_grad, x_acc, kv_grad, dq_acc, *, block):
-    length = length_ref[0]
-    blocks = (length + block - 1) // block
-    rows = x_own.shape[0]
-    pair = pl.program_id(0)
-    full = x_all.shape[0]
-    q_pair = q_in[0]
-    grad_pair = grad_in[...]
-    q_heads = [one_head(q_pair, h) for h in range(2)]
-    g_heads = [one_head(grad_pair, h) for h in range(2)]
-    prod = grad_pair.astype(F32).T * att_t[0]
-    delta = [jnp.sum(prod[h * HD:(h + 1) * HD], axis=0, keepdims=True) for h in range(2)]
-    tops = [lse[0, h:h + 1, :] for h in range(2)]
-    dq_acc[...] = jnp.zeros_like(dq_acc)
-
-    @pl.when(pair == 0)
-    def _():
-        x_acc[...] = jnp.zeros_like(x_acc)
-
-    w_grad[0] = jnp.zeros(w_grad.shape[1:], F32)
-
-    def step(j, vsum):
-        at = pl.ds(pl.multiple_of(j * block, block), block)
-        k_blk = k_in[0, at, :]
-        v_blk = v_in[0, at, :]
-        keep = (lax.broadcasted_iota(jnp.int32, (block, rows), 0) + j * block) < length
-        dk = jnp.zeros((block, PAIR), F32)
-        dv = jnp.zeros((block, PAIR), F32)
-        for h in range(2):
-            s = nt(k_blk, q_heads[h]) * LOG2E
-            p = jnp.where(keep, jnp.exp2(s - tops[h]), 0.0)
-            dp = nt(v_blk, g_heads[h])
-            ds = (p * (dp - delta[h])).astype(BF16)
-            dv += nn(p.astype(BF16), g_heads[h])
-            dk += nn(ds, q_heads[h])
-            dq_acc[h] += tn(k_blk, ds)
-        dv = dv.astype(BF16)
-        both = jnp.concatenate([dk.astype(BF16), dv], axis=1)
-        x_acc[at, :] += nn(both, weight[0, PAIR:, :])
-        w_grad[0, PAIR:, :] += tn(both, x_all[at, :])
-        return vsum + fold8(dv.astype(F32), jnp.sum)
-
-    vsum = lax.fori_loop(0, blocks, step, jnp.zeros((8, PAIR), F32))
-    vb_grad[0] = jnp.broadcast_to(jnp.sum(vsum, axis=0, keepdims=True), (8, PAIR))
-    dq_t = jnp.concatenate([dq_acc[h, h * HD:(h + 1) * HD, :] for h in range(2)], axis=0) * (HD ** -0.5)
-    dq = dq_t.T.astype(BF16)
-    qb_grad[0] = jnp.broadcast_to(jnp.sum(dq.astype(F32), axis=0, keepdims=True), (8, PAIR))
-    mine = pl.ds(pl.multiple_of(place_ref[0] * rows, rows), rows)
-    x_acc[mine, :] += nn(dq, weight[0, :PAIR, :])
-    w_grad[0, :PAIR, :] += tn(dq, x_own[...])
-
-    @pl.when(pair == pl.num_programs(0) - 1)
-    def _():
-        x_grad[...] = x_acc[...].astype(BF16)
-
-
-def whole(shape):
-    return pl.BlockSpec(shape, lambda *_: (0,) * len(shape))
-
-
 MESH = pl.DeviceIdType.MESH
 CONSTANT = pl.Buffered(1)
 PIECES = 8
+TAIL_POINTS = (0, 2, 3, 4, 6, 7, 8, 9, 11, 12)
 
 
 class Relay:
@@ -168,7 +107,7 @@
                   lengths, pair_ids, tok, embed, cot, qkv_w, q_bias, v_bias, out_w, b_out,
                   w_in, b_in, w_last, b_last,
                   x_out, w_out, q_out, k_out, v_out, att_t_out, lse_out,
-                  result, mixed_grad, att_grad, g_all, g_bias,
+                  result, mixed_grad, att_grad, g_all,
                   x_all, w_all, w_o, biases, s_all, acc, att_rows_all, grads, grad_rows,
                   x_send, x_recv, x_copy, w_send, w_recv, plane_send, plane_recv):
     seq, pair = pl.program_id(0), pl.program_id(1)
@@ -382,7 +321,9 @@
             return 0
 
         lax.fori_loop(0, grads.shape[0] // width, narrow, 0)
-        g_bias[...] = grad_rows[...]
+        rest = g_all.shape[0] - grads.shape[0]
+        g_all[grads.shape[0]:, :] = jnp.concatenate(
+            [grad_rows[...], jnp.zeros((rest - 8, width), F32)], axis=0).astype(BF16)
         for s in range(seqs):
             x_relay(s).drain()
             hbm_copy(s).wait()
@@ -401,6 +342,7 @@
     pairs = width // PAIR
     block = min(512, full)
     w_rows = -(-(heads_dev * 4 * HD + 16) // (16 * PIECES)) * 16 * PIECES
+    g_rows = -(-(2 * hidden + width + 16) // 1024) * 1024
     in_smem = pl.BlockSpec(memory_space=pltpu.SMEM)
     per_seq = lambda: pl.BlockSpec((1, rows, width), lambda s, p: (s, 0, 0))
     per_pair = lambda *tail: pl.BlockSpec((1, 1) + tail, lambda s, p: (s, p, 0, 0))
@@ -414,7 +356,7 @@
         out_specs=[pl.BlockSpec(memory_space=pl.ANY), fixed((pairs, 3 * PAIR, width)),
                    per_pair(rows, PAIR), per_pair(full, PAIR), per_pair(full, PAIR),
                    per_pair(PAIR, rows), per_pair(8, rows),
-                   per_seq(), per_seq(), per_seq(), fixed((2 * hidden + width, width)), fixed((8, width))],
+                   per_seq(), per_seq(), per_seq(), fixed((g_rows, width))],
         out_shape=[
             shape((seqs, full, width), BF16),
             shape((pairs, 3 * PAIR, width), BF16),
@@ -426,8 +368,7 @@
             shape((seqs, rows, width), BF16),
             shape((seqs, rows, width), BF16),
             shape((seqs, rows, width), BF16),
-            shape((2 * hidden + width, width), BF16),
-            shape((8, width), F32),
+            shape((g_rows, width), BF16),
         ],
         scratch_shapes=[
             pltpu.VMEM((seqs, full, width), BF16),
@@ -455,36 +396,443 @@
     )(lengths, pair_ids, tok, embed, cot, qkv_w, q_bias, v_bias, out_w, b_out, w_in, b_in, w_last, b_last)
 
 
-def call_backward(length, place, x_all, x_own, weight, q, k, v, att_t, lse, grad):
-    full, width = x_all.shape
-    rows = x_own.shape[0]
+def row_step(size):
+    for step in (256, 160, 128, 80, 64, 32, 16):
+        if size % step == 0:
+            return step
+    return size
+
+
+def aligned(start, size, unit=16):
+    return pl.ds(pl.multiple_of(start, unit), size)
+
+
+class Reducer:
+    def __init__(self, data, land, group, rows, bits, where_at, send_sem, recv_sem, free_sem=None):
+        self.data, self.land, self.group = data, land, group
+        self.send_sem, self.recv_sem, self.free_sem = send_sem, recv_sem, free_sem
+        self.stages, self.landed = [], 0
+        start, size = 0, rows
+        for axis, bit in bits:
+            index = where_at[axis]
+            digit = (index // bit) % 2
+            halves = (size // 2) % 16 == 0
+            if halves:
+                size //= 2
+                keep, other = start + digit * size, start + (1 - digit) * size
+            else:
+                keep = other = start
+            self.stages.append((axis, flip(index, bit), halves, keep, other, size, self.landed))
+            self.landed += size
+            start = keep
+        self.start, self.size = start, size
+
+    def copy(self, j):
+        axis, partner, _, _, other, size, landed = self.stages[j]
+        return pltpu.make_async_remote_copy(
+            src_ref=self.data.at[self.group, :, aligned(other, size)],
+            dst_ref=self.land.at[self.group, :, pl.ds(landed, size)],
+            send_sem=self.send_sem.at[self.group, j],
+            recv_sem=self.recv_sem.at[self.group, j],
+            device_id={axis: partner}, device_id_type=MESH)
+
+    def finish(self, j):
+        self.copy(j).wait()
+        axis, partner, halves, keep, _, size, landed = self.stages[j]
+        if self.free_sem is not None and halves:
+            pl.semaphore_signal(self.free_sem.at[self.group, j], 1, device_id={axis: partner},
+                                device_id_type=MESH)
+        step = row_step(size)
+        slots = self.data.shape[1]
+        for slot in range(slots):
+            def add(r, _):
+                at = aligned(keep + r * step, step)
+                more = self.land[self.group, slot, aligned(landed + r * step, step), :]
+                self.data[self.group, slot, at, :] = (
+                    self.data[self.group, slot, at, :].astype(F32) + more.astype(F32)).astype(BF16)
+                return 0
+
+            lax.fori_loop(0, size // step, add, 0)
+
+    def back(self, j):
+        axis, partner, _, keep, _, size, _ = self.stages[j]
+        view = self.data.at[self.group, :, aligned(keep, size)]
+        at = len(self.stages) + j
+        return pltpu.make_async_remote_copy(
+            src_ref=view, dst_ref=view, send_sem=self.send_sem.at[self.group, at],
+            recv_sem=self.recv_sem.at[self.group, at],
+            device_id={axis: partner}, device_id_type=MESH)
+
+    def back_start(self, j):
+        pl.semaphore_wait(self.free_sem.at[self.group, j], 1)
+        self.back(j).start()
+
+    def events(self):
+        doubling = [j for j in range(len(self.stages)) if self.stages[j][2]][::-1]
+        run = [lambda: self.copy(0).start()]
+        for j in range(len(self.stages)):
+            def after(j=j):
+                self.finish(j)
+                if j + 1 < len(self.stages):
+                    self.copy(j + 1).start()
+                elif doubling:
+                    self.back_start(doubling[0])
+            run.append(after)
+        for i, j in enumerate(doubling):
+            def after_back(i=i, j=j):
+                self.back(j).wait()
+                if i + 1 < len(doubling):
+                    self.back_start(doubling[i + 1])
+            run.append(after_back)
+        return run
+
+
+def bit_list(size):
+    return [1 << b for b in range(size.bit_length() - 1)]
+
+
+def far_first(count):
+    table = []
+    for m in range(count):
+        order = []
+        for k in range(count - 1, 0, -1):
+            order += [c for c in (m + k, m - k) if 0 <= c < count]
+        table.append(order + [m])
+    return table
+
+
+def backward_layer(count, data_count, heads_dev, tail_points,
+                   lengths, pair_ids, x_seq, weight, q_in, k_in, v_in, att_t, lse, grad_in, mixed_grad, g_in,
+                   token_grad, g_out, own_out,
+                   a_buf, a_land, b_buf, b_land, b_parts, own_buf, parts, land, x_acc, dq_acc, delta_all,
+                   w_acc, bias_acc, col_acc, table_acc,
+                   load_sem, a_send, a_recv, a_free, b_send, b_recv, s_send, s_recv, r_send, r_recv):
+    seq, turn = pl.program_id(0), pl.program_id(1)
+    seqs, pairs = token_grad.shape[0], weight.shape[0]
+    rows, width = token_grad.shape[1], token_grad.shape[2]
+    place, data_at = lax.axis_index("mp"), lax.axis_index("dp")
+    where_at = {"mp": place, "dp": data_at}
+    point = seq * count + turn
+    data_bits, place_bits = bit_list(data_count), bit_list(count)
+    swapped = [{2: 4, 4: 2}.get(b, b) for b in data_bits]
+
+    order = far_first(count)
+    chunk = sum(jnp.where((place == m) & (turn == i), order[m][i], 0)
+                for m in range(count) for i in range(count))
+
+    a_sums = [
+        Reducer(a_buf, a_land, g, a_buf.shape[2],
+                [("dp", b) for b in (data_bits, swapped)[g]] + [("mp", b) for b in place_bits],
+                where_at, a_send, a_recv, a_free)
+        for g in range(2)]
+    a_events = [s.events() for s in a_sums]
+    b_sums = [
+        Reducer(b_buf, b_land, g, b_buf.shape[2], [("dp", b) for b in (data_bits, swapped)[g]],
+                where_at, b_send, b_recv)
+        for g in range(2)]
+
+    def send_part(s, c, downward):
+        slot = jnp.where((place - 1 == c) & (downward == 1), count, c)
+        return pltpu.make_async_remote_copy(
+            src_ref=parts.at[s, c], dst_ref=land.at[s, slot],
+            send_sem=s_send.at[s, c], recv_sem=s_recv.at[s, slot],
+            device_id={"mp": place - 1 if downward else place + 1}, device_id_type=MESH)
+
+    def await_part(s, slot):
+        pltpu.make_async_remote_copy(
+            src_ref=land.at[s, slot], dst_ref=land.at[s, slot],
+            send_sem=s_send.at[s, 0], recv_sem=s_recv.at[s, slot],
+            device_id={"mp": (place + 1) % count}, device_id_type=MESH).wait_recv()
+
+    def combine(s, k):
+        for downward in (0, 1):
+            c = place - k if downward else place + k
+            go = ((c >= 0) & (place + 1 < count)) if downward else ((c < count) & (place >= 1))
+
+            @pl.when(go)
+            def _():
+                await_part(s, c)
+                parts[s, c] = (parts[s, c].astype(F32) + land[s, c].astype(F32)).astype(BF16)
+                send_part(s, c, downward).start()
+
+    def conclude(s):
+        for downward in (0, 1):
+            slot = count if downward else place
+
+            @pl.when((place + 1 < count) if downward else (place >= 1))
+            def _():
+                await_part(s, slot)
+                token_grad[s] += land[s, slot].astype(F32)
+
+    def load():
+        return pltpu.make_async_copy(g_in, a_buf, load_sem.at[0])
+
+    def store():
+        return pltpu.make_async_copy(a_buf, g_out, load_sem.at[1])
+
+    partners = [flip(data_at, b) for b in data_bits]
+
+    @pl.when(point == 0)
+    def _():
+        greet(place, count, partners)
+        load().start()
+        w_acc[...] = jnp.zeros_like(w_acc)
+        bias_acc[...] = jnp.zeros_like(bias_acc)
+        table_acc[...] = jnp.zeros_like(table_acc)
+        await_greetings(count, partners)
+        load().wait()
+        for events in a_events:
+            events[0]()
+
+    @pl.when(turn == 0)
+    def _():
+        col_acc[...] = jnp.zeros_like(col_acc)
+        dq_acc[...] = jnp.zeros_like(dq_acc)
+        for p in range(pairs):
+            prod = grad_in[0, :, p * PAIR:(p + 1) * PAIR].astype(F32).T * att_t[0, p]
+            delta_all[p, 0:1, :] = jnp.sum(prod[:HD], axis=0, keepdims=True)
+            delta_all[p, 1:2, :] = jnp.sum(prod[HD:], axis=0, keepdims=True)
+
+    length = lengths[seq]
+    at = aligned(chunk * rows, rows, rows)
+    own = aligned(place * rows, rows, rows)
+    x_acc[...] = jnp.zeros_like(x_acc)
+
+    def pair_step(p, _):
+        lanes = aligned(p * PAIR, PAIR, PAIR)
+        q_pair = q_in[0, p]
+        grad_pair = grad_in[0, :, lanes]
+        k_blk = k_in[0, p, at, :]
+        v_blk = v_in[0, p, at, :]
+        keep = (lax.broadcasted_iota(jnp.int32, (rows, rows), 0) + chunk * rows) < length
+        dk = jnp.zeros((rows, PAIR), F32)
+        dv = jnp.zeros((rows, PAIR), F32)
+        for h in range(2):
+            q_head, g_head = one_head(q_pair, h), one_head(grad_pair, h)
+            s = jnp.where(keep, nt(k_blk, q_head) * LOG2E, NEGATIVE)
+            pr = jnp.exp2(s - lse[0, p, h:h + 1, :])
+            dp = nt(v_blk, g_head)
+            ds = (pr * (dp - delta_all[p, h:h + 1, :])).astype(BF16)
+            dv += nn(pr.astype(BF16), g_head)
+            dk += nn(ds, q_head)
+            dq_acc[p, h] += tn(k_blk, ds)
+        dv = dv.astype(BF16)
+        both = jnp.concatenate([dk.astype(BF16), dv], axis=1)
+        x_acc[...] += nn(both, weight[p, PAIR:, :])
+        w_acc[p, PAIR:, :] += tn(both, x_seq[0, at, :])
+        bias_acc[1:2, lanes] += jnp.sum(dv.astype(F32), axis=0, keepdims=True)
+        return 0
+
+    lax.fori_loop(0, pairs, pair_step, 0)
+
+    @pl.when(turn < count - 1)
+    def _():
+        parts[seq, chunk] = x_acc[...].astype(BF16)
+        for downward in (0, 1):
+            @pl.when((place == (count - 1 if downward else 0)) & (chunk != place))
+            def _():
+                send_part(seq, chunk, downward).start()
+
+    @pl.when(turn == count - 1)
+    def _():
+        def query_step(p, _):
+            lanes = aligned(p * PAIR, PAIR, PAIR)
+            dq_t = jnp.concatenate(
+                [dq_acc[p, h, h * HD:(h + 1) * HD, :] for h in range(2)], axis=0) * (HD ** -0.5)
+            dq = dq_t.T.astype(BF16)
+            x_acc[...] += nn(dq, weight[p, :PAIR, :])
+            w_acc[p, :PAIR, :] += tn(dq, x_seq[0, own, :])
+            bias_acc[0:1, lanes] += jnp.sum(dq.astype(F32), axis=0, keepdims=True)
+            return 0
+
+        lax.fori_loop(0, pairs, query_step, 0)
+        x_acc[...] += mixed_grad[0].astype(F32)
+        token_grad[seq] = x_acc[...]
+
+    col_acc[0:1, :] += jnp.sum(x_acc[...], axis=0, keepdims=True)
+
+    @pl.when(turn == count - 1)
+    def _():
+        line = lax.broadcasted_iota(jnp.int32, table_acc.shape, 0)
+        table_acc[...] += jnp.where(line == pair_ids[seq], col_acc[0:1, :], 0.0)
+
+    slots = {2: 2, 1: 4} if count == 4 else {k: count + (count - 2 - k) for k in range(1, count - 1)}
+    for k in range(count - 2, 0, -1):
+        turns, seq_back = slots[k] % count, slots[k] // count
+
+        @pl.when((turn == turns) & (seq >= seq_back))
+        def _():
+            combine(seq - seq_back, k)
+
+    @pl.when((turn == count - 1) & (seq >= 1))
+    def _():
+        conclude(seq - 1)
+
+    total = seqs * count
+    later = len(a_events[0]) - 1
+    in_tail = []
+    for e in range(1, later + 1):
+        when_at = tail_points[e - 1] if tail_points else (e * total) // (later + 1)
+        if when_at >= total:
+            in_tail.append(e)
+            continue
+
+        @pl.when(point == when_at)
+        def _():
+            for events in a_events:
+                events[e]()
+
+    @pl.when(point == total - 1)
+    def _():
+        last = seqs - 1
+        base = heads_dev * 3 * HD
+        half = count // 2
+        for m in range(count):
+            g, slot = m // half, m % half
+            if heads_dev == 2:
+                b_buf[g, slot, 0:base, :] = w_acc[m].astype(BF16)
+            else:
+                for j in range(3):
+                    lo = j * PAIR + (m % 2) * HD
+                    b_buf[g, slot, j * HD:(j + 1) * HD, :] = w_acc[m // 2, lo:lo + HD, :].astype(BF16)
+            b_buf[g, slot, base:base + 16, :] = bias_acc[...].astype(BF16)
+            b_buf[g, slot, base + 16:base + 32, :] = table_acc[...].astype(BF16)
+            rest = b_buf.shape[2] - base - 32
+            b_buf[g, slot, base + 32:, :] = jnp.zeros((rest, width), BF16)
+        stages = len(b_sums[0].stages)
+        for b in b_sums:
+            b.copy(0).start()
+        tail_k = [k for k in range(count - 2, 0, -1) if slots[k] >= count]
+        for j in range(stages):
+            for b in b_sums:
+                b.finish(j)
+                if j + 1 < stages:
+                    b.copy(j + 1).start()
+            if tail_k:
+                combine(last, tail_k.pop(0))
+        strip = b_sums[0].size
+        mine = place // half
+        start = jnp.where(mine == 0, b_sums[0].start, b_sums[1].start)
+
+        def scatter(k):
+            target = (place + k) % count
+            g = target // half
+            begin = jnp.where(g == 0, b_sums[0].start, b_sums[1].start)
+            return pltpu.make_async_remote_copy(
+                src_ref=b_buf.at[g, target % half, aligned(begin, strip)],
+                dst_ref=b_parts.at[k - 1],
+                send_sem=r_send.at[k - 1], recv_sem=r_recv.at[k - 1],
+                device_id={"mp": target}, device_id_type=MESH)
+
+        for k in range(1, count):
+            scatter(k).start()
+        for k in tail_k:
+            combine(last, k)
+        for e in in_tail:
+            for events in a_events:
+                events[e]()
+        store().start()
+        for k in range(1, count):
+            scatter(k).wait()
+        home = b_buf[mine, place % half, aligned(start, strip), :].astype(F32)
+        for k in range(1, count):
+            home += b_parts[k - 1].astype(F32)
+        own_buf[aligned(start, strip), :] = home.astype(BF16)
+
+        def back(j):
+            partner = jnp.where(mine == 0, b_sums[0].stages[j][1], b_sums[1].stages[j][1])
+            keep = jnp.where(mine == 0, b_sums[0].stages[j][3], b_sums[1].stages[j][3])
+            size = b_sums[0].stages[j][5]
+            view = own_buf.at[aligned(keep, size)]
+            return pltpu.make_async_remote_copy(
+                src_ref=view, dst_ref=view, send_sem=r_send.at[count - 1 + j],
+                recv_sem=r_recv.at[count - 1 + j], device_id={"dp": partner}, device_id_type=MESH)
+
+        for j in reversed(range(stages)):
+            back(j).start()
+            back(j).wait()
+        own_out[...] = own_buf[...]
+        conclude(last)
+        store().wait()
+        for s in range(seqs):
+            for k in range(1, count):
+                for downward in (0, 1):
+                    c = place - k if downward else place + k
+
+                    @pl.when((c >= 0) if downward else (c < count))
+                    def _():
+                        send_part(s, c, downward).wait_send()
+
+
+def call_backward(count, data_count, heads_dev, lengths, pair_ids, x_all, weight, q, k, v, att_t, lse,
+                  grad, mixed_grad, g_all):
+    seqs, full, width = x_all.shape
+    rows = full // count
     pairs = weight.shape[0]
-    block = min(512, full)
-    per_pair = lambda *tail: pl.BlockSpec((1,) + tail, lambda p, *_: (p, 0, 0))
+    a_rows = g_all.shape[0] // 2
+    base = heads_dev * 3 * HD
+    slot_rows = -(-(base + 32) // 128) * 128
+    data_bits, place_bits = bit_list(data_count), bit_list(count)
+
+    def landing(size, bits):
+        landed = 0
+        for _ in range(bits):
+            size = size // 2 if (size // 2) % 16 == 0 else size
+            landed += size
+        return landed, size
+
+    a_landed, _ = landing(a_rows, len(data_bits) + len(place_bits))
+    b_landed, strip = landing(slot_rows, len(data_bits))
+    a_stages, b_stages = len(data_bits) + len(place_bits), len(data_bits)
+    tail_points = TAIL_POINTS if (count, data_count) == (4, 8) else None
+    in_smem = pl.BlockSpec(memory_space=pltpu.SMEM)
+    in_hbm = pl.BlockSpec(memory_space=pl.ANY)
+    seq_block = lambda shape, mode=None: pl.BlockSpec(
+        (1,) + shape[1:], lambda s, i: (s,) + (0,) * (len(shape) - 1), pipeline_mode=mode)
+    shape = jax.ShapeDtypeStruct
+    dma = pltpu.SemaphoreType.DMA
     return pl.pallas_call(
-        functools.partial(attend_backward, block=block),
-        grid_spec=pltpu.PrefetchScalarGridSpec(
-            num_scalar_prefetch=2,
-            grid=(pairs,),
-            in_specs=[whole((full, width)), whole((rows, width)), per_pair(3 * PAIR, width),
-                      per_pair(rows, PAIR), per_pair(full, PAIR), per_pair(full, PAIR),
-                      per_pair(PAIR, rows), per_pair(8, rows),
-                      pl.BlockSpec((rows, PAIR), lambda p, *_: (0, p))],
-            out_specs=[whole((full, width)), per_pair(3 * PAIR, width), per_pair(8, PAIR), per_pair(8, PAIR)],
-            scratch_shapes=[pltpu.VMEM((full, width), F32), pltpu.VMEM((full, 2 * PAIR), BF16),
-                            pltpu.VMEM((2, PAIR, rows), F32)],
-        ),
+        functools.partial(backward_layer, count, data_count, heads_dev, tail_points),
+        grid=(seqs, count),
+        in_specs=[in_smem, in_smem, seq_block(x_all.shape, CONSTANT), fixed(weight.shape),
+                  seq_block(q.shape, CONSTANT), seq_block(k.shape, CONSTANT),
+                  seq_block(v.shape, CONSTANT), seq_block(att_t.shape, CONSTANT),
+                  seq_block(lse.shape), seq_block(grad.shape), seq_block(mixed_grad.shape), in_hbm],
+        out_specs=[fixed((seqs, rows, width)), in_hbm, fixed((slot_rows, width))],
         out_shape=[
-            jax.ShapeDtypeStruct((full, width), BF16),
-            jax.ShapeDtypeStruct((pairs, 3 * PAIR, width), F32),
-            jax.ShapeDtypeStruct((pairs, 8, PAIR), F32),
-            jax.ShapeDtypeStruct((pairs, 8, PAIR), F32),
+            shape((seqs, rows, width), F32),
+            shape((2, 1, a_rows, width), BF16),
+            shape((slot_rows, width), BF16),
         ],
-        cost_estimate=pl.CostEstimate(flops=40 * pairs * full * rows * PAIR, bytes_accessed=16 << 20,
-                                      transcendentals=2 * pairs * full * rows),
-        compiler_params=pltpu.CompilerParams(vmem_limit_bytes=VMEM_LIMIT),
-        name="attend_backward",
-    )(length, place, x_all, x_own, weight, q, k, v, att_t, lse, grad)
+        scratch_shapes=[
+            pltpu.VMEM((2, 1, a_rows, width), BF16),
+            pltpu.VMEM((2, 1, a_landed, width), BF16),
+            pltpu.VMEM((2, count // 2, slot_rows, width), BF16),
+            pltpu.VMEM((2, count // 2, b_landed, width), BF16),
+            pltpu.VMEM((count - 1, strip, width), BF16),
+            pltpu.VMEM((slot_rows, width), BF16),
+            pltpu.VMEM((seqs, count, rows, width), BF16),
+            pltpu.VMEM((seqs, count + 1, rows, width), BF16),
+            pltpu.VMEM((rows, width), F32),
+            pltpu.VMEM((pairs, 2, PAIR, rows), F32),
+            pltpu.VMEM((pairs, 8, rows), F32),
+            pltpu.VMEM((pairs, 3 * PAIR, width), F32),
+            pltpu.VMEM((16, width), F32),
+            pltpu.VMEM((8, width), F32),
+            pltpu.VMEM((16, width), F32),
+            dma((2,)), dma((2, 2 * a_stages)), dma((2, 2 * a_stages)),
+            pltpu.SemaphoreType.REGULAR((2, a_stages)),
+            dma((2, b_stages)), dma((2, b_stages)),
+            dma((seqs, count)), dma((seqs, count + 1)),
+            dma((count - 1 + b_stages,)), dma((count - 1 + b_stages,)),
+        ],
+        cost_estimate=pl.CostEstimate(flops=200 * 10 ** 9, bytes_accessed=60 << 20,
+                                      transcendentals=seqs * pairs * 2 * full * rows),
+        compiler_params=pltpu.CompilerParams(
+            collective_id=1, has_side_effects=True, vmem_limit_bytes=VMEM_LIMIT),
+        name="backward_layer",
+    )(lengths, pair_ids, x_all, weight, q, k, v, att_t, lse, grad, mixed_grad,
+      g_all.reshape(2, 1, a_rows, width))
 
 
 def body(
@@ -509,69 +857,46 @@
     place = lax.axis_index("mp").astype(jnp.int32).reshape(1)
     tok = jnp.transpose(tokens, (1, 0, 2))
     cot = jnp.transpose(cotangent, (1, 0, 2))
-    select = (pair_ids[:, None] == lax.iota(jnp.int32, table_rows)[None, :]).astype(F32)
     bias_len = q_bias.shape[0]
     spread = lambda v: lax.dynamic_update_slice(
         jnp.zeros((1, width), BF16), v[None], (0, place[0] * bias_len))
-    (x_all, w_pairs, q, k, v, att_t, lse, result, mixed_grad, att_grad, g_all, g_bias) = call_layer(
+    (x_all, w_pairs, q, k, v, att_t, lse, result, mixed_grad, att_grad, g_all) = call_layer(
         count, lengths, pair_ids, tok, pair_embed, cot, qkv_weight, spread(q_bias), spread(v_bias),
         out_weight, out_bias[None], ffn_in_weight, ffn_in_bias[None], ffn_out_weight,
         ffn_out_bias[None])
+    heads_dev = bias_len // HD
+    tokens_grad, g_sum, own = call_backward(
+        count, lax.axis_size("dp"), heads_dev, lengths, pair_ids, x_all, w_pairs, q, k, v, att_t, lse,
+        att_grad, mixed_grad, g_all)
+
     hidden = ffn_in_weight.shape[1]
-    pairs = w_pairs.shape[0]
-    g_sum = lax.psum(g_all, ("dp", "mp"))
-    g_last_sum = g_sum[:hidden]
+    g_sum = g_sum.reshape(-1, width)
+    g_last_sum = g_sum[:hidden].astype(F32)
     g_in_sum = jnp.transpose(
-        g_sum[hidden:2 * hidden].reshape(hidden // width, width, width), (1, 0, 2)).reshape(width, hidden)
+        g_sum[hidden:2 * hidden].reshape(hidden // width, width, width), (1, 0, 2)
+    ).reshape(width, hidden).astype(F32)
     out_rows = out_weight.shape[0]
-    g_out_own = lax.dynamic_slice_in_dim(g_sum, 2 * hidden + place[0] * out_rows, out_rows)
+    g_out_own = lax.dynamic_slice_in_dim(
+        g_sum, 2 * hidden + place[0] * out_rows, out_rows).astype(F32)
+    small = g_sum[2 * hidden + width:2 * hidden + width + 8].astype(F32)
     at = hidden // width
-    gb_in, gb_last, gb_out = g_bias[:at].reshape(-1), g_bias[at], g_bias[at + 1]
-
-    token_grads, w_grads, qb_grads, vb_grads = [], [], [], []
-    for s in range(seqs):
-        x_grad, w_grad, qb, vb = call_backward(
-            lengths[s:s + 1], place, x_all[s],
-            lax.dynamic_slice_in_dim(x_all[s], place[0] * local_rows, local_rows),
-            w_pairs, q[s], k[s], v[s], att_t[s], lse[s], att_grad[s])
-        own = lax.psum_scatter(x_grad, "mp", scatter_dimension=0, tiled=True)
-        token_grads.append(mixed_grad[s].astype(F32) + own.astype(F32))
-        w_grads.append(w_grad)
-        qb_grads.append(qb[:, 0])
-        vb_grads.append(vb[:, 0])
-
-    w_grad = sum(w_grads).astype(BF16).reshape(pairs, 3, 2, HD, width)
-    w_grad = jnp.transpose(w_grad, (0, 2, 1, 3, 4)).reshape(pairs * 2 * 3 * HD, width)
-    w_grad = lax.psum(lax.psum_scatter(w_grad, "mp", scatter_dimension=0, tiled=True), "dp")
-    qkv_sum = w_grad.astype(F32).T
-    seq_sums = jnp.stack([jnp.sum(t, axis=0) for t in token_grads])
-    table_grad = lax.dot_general(select, seq_sums, (((0,), (0,)), ((), ())), precision=HIGHEST)
-    small = jnp.concatenate([
-        table_grad.reshape(-1), sum(qb_grads).reshape(-1), sum(vb_grads).reshape(-1),
-        gb_out.reshape(-1), gb_in.reshape(-1), gb_last.reshape(-1)])
-    small = lax.psum(small, ("dp", "mp"))
-    sizes = [table_grad.size, width, width, width, gb_in.size, width]
-    parts, at = [], 0
-    for size in sizes:
-        parts.append(small[at:at + size])
-        at += size
-    table_sum, qb_sum, vb_sum, out_bias_sum, in_bias_sum, last_bias_sum = parts
-    qb_own = lax.dynamic_slice_in_dim(qb_sum, place[0] * bias_len, bias_len)
-    vb_own = lax.dynamic_slice_in_dim(vb_sum, place[0] * bias_len, bias_len)
-    tokens_grad = jnp.transpose(jnp.stack(token_grads), (1, 0, 2))
+    base = heads_dev * 3 * HD
+    qkv_sum = jnp.transpose(
+        own[:base].reshape(3, heads_dev, HD, width), (3, 1, 0, 2)).reshape(width, base).astype(F32)
+    bias_rows = lax.dynamic_slice_in_dim(own[base:base + 2], place[0] * bias_len, bias_len, axis=1)
     return (
         jnp.transpose(result, (1, 0, 2)),
-        tokens_grad,
-        table_sum.reshape(table_rows, width),
+        jnp.transpose(tokens_grad, (1, 0, 2)),
+        own[base + 16:base + 16 + table_rows].astype(F32),
         qkv_sum,
-        qb_own,
-        vb_own,
-        g_out_own.astype(F32),
-        out_bias_sum,
-        g_in_sum.astype(F32),
-        in_bias_sum,
-        g_last_sum.astype(F32),
-        last_bias_sum,
+        bias_rows[0].astype(F32),
+        bias_rows[1].astype(F32),
+        g_out_own,
+        small[at + 1],
+        g_in_sum,
+        small[:at].reshape(-1),
+        g_last_sum,
+        small[at],
     )
 
 

time: 666 us -> 355 us (0.53)
  waiting for transfers between devices: 307 us -> 0 us
  Pallas kernels: 242 us -> 332 us
  blocking collectives: 39.7 us -> 0 us
  local copies, waits for them, and re-layouts: 41 us -> 12.9 us
  between operations: 15.4 us -> 0.71 us
    psum x2 -> x0, waiting for transfers between devices: 243 us -> none  [the longest x1 197 us: body(): g_sum = lax.psum(g_all, ('dp', 'mp'))]
    pallas_call x3 -> x1, Pallas kernels: 84 us -> 174 us  [call_backward(): pl.pallas_call(functools.partial(backward_layer, count, data_count, heads...]
    reduce_scatter x4 -> x0, waiting for transfers between devices: 61.5 us -> none  [the longest x1 61.5 us: body(): lax.psum_scatter(w_grad, 'mp', scatter_dimension=0, tiled=True)]
    psum x1 -> x0, blocking collectives: 39.7 us -> none  [body(): small = lax.psum(small, ('dp', 'mp'))]
    squeeze x5 -> x0, local copies, waits for them, and re-layouts: 16.2 us -> none  [the longest x1 9.38 us: body(): v[s]]
    slice x7 -> x3, local copies, waits for them, and re-layouts: 9.09 us -> 2.31 us  [the longest x1 1.02 us: body(): own[:base].reshape(3, heads_dev, HD, width)]
  transfers between devices with their start and end apart: 6 -> 0, of which waited for: 3 -> 0; matrix products, arithmetic and copies ran while one was open for 2% -> 0% of each run, Pallas kernels for 0% -> 0%
where the time goes in v3:
time: 355 us
  Pallas kernels  332 us (94%)
  local copies, waits for them, and re-layouts  12.9 us (4%)
  other arithmetic  9.71 us (3%)
    pallas_call x1, Pallas kernels, call_backward(): pl.pallas_call(functools.partial(backward_layer, count, data_count, heads...  174 us
    pallas_call x1, Pallas kernels, call_layer(): pl.pallas_call(functools.partial(forward_layer, count, heads_dev, block),...  158 us

profile of v3, /device:TPU:0, one launch (start us, length us, event | category | flops | bytes accessed | tf_op | source)
XLA Modules:
  0.0 355.1 jit_solution(7339271441049693299)
XLA Ops:
  0.7 0.7 constant_dynamic-update-slice_fusion.1.q_bias
  1.3 0.7 constant_dynamic-update-slice_fusion.v_bias
  2.0 0.0 copy-done.3
  2.0 0.6 copy-done.2
  2.6 158.0 %forward_layer.1 = (bf16[3,2048,512]{2,1,0:T(8,128)(2,1)}, bf16[4,384,512]{2,1,0:T(8,128)(2,1)}, bf16[3,4,512,128]{3,2,1,0:T(8,128)(2,1)}, bf16[3,4,2048,128]{3,...) custom-call(s32[3]{0:T(128)} %lengths.3, ...), custom_call_target="tpu_custom_call" | custom-call | flops 120000004096 | bytes 62914560 | tf_op jit(solution)/shard_map/forward_layer/pallas_call | solution.py:350
  160.6 173.8 %backward_layer.1 = (f32[3,512,512]{2,1,0:T(8,128)}, bf16[2,1,2560,512]{3,2,1,0:T(8,128)(2,1)}, bf16[512,512]{1,0:T(8,128)(2,1)}) custom-call(s32[3]{0:T(128)} %lengths.3, s32[3]{0:T(128)} %pair_ids.3, bf16[3,2048,512]{2,1,0:T(8,128)(2,1)} %get-tuple-element.27.x_seq, bf16[4,384,512]{2,1,0:T(8,128)(2,1)} %get-tuple-element.28.weight, ...), custom_call_target="tpu_custom_call" | custom-call | flops 199999995904 | bytes 62914560 | tf_op jit(solution)/shard_map/backward_layer/pallas_call | solution.py:794
  334.4 0.7 slice.35
  335.1 0.5 bitcast_convert_fusion
  335.6 0.7 slice_convert_fusion.2
  336.3 0.6 fusion
  336.9 0.6 copy.32
  337.5 1.3 slice_convert_fusion.1
  338.9 1.0 slice.34
  339.9 1.6 dynamic-slice_convert_fusion
  341.5 0.1 copy.28
  341.6 1.2 copy.30
  342.8 4.9 %slice_convert_fusion = (f32[2048,512]{1,0:T(8,128)}, bf16[2048,512]{1,0:T(8,128)(2,1)S(1)}) fusion(bf16[5120,512]{1,0:T(8,128)(2,1)} %bitcast.39), kind=kLoop, calls=%fused_computation.1 | loop fusion | flops 1048576 | bytes 10485760 | tf_op jit(solution)/shard_map/convert_element_type | solution.py:874
  347.7 0.6 convert_bitcast_fusion
  348.3 0.0 copy-start.1
  348.3 2.7 copy.31
  351.0 0.0 copy-done.1
  351.0 1.1 copy.37
  352.1 1.3 copy-done
  353.4 1.7 copy.38
  (7 shorter events, 0.0 us)
Async XLA Ops:
  1.3 0.7 copy-start.3
  2.0 0.6 copy-start.2
  348.3 2.7 copy-start.1
  351.0 2.5 copy-start

commit v4 on v3

--- a/solution.py
+++ b/solution.py
@@ -46,7 +46,7 @@
 MESH = pl.DeviceIdType.MESH
 CONSTANT = pl.Buffered(1)
 PIECES = 8
-TAIL_POINTS = (0, 2, 3, 4, 6, 7, 8, 9, 11, 12)
+TAIL_POINTS = (0, 2, 3, 5, 7, 9, 10, 12, 12)
 
 
 class Relay:
@@ -342,7 +342,7 @@
     pairs = width // PAIR
     block = min(512, full)
     w_rows = -(-(heads_dev * 4 * HD + 16) // (16 * PIECES)) * 16 * PIECES
-    g_rows = -(-(2 * hidden + width + 16) // 1024) * 1024
+    g_rows = -(-(2 * hidden + width + 16) // 256) * 256
     in_smem = pl.BlockSpec(memory_space=pltpu.SMEM)
     per_seq = lambda: pl.BlockSpec((1, rows, width), lambda s, p: (s, 0, 0))
     per_pair = lambda *tail: pl.BlockSpec((1, 1) + tail, lambda s, p: (s, p, 0, 0))
@@ -448,8 +448,7 @@
             def add(r, _):
                 at = aligned(keep + r * step, step)
                 more = self.land[self.group, slot, aligned(landed + r * step, step), :]
-                self.data[self.group, slot, at, :] = (
-                    self.data[self.group, slot, at, :].astype(F32) + more.astype(F32)).astype(BF16)
+                self.data[self.group, slot, at, :] = self.data[self.group, slot, at, :] + more
                 return 0
 
             lax.fori_loop(0, size // step, add, 0)
@@ -467,17 +466,26 @@
         pl.semaphore_wait(self.free_sem.at[self.group, j], 1)
         self.back(j).start()
 
-    def events(self):
+    def events(self, line=None):
         doubling = [j for j in range(len(self.stages)) if self.stages[j][2]][::-1]
+        middle = line.events(self.start, self.size) if line else []
         run = [lambda: self.copy(0).start()]
         for j in range(len(self.stages)):
             def after(j=j):
                 self.finish(j)
                 if j + 1 < len(self.stages):
                     self.copy(j + 1).start()
-                elif doubling:
+                elif middle:
+                    middle[0]()
+                else:
                     self.back_start(doubling[0])
             run.append(after)
+        for i in range(1, len(middle)):
+            def after_line(i=i):
+                middle[i]()
+                if i + 1 == len(middle):
+                    self.back_start(doubling[0])
+            run.append(after_line)
         for i, j in enumerate(doubling):
             def after_back(i=i, j=j):
                 self.back(j).wait()
@@ -485,6 +493,71 @@
                     self.back_start(doubling[i + 1])
             run.append(after_back)
         return run
+
+
+class Line:
+    def __init__(self, data, land, group, landed, place, send_sem, recv_sem):
+        self.data, self.land, self.group, self.landed = data, land, group, landed
+        self.place, self.send_sem, self.recv_sem = place, send_sem, recv_sem
+        self.end = (place == 0) | (place == 3)
+        self.inner = (place == 1) | (place == 2)
+
+    def copy(self, step, target, start, size):
+        return pltpu.make_async_remote_copy(
+            src_ref=self.data.at[self.group, :, aligned(start, size)],
+            dst_ref=self.land.at[self.group, :, pl.ds(self.landed + step * size, size)],
+            send_sem=self.send_sem.at[self.group, step], recv_sem=self.recv_sem.at[self.group, step],
+            device_id={"mp": target}, device_id_type=MESH)
+
+    def events(self, start, size):
+        inward = jnp.where(self.place < 2, 1, 2)
+        across = jnp.where(self.place < 2, 2, 1)
+        outward = jnp.where(self.place < 2, 0, 3)
+        first = self.copy(0, inward, start, size)
+        second = self.copy(1, across, start, size)
+        third = self.copy(2, outward, start, size)
+        unit = row_step(size)
+
+        def take(step, add):
+            def move(r, _):
+                at = aligned(start + r * unit, unit)
+                more = self.land[self.group, 0, aligned(self.landed + step * size + r * unit, unit), :]
+                if add:
+                    more = self.data[self.group, 0, at, :] + more
+                self.data[self.group, 0, at, :] = more
+                return 0
+
+            lax.fori_loop(0, size // unit, move, 0)
+
+        def begin():
+            pl.when(self.end)(first.start)
+
+        def swap():
+            @pl.when(self.inner)
+            def _():
+                first.wait_recv()
+                take(0, True)
+                second.start()
+
+        def hand_back():
+            @pl.when(self.inner)
+            def _():
+                second.wait()
+                take(1, True)
+                third.start()
+
+        def close():
+            @pl.when(self.inner)
+            def _():
+                third.wait_send()
+
+            @pl.when(self.end)
+            def _():
+                first.wait_send()
+                third.wait_recv()
+                take(2, False)
+
+        return [begin, swap, hand_back, close]
 
 
 def bit_list(size):
@@ -506,7 +579,7 @@
                    token_grad, g_out, own_out,
                    a_buf, a_land, b_buf, b_land, b_parts, own_buf, parts, land, x_acc, dq_acc, delta_all,
                    w_acc, bias_acc, col_acc, table_acc,
-                   load_sem, a_send, a_recv, a_free, b_send, b_recv, s_send, s_recv, r_send, r_recv):
+                   load_sem, a_send, a_recv, a_free, l_send, l_recv, b_send, b_recv, s_send, s_recv, r_send, r_recv):
     seq, turn = pl.program_id(0), pl.program_id(1)
     seqs, pairs = token_grad.shape[0], weight.shape[0]
     rows, width = token_grad.shape[1], token_grad.shape[2]
@@ -520,12 +593,15 @@
     chunk = sum(jnp.where((place == m) & (turn == i), order[m][i], 0)
                 for m in range(count) for i in range(count))
 
+    in_line = count == 4
     a_sums = [
         Reducer(a_buf, a_land, g, a_buf.shape[2],
-                [("dp", b) for b in (data_bits, swapped)[g]] + [("mp", b) for b in place_bits],
+                [("dp", b) for b in (data_bits, swapped)[g]] + [("mp", b) for b in place_bits if not in_line],
                 where_at, a_send, a_recv, a_free)
         for g in range(2)]
-    a_events = [s.events() for s in a_sums]
+    a_events = [
+        a.events(Line(a_buf, a_land, g, a.landed, place, l_send, l_recv) if in_line else None)
+        for g, a in enumerate(a_sums)]
     b_sums = [
         Reducer(b_buf, b_land, g, b_buf.shape[2], [("dp", b) for b in (data_bits, swapped)[g]],
                 where_at, b_send, b_recv)
@@ -552,7 +628,7 @@
             @pl.when(go)
             def _():
                 await_part(s, c)
-                parts[s, c] = (parts[s, c].astype(F32) + land[s, c].astype(F32)).astype(BF16)
+                parts[s, c] = parts[s, c] + land[s, c]
                 send_part(s, c, downward).start()
 
     def conclude(s):
@@ -623,7 +699,7 @@
         bias_acc[1:2, lanes] += jnp.sum(dv.astype(F32), axis=0, keepdims=True)
         return 0
 
-    lax.fori_loop(0, pairs, pair_step, 0)
+    lax.fori_loop(0, pairs, pair_step, 0, unroll=4)
 
     @pl.when(turn < count - 1)
     def _():
@@ -781,7 +857,11 @@
             landed += size
         return landed, size
 
-    a_landed, _ = landing(a_rows, len(data_bits) + len(place_bits))
+    if count == 4:
+        a_landed, strip = landing(a_rows, len(data_bits))
+        a_landed += 3 * strip
+    else:
+        a_landed, _ = landing(a_rows, len(data_bits) + len(place_bits))
     b_landed, strip = landing(slot_rows, len(data_bits))
     a_stages, b_stages = len(data_bits) + len(place_bits), len(data_bits)
     tail_points = TAIL_POINTS if (count, data_count) == (4, 8) else None
@@ -821,7 +901,7 @@
             pltpu.VMEM((8, width), F32),
             pltpu.VMEM((16, width), F32),
             dma((2,)), dma((2, 2 * a_stages)), dma((2, 2 * a_stages)),
-            pltpu.SemaphoreType.REGULAR((2, a_stages)),
+            pltpu.SemaphoreType.REGULAR((2, a_stages)), dma((2, 3)), dma((2, 3)),
             dma((2, b_stages)), dma((2, b_stages)),
             dma((seqs, count)), dma((seqs, count + 1)),
             dma((count - 1 + b_stages,)), dma((count - 1 + b_stages,)),
@@ -833,6 +913,64 @@
         name="backward_layer",
     )(lengths, pair_ids, x_all, weight, q, k, v, att_t, lse, grad, mixed_grad,
       g_all.reshape(2, 1, a_rows, width))
+
+
+def finish(place_ref, sums, own, token_in, result_in, last_grad, in_grad, small_sums, out_grad,
+           qkv_grad, q_bias_grad, v_bias_grad, table, token_out, result_out, *, heads_dev, hidden):
+    part = pl.program_id(0)
+    width = own.shape[1]
+    place = place_ref[0]
+    last_grad[...] = sums[pl.ds(pl.multiple_of(part * width, width), width), :].astype(F32)
+    in_grad[...] = sums[pl.ds(pl.multiple_of(hidden + part * width, width), width), :].astype(F32)
+    token_out[...] = token_in[...]
+    result_out[...] = result_in[...]
+
+    @pl.when(part == 0)
+    def _():
+        base = heads_dev * 3 * HD
+        out_rows = out_grad.shape[0]
+        out_grad[...] = sums[
+            pl.ds(pl.multiple_of(2 * hidden + place * out_rows, out_rows), out_rows), :].astype(F32)
+        small_sums[...] = sums[2 * hidden + width:2 * hidden + width + 16, :].astype(F32)[:8]
+        turned = own[:base, :].astype(F32).T
+        parts = []
+        for h in range(heads_dev):
+            for j in range(3):
+                lo = (j * heads_dev + h) * HD
+                parts.append(turned[:, lo:lo + HD])
+        qkv_grad[...] = jnp.concatenate(parts, axis=1)
+        rows = own[base:base + 16, :].astype(F32)
+        q_bias_grad[...] = rows[0:1]
+        v_bias_grad[...] = rows[1:2]
+        table[...] = own[base + 16:base + 32, :].astype(F32)[:table.shape[0]]
+
+
+def call_finish(place, sums, own, token_grad, result, heads_dev, hidden, table_rows):
+    seqs, rows, width = token_grad.shape
+    parts = hidden // width
+    base = heads_dev * 3 * HD
+    out_rows = heads_dev * HD
+    shape = jax.ShapeDtypeStruct
+    strip = lambda: pl.BlockSpec((seqs, rows // parts, width), lambda i, *_: (0, i, 0))
+    return pl.pallas_call(
+        functools.partial(finish, heads_dev=heads_dev, hidden=hidden),
+        grid_spec=pltpu.PrefetchScalarGridSpec(
+            num_scalar_prefetch=1,
+            grid=(parts,),
+            in_specs=[fixed(sums.shape), fixed(own.shape), strip(), strip()],
+            out_specs=[pl.BlockSpec((width, width), lambda i, *_: (i, 0)),
+                       pl.BlockSpec((width, width), lambda i, *_: (0, i)),
+                       fixed((8, width)), fixed((out_rows, width)), fixed((width, base)),
+                       fixed((1, width)), fixed((1, width)), fixed((table_rows, width)),
+                       strip(), strip()],
+        ),
+        out_shape=[shape((hidden, width), F32), shape((width, hidden), F32), shape((8, width), F32),
+                   shape((out_rows, width), F32), shape((width, base), F32), shape((1, width), F32),
+                   shape((1, width), F32), shape((table_rows, width), F32),
+                   shape(token_grad.shape, F32), shape(result.shape, BF16)],
+        compiler_params=pltpu.CompilerParams(vmem_limit_bytes=VMEM_LIMIT),
+        name="finish",
+    )(place, sums, own, token_grad, result)
 
 
 def body(
@@ -870,27 +1008,18 @@
         att_grad, mixed_grad, g_all)
 
     hidden = ffn_in_weight.shape[1]
-    g_sum = g_sum.reshape(-1, width)
-    g_last_sum = g_sum[:hidden].astype(F32)
-    g_in_sum = jnp.transpose(
-        g_sum[hidden:2 * hidden].reshape(hidden // width, width, width), (1, 0, 2)
-    ).reshape(width, hidden).astype(F32)
-    out_rows = out_weight.shape[0]
-    g_out_own = lax.dynamic_slice_in_dim(
-        g_sum, 2 * hidden + place[0] * out_rows, out_rows).astype(F32)
-    small = g_sum[2 * hidden + width:2 * hidden + width + 8].astype(F32)
+    (g_last_sum, g_in_sum, small, g_out_own, qkv_sum, qb_sum, vb_sum, table_sum, tokens_grad,
+     result) = call_finish(
+        place, g_sum.reshape(-1, width), own, tokens_grad, result, heads_dev, hidden, table_rows)
     at = hidden // width
-    base = heads_dev * 3 * HD
-    qkv_sum = jnp.transpose(
-        own[:base].reshape(3, heads_dev, HD, width), (3, 1, 0, 2)).reshape(width, base).astype(F32)
-    bias_rows = lax.dynamic_slice_in_dim(own[base:base + 2], place[0] * bias_len, bias_len, axis=1)
+    own_bias = lambda v: lax.dynamic_slice_in_dim(v[0], place[0] * bias_len, bias_len)
     return (
         jnp.transpose(result, (1, 0, 2)),
         jnp.transpose(tokens_grad, (1, 0, 2)),
-        own[base + 16:base + 16 + table_rows].astype(F32),
+        table_sum,
         qkv_sum,
-        bias_rows[0].astype(F32),
-        bias_rows[1].astype(F32),
+        own_bias(qb_sum),
+        own_bias(vb_sum),
         g_out_own,
         small[at + 1],
         g_in_sum,

time: 355 us -> 327 us (0.921)
  Pallas kernels: 332 us -> 320 us
  other arithmetic: 9.71 us -> 0 us
  local copies, waits for them, and re-layouts: 12.9 us -> 5.81 us
    pallas_call x1, Pallas kernels: 174 us -> 153 us  [call_backward(): pl.pallas_call(functools.partial(backward_layer, count, data_count, heads...]
    pallas_call x0 -> x1, Pallas kernels: none -> 9.43 us  [call_finish(): pl.pallas_call(functools.partial(finish, heads_dev=heads_dev, hidden=hidd...]
    convert_element_type x5 -> x0, other arithmetic: 9.14 us -> none  [the longest x1 4.94 us: body(): g_last_sum = g_sum[:hidden].astype(F32)]
    unnamed x13 -> x6, local copies, waits for them, and re-layouts: 6.46 us -> 1.9 us
where the time goes in v4:
time: 327 us
  Pallas kernels  320 us (98%)
  local copies, waits for them, and re-layouts  5.81 us (2%)
    pallas_call x1, Pallas kernels, call_layer(): pl.pallas_call(functools.partial(forward_layer, count, heads_dev, block),...  158 us
    pallas_call x1, Pallas kernels, call_backward(): pl.pallas_call(functools.partial(backward_layer, count, data_count, heads...  153 us
    pallas_call x1, Pallas kernels, call_finish(): pl.pallas_call(functools.partial(finish, heads_dev=heads_dev, hidden=hidd...  9.43 us

profile of v4, /device:TPU:0, one launch (start us, length us, event | category | flops | bytes accessed | tf_op | source)
XLA Modules:
  0.0 326.5 jit_solution(7818815484808416728)
XLA Ops:
  0.7 0.7 constant_dynamic-update-slice_fusion.1.q_bias
  1.3 0.0 copy-start.1
  1.3 0.7 constant_dynamic-update-slice_fusion.v_bias
  2.0 0.0 copy-done.1
  2.0 0.0 copy-start
  2.0 0.6 copy-done
  2.6 157.9 %forward_layer.1 = (bf16[3,2048,512]{2,1,0:T(8,128)(2,1)}, bf16[4,384,512]{2,1,0:T(8,128)(2,1)}, bf16[3,4,512,128]{3,2,1,0:T(8,128)(2,1)}, bf16[3,4,2048,128]{3,...) custom-call(s32[3]{0:T(128)} %lengths.3, ...), custom_call_target="tpu_custom_call" | custom-call | flops 120000004096 | bytes 62914560 | tf_op jit(solution)/shard_map/forward_layer/pallas_call | solution.py:350
  160.5 152.7 %backward_layer.1 = (f32[3,512,512]{2,1,0:T(8,128)}, bf16[2,1,2432,512]{3,2,1,0:T(8,128)(2,1)}, bf16[512,512]{1,0:T(8,128)(2,1)}) custom-call(s32[3]{0:T(128)} %lengths.3, s32[3]{0:T(128)} %pair_ids.3, bf16[3,2048,512]{2,1,0:T(8,128)(2,1)} %get-tuple-element.36.x_seq, bf16[4,384,512]{2,1,0:T(8,128)(2,1)} %get-tuple-element.37.weight, ...), custom_call_target="tpu_custom_call" | custom-call | flops 199999995904 | bytes 62914560 | tf_op jit(solution)/shard_map/backward_layer/pallas_call | solution.py:874
  313.2 9.4 %finish.1 = (f32[2048,512]{1,0:T(8,128)}, f32[512,2048]{1,0:T(8,128)}, f32[8,512]{1,0:T(8,128)}, f32[128,512]{1,0:T(8,128)}, f32[512,384]{1,0:T(8,128)}, /*index...) custom-call(s32[1]{0:T(128)} %bitcast.place_ref, ...), custom_call_target="tpu_custom_call" | custom-call | tf_op jit(solution)/shard_map/finish/pallas_call | solution.py:955
  322.6 1.2 fusion
  323.8 1.4 fusion.2
  325.2 0.7 slice_bitcast_fusion
  325.9 0.6 copy.26
  (2 shorter events, 0.0 us)
Async XLA Ops:
  1.3 0.7 copy-start.1
  2.0 0.6 copy-start

commit v5 on v4

--- a/solution.py
+++ b/solution.py
@@ -14,7 +14,7 @@
 LOG2E = math.log2(math.e)
 F32 = jnp.float32
 BF16 = jnp.bfloat16
-VMEM_LIMIT = 56 * 1024 * 1024
+VMEM_LIMIT = 60 * 1024 * 1024
 
 
 def nn(a, b):
@@ -46,6 +46,7 @@
 MESH = pl.DeviceIdType.MESH
 CONSTANT = pl.Buffered(1)
 PIECES = 8
+UNROLL = 4
 TAIL_POINTS = (0, 2, 3, 5, 7, 9, 10, 12, 12)
 
 
@@ -103,62 +104,68 @@
     return index + bit - 2 * bit * ((index // bit) % 2)
 
 
-def forward_layer(count, heads_dev, block,
+def near_first(count):
+    return [order[::-1] for order in far_first(count)]
+
+
+def forward_layer(count, heads_dev,
                   lengths, pair_ids, tok, embed, cot, qkv_w, q_bias, v_bias, out_w, b_out,
                   w_in, b_in, w_last, b_last,
                   x_out, w_out, q_out, k_out, v_out, att_t_out, lse_out,
                   result, mixed_grad, att_grad, g_all,
-                  x_all, w_all, w_o, biases, s_all, acc, att_rows_all, grads, grad_rows,
-                  x_send, x_recv, x_copy, w_send, w_recv, plane_send, plane_recv):
-    seq, pair = pl.program_id(0), pl.program_id(1)
+                  x_all, w_all, w_o, bias_land, biases, acc, stats, att_rows_all, grads, grad_rows,
+                  x_send, x_recv, x_copy, w_send, w_recv, plane_send, plane_recv, bias_send, bias_recv):
+    seq, turn = pl.program_id(0), pl.program_id(1)
     seqs, pairs = tok.shape[0], w_out.shape[0]
     rows, width = tok.shape[1], tok.shape[2]
-    full = count * rows
     hidden = w_in.shape[1]
     base = heads_dev * 4 * HD
-    piece_rows = w_all.shape[1] // PIECES
+    piece_rows = base // PIECES
     place, data_at = lax.axis_index("mp"), lax.axis_index("dp")
-    last_step = (seq == seqs - 1) & (pair == pairs - 1)
+    order = near_first(count)
+    chunk = sum(jnp.where((place == m) & (turn == i), order[m][i], 0)
+                for m in range(count) for i in range(count))
 
     def x_relay(s):
         return Relay(
             place, count,
-            lambda chunk: x_all.at[s, pl.ds(pl.multiple_of(chunk * rows, rows), rows)],
+            lambda c: x_all.at[s, pl.ds(pl.multiple_of(c * rows, rows), rows)],
             lambda downward, step: x_send.at[s, downward * (count - 1) + step],
-            lambda chunk: x_recv.at[s, chunk])
-
-    low_bits = [(data_at // bit) % 2 for bit in (4, 2, 1)]
-    piece = low_bits[0] + 2 * low_bits[1] + 4 * low_bits[2]
+            lambda c: x_recv.at[s, c])
+
+    core, near_x, near_y = [(data_at // bit) % 2 for bit in (1, 2, 4)]
+    piece = near_x + 2 * near_y + 4 * core
 
     def w_span(start, size):
         return pl.ds(pl.multiple_of(start * piece_rows, piece_rows), size * piece_rows)
 
     w_relay = Relay(
-        place, count, lambda chunk: w_all.at[chunk, w_span(piece, 1)],
+        place, count, lambda c: w_all.at[c, w_span(piece, 1)],
         lambda downward, step: w_send.at[downward * (count - 1) + step],
-        lambda chunk: w_recv.at[chunk])
-    partners = [flip(data_at, bit) for bit in (4, 2, 1)]
-    spans = [w_span(piece, 1), w_span(2 * low_bits[1] + 4 * low_bits[2], 2), w_span(4 * low_bits[2], 4)]
+        lambda c: w_recv.at[c])
+    partners = [flip(data_at, 2), flip(data_at, 4), flip(flip(data_at, 2), 4), flip(data_at, 1)]
 
     def plane(stage):
+        span = w_span(4 * core, 4) if stage == 3 else w_span(piece, 1)
         copies = []
         for k in range(1, count):
             source = (place + k) % count
             copies.append(pltpu.make_async_remote_copy(
-                src_ref=w_all.at[source, spans[stage]], dst_ref=w_all.at[source, spans[stage]],
+                src_ref=w_all.at[source, span], dst_ref=w_all.at[source, span],
                 send_sem=plane_send.at[stage, k - 1], recv_sem=plane_recv.at[stage, k - 1],
                 device_id={"dp": partners[stage]}, device_id_type=MESH))
         return copies
 
-    def plane_start(stage):
-        for copy in plane(stage):
-            copy.start()
-
-    def plane_wait(stage):
-        for copy in plane(stage):
-            copy.wait()
-
-    @pl.when((seq == 0) & (pair == 0))
+    def bias_copies():
+        copies = []
+        for k in range(1, count):
+            copies.append(pltpu.make_async_remote_copy(
+                src_ref=bias_land.at[0], dst_ref=bias_land.at[k],
+                send_sem=bias_send.at[k - 1], recv_sem=bias_recv.at[k - 1],
+                device_id={"mp": (place + k) % count}, device_id_type=MESH))
+        return copies
+
+    @pl.when((seq == 0) & (turn == 0))
     def _():
         greet(place, count, partners)
         turned = qkv_w[...].T
@@ -168,38 +175,47 @@
                 parts.append(turned[(h * 3 + j) * HD:(h * 3 + j + 1) * HD])
         w_all[place, 0:heads_dev * 3 * HD, :] = jnp.concatenate(parts, axis=0)
         w_all[place, heads_dev * 3 * HD:base, :] = out_w[...]
-        first = lax.broadcasted_iota(jnp.int32, (w_all.shape[1] - base, width), 0)
-        w_all[place, base:, :] = jnp.where(
-            first == 0, q_bias[...].astype(F32),
-            jnp.where(first == 1, v_bias[...].astype(F32), 0.0)).astype(BF16)
+        line = lax.broadcasted_iota(jnp.int32, bias_land.shape[1:], 0)
+        bias_land[0] = jnp.where(
+            line == 0, q_bias[...].astype(F32),
+            jnp.where(line == 1, v_bias[...].astype(F32), 0.0)).astype(BF16)
+        await_greetings(count, partners)
+        w_relay.advance(0)
+        for copy in bias_copies():
+            copy.start()
+        own = pl.ds(pl.multiple_of(place * rows, rows), rows)
         for s in range(seqs):
             row = embed[pl.ds(pair_ids[s], 1), :]
-            own = pl.ds(pl.multiple_of(place * rows, rows), rows)
             x_all[s, own, :] = (tok[s].astype(F32) + row).astype(BF16)
-        await_greetings(count, partners)
-        w_relay.advance(0)
         if count > 2:
             w_relay.advance(1)
         x_relay(0).advance(0)
         for step in range(2 if count > 2 else 1, count):
             w_relay.advance(step)
-        plane_start(0)
-        plane_wait(0)
-        plane_start(1)
-        if count > 2:
-            x_relay(0).advance(1)
-        plane_wait(1)
-        plane_start(2)
-        for step in range(2, count - 1):
-            x_relay(0).advance(step)
+        across = [plane(stage) for stage in range(3)]
+        for copies in across:
+            for copy in copies:
+                copy.start()
         grads[...] = jnp.zeros_like(grads)
         grad_rows[...] = jnp.zeros_like(grad_rows)
-        plane_wait(2)
+        for copies in across:
+            for copy in copies:
+                copy.wait()
+        for copy in plane(3):
+            copy.start()
+        for copy in bias_copies():
+            copy.wait()
+        for p in range(pairs):
+            if heads_dev == 2:
+                both = bias_land[(place + count - p) % count].astype(F32)
+            else:
+                both = jnp.concatenate(
+                    [bias_land[(place + count - 2 * p - half) % count].astype(F32) for half in range(2)],
+                    axis=1)
+            biases[:, p * PAIR:(p + 1) * PAIR] = both
+        for copy in plane(3):
+            copy.wait()
         w_relay.drain()
-        total = jnp.zeros((16, width), F32)
-        for m in range(count):
-            total += w_all[m, base:base + 16, :].astype(F32)
-        biases[...] = total
         for p in range(pairs):
             if heads_dev == 2:
                 w_out[p] = w_all[p, 0:3 * PAIR, :]
@@ -216,72 +232,84 @@
     def hbm_copy(s):
         return pltpu.make_async_copy(x_all.at[s], x_out.at[s], x_copy.at[s])
 
-    @pl.when(pair == 0)
-    def _():
-        x_relay(seq).advance(count - 1)
+    for t in range(1, count):
+        @pl.when((seq == 0) & (turn == t))
+        def _():
+            x_relay(0).advance(t)
+    for t in range(2, count - 1):
+        @pl.when((seq >= 1) & (turn == t - 1))
+        def _():
+            x_relay(seq).advance(t)
+    if count > 2:
+        @pl.when((seq >= 1) & (turn == count - 1))
+        def _():
+            x_relay(seq).advance(count - 1)
+
+    ahead = jnp.where(seq == 0, max(count - 2, 0), max(count - 3, 0))
+
+    @pl.when((turn == ahead) & (seq + 1 < seqs))
+    def _():
+        x_relay(seq + 1).advance(0)
+
+    length = lengths[seq]
+    own = pl.ds(pl.multiple_of(place * rows, rows), rows)
+    at = pl.ds(pl.multiple_of(chunk * rows, rows), rows)
+
+    @pl.when(turn == 0)
+    def _():
+        acc[...] = jnp.zeros_like(acc)
+        line = lax.broadcasted_iota(jnp.int32, stats.shape, 1)
+        stats[...] = jnp.where(line < 2, NEGATIVE, 0.0)
+
+        def query_step(p, _):
+            lanes = pl.ds(pl.multiple_of(p * PAIR, PAIR), PAIR)
+            q_pair = (nt(x_all[seq, own, :], w_out[p, 0:PAIR, :]) + biases[0:1, lanes]).astype(BF16)
+            q_out[0, p] = q_pair * BF16(HD ** -0.5)
+            return 0
+
+        lax.fori_loop(0, pairs, query_step, 0)
+
+    for p in range(pairs):
+        kv = nt(x_all[seq, at, :], w_out[p, PAIR:3 * PAIR, :])
+        k_out[0, p, at, :] = kv[:, :PAIR].astype(BF16)
+        v_out[0, p, at, :] = (kv[:, PAIR:] + biases[1:2, p * PAIR:(p + 1) * PAIR]).astype(BF16)
+
+    def pair_step(p, _):
+        k_blk, v_blk, q_pair = k_out[0, p, at, :], v_out[0, p, at, :], q_out[0, p]
+        keep = (lax.broadcasted_iota(jnp.int32, (rows, rows), 0) + chunk * rows) < length
+        scores = [jnp.where(keep, nt(k_blk, one_head(q_pair, h)), NEGATIVE) for h in range(2)]
+        before = [stats[p, h:h + 1, :] for h in range(2)]
+        tops = [jnp.maximum(before[h], jnp.max(scores[h], axis=0, keepdims=True) * LOG2E) for h in range(2)]
+        probs = [jnp.exp2(scores[h] * LOG2E - tops[h]) for h in range(2)]
+        added = tn(v_blk, jnp.concatenate([pr.astype(BF16) for pr in probs], axis=1))
+        for h in range(2):
+            half = slice(h * HD, (h + 1) * HD)
+            shrink = jnp.exp2(before[h] - tops[h])
+            stats[p, h:h + 1, :] = tops[h]
+            stats[p, 2 + h:3 + h, :] = (
+                stats[p, 2 + h:3 + h, :] * shrink + jnp.sum(probs[h], axis=0, keepdims=True))
+            acc[p, half, :] = acc[p, half, :] * shrink + added[half, h * rows:(h + 1) * rows]
+        return 0
+
+    lax.fori_loop(0, pairs, pair_step, 0, unroll=UNROLL)
+
+    @pl.when(turn == count - 1)
+    def _():
+        hbm_copy(seq).start()
 
         @pl.when(seq + 1 < seqs)
         def _():
-            x_relay(seq + 1).advance(0)
-        hbm_copy(seq).start()
-
-    length = lengths[seq]
-    lanes = pl.ds(pl.multiple_of(pair * PAIR, PAIR), PAIR)
-    own = pl.ds(pl.multiple_of(place * rows, rows), rows)
-    q_pair = (nt(x_all[seq, own, :], w_out[pair, 0:PAIR, :]) + biases[0:1, lanes]).astype(BF16)
-    q_pair = q_pair * BF16(HD ** -0.5)
-    q_out[0, 0] = q_pair
-    q_heads = [one_head(q_pair, 0), one_head(q_pair, 1)]
-    v_row = biases[1:2, lanes]
-
-    def score_step(j, tops):
-        at = pl.ds(pl.multiple_of(j * block, block), block)
-        kv = nt(x_all[seq, at, :], w_out[pair, PAIR:3 * PAIR, :])
-        k_blk = kv[:, :PAIR].astype(BF16)
-        k_out[0, 0, at, :] = k_blk
-        v_out[0, 0, at, :] = (kv[:, PAIR:] + v_row).astype(BF16)
-        keep = (lax.broadcasted_iota(jnp.int32, (block, rows), 0) + j * block) < length
-        new = []
-        for h in range(2):
-            s = nt(k_blk, q_heads[h]) * LOG2E
-            s = jnp.where(keep, s, NEGATIVE)
-            s_all[h, at, :] = s
-            new.append(jnp.maximum(tops[h], fold8(s, jnp.max)))
-        return tuple(new)
-
-    start = jnp.full((8, rows), NEGATIVE, F32)
-    tops = lax.fori_loop(0, full // block, score_step, (start, start))
-    tops = [jnp.max(t, axis=0, keepdims=True) for t in tops]
-    acc[...] = jnp.zeros_like(acc)
-
-    def value_step(j, sums):
-        at = pl.ds(pl.multiple_of(j * block, block), block)
-        v_blk = v_out[0, 0, at, :]
-        new = []
-        for h in range(2):
-            p = jnp.exp2(s_all[h, at, :] - tops[h])
-            new.append(sums[h] + fold8(p, jnp.sum))
-            acc[h] += tn(v_blk, p.astype(BF16))
-        return tuple(new)
-
-    zero = jnp.zeros((8, rows), F32)
-    sums = lax.fori_loop(0, full // block, value_step, (zero, zero))
-    sums = [jnp.sum(t, axis=0, keepdims=True) for t in sums]
-    att_t = jnp.concatenate([acc[h, h * HD:(h + 1) * HD, :] * (1.0 / sums[h]) for h in range(2)], axis=0)
-    att_t_out[0, 0] = att_t
-    att_rows_all[:, lanes] = att_t.T.astype(BF16)
-    lse_out[0, 0] = jnp.concatenate(
-        [tops[h] + jnp.log2(sums[h]) for h in range(2)] + [jnp.zeros((6, rows), F32)], axis=0)
-
-    for step in range(1, count - 1):
-        after = max(0, (step * pairs) // (count - 2) - 1)
-
-        @pl.when((pair == after) & (seq + 1 < seqs))
-        def _():
-            x_relay(seq + 1).advance(step)
-
-    @pl.when(pair == pairs - 1)
-    def _():
+            x_relay(seq + 1).advance(1)
+        for p in range(pairs):
+            total = stats[p, 2:4, :]
+            inverse = 1.0 / total
+            att_t = jnp.concatenate(
+                [acc[p, h * HD:(h + 1) * HD, :] * inverse[h:h + 1] for h in range(2)], axis=0)
+            att_t_out[0, p] = att_t
+            att_rows_all[:, p * PAIR:(p + 1) * PAIR] = att_t.T.astype(BF16)
+            lse_out[0, p] = jnp.concatenate(
+                [stats[p, 0:2, :] + jnp.log2(total), jnp.zeros((6, rows), F32)], axis=0)
+
         cot_rows = cot[0]
         att_rows = att_rows_all[...]
         row = embed[pl.ds(pair_ids[seq], 1), :]
@@ -313,7 +341,7 @@
         grads[2 * hidden:, :] += tn(att_rows, back_low)
         att_grad[0] = nt(back_low, w_o[...]).astype(BF16)
 
-    @pl.when(last_step)
+    @pl.when((seq == seqs - 1) & (turn == count - 1))
     def _():
         def narrow(j, _):
             at = pl.ds(pl.multiple_of(j * width, width), width)
@@ -340,16 +368,14 @@
     heads_dev = qkv_w.shape[1] // (3 * HD)
     full = count * rows
     pairs = width // PAIR
-    block = min(512, full)
-    w_rows = -(-(heads_dev * 4 * HD + 16) // (16 * PIECES)) * 16 * PIECES
     g_rows = -(-(2 * hidden + width + 16) // 256) * 256
     in_smem = pl.BlockSpec(memory_space=pltpu.SMEM)
     per_seq = lambda: pl.BlockSpec((1, rows, width), lambda s, p: (s, 0, 0))
-    per_pair = lambda *tail: pl.BlockSpec((1, 1) + tail, lambda s, p: (s, p, 0, 0))
+    per_pair = lambda *tail: pl.BlockSpec((1, pairs) + tail, lambda s, p: (s, 0, 0, 0))
     shape = jax.ShapeDtypeStruct
     return pl.pallas_call(
-        functools.partial(forward_layer, count, heads_dev, block),
-        grid=(seqs, pairs),
+        functools.partial(forward_layer, count, heads_dev),
+        grid=(seqs, count),
         in_specs=[in_smem, in_smem, fixed(tok.shape), fixed(embed.shape), per_seq(), fixed(qkv_w.shape),
                   fixed(q_bias.shape), fixed(v_bias.shape), fixed(out_w.shape), fixed(b_out.shape),
                   fixed(w_in.shape), fixed(b_in.shape), fixed(w_last.shape), fixed(b_last.shape)],
@@ -372,11 +398,12 @@
         ],
         scratch_shapes=[
             pltpu.VMEM((seqs, full, width), BF16),
-            pltpu.VMEM((count, w_rows, width), BF16),
+            pltpu.VMEM((count, heads_dev * 4 * HD, width), BF16),
             pltpu.VMEM((width, width), BF16),
+            pltpu.VMEM((count, 16, heads_dev * HD), BF16),
             pltpu.VMEM((16, width), F32),
-            pltpu.VMEM((2, full, rows), F32),
-            pltpu.VMEM((2, PAIR, rows), F32),
+            pltpu.VMEM((pairs, PAIR, rows), F32),
+            pltpu.VMEM((pairs, 8, rows), F32),
             pltpu.VMEM((rows, width), BF16),
             pltpu.VMEM((2 * hidden + width, width), F32),
             pltpu.VMEM((8, width), F32),
@@ -385,8 +412,10 @@
             pltpu.SemaphoreType.DMA((seqs,)),
             pltpu.SemaphoreType.DMA((2 * (count - 1),)),
             pltpu.SemaphoreType.DMA((count,)),
-            pltpu.SemaphoreType.DMA((3, count - 1)),
-            pltpu.SemaphoreType.DMA((3, count - 1)),
+            pltpu.SemaphoreType.DMA((4, count - 1)),
+            pltpu.SemaphoreType.DMA((4, count - 1)),
+            pltpu.SemaphoreType.DMA((count - 1,)),
+            pltpu.SemaphoreType.DMA((count - 1,)),
         ],
         cost_estimate=pl.CostEstimate(flops=120 * 10 ** 9, bytes_accessed=60 << 20,
                                       transcendentals=seqs * pairs * 2 * full * rows),
@@ -996,10 +1025,8 @@
     tok = jnp.transpose(tokens, (1, 0, 2))
     cot = jnp.transpose(cotangent, (1, 0, 2))
     bias_len = q_bias.shape[0]
-    spread = lambda v: lax.dynamic_update_slice(
-        jnp.zeros((1, width), BF16), v[None], (0, place[0] * bias_len))
     (x_all, w_pairs, q, k, v, att_t, lse, result, mixed_grad, att_grad, g_all) = call_layer(
-        count, lengths, pair_ids, tok, pair_embed, cot, qkv_weight, spread(q_bias), spread(v_bias),
+        count, lengths, pair_ids, tok, pair_embed, cot, qkv_weight, q_bias[None], v_bias[None],
         out_weight, out_bias[None], ffn_in_weight, ffn_in_bias[None], ffn_out_weight,
         ffn_out_bias[None])
     heads_dev = bias_len // HD

time: 327 us -> 314 us (0.960)
  Pallas kernels: 320 us -> 309 us
    pallas_call x1, Pallas kernels: 158 us -> 149 us  [call_layer(): pl.pallas_call(functools.partial(forward_layer, count, heads_dev), grid=(...]
where the time goes in v5:
time: 314 us
  Pallas kernels  309 us (98%)
  local copies, waits for them, and re-layouts  3.9 us (1%)
    pallas_call x1, Pallas kernels, call_backward(): pl.pallas_call(functools.partial(backward_layer, count, data_count, heads...  151 us
    pallas_call x1, Pallas kernels, call_layer(): pl.pallas_call(functools.partial(forward_layer, count, heads_dev), grid=(...  149 us
    pallas_call x1, Pallas kernels, call_finish(): pl.pallas_call(functools.partial(finish, heads_dev=heads_dev, hidden=hidd...  9.43 us

profile of v5, /device:TPU:0, one launch (start us, length us, event | category | flops | bytes accessed | tf_op | source)
XLA Modules:
  0.0 314.0 jit_solution(12523321568383994774)
XLA Ops:
  0.6 148.9 %forward_layer.1 = (bf16[3,2048,512]{2,1,0:T(8,128)(2,1)}, bf16[4,384,512]{2,1,0:T(8,128)(2,1)}, bf16[3,4,512,128]{3,2,1,0:T(8,128)(2,1)}, bf16[3,4,2048,128]{3,...) custom-call(s32[3]{0:T(128)} %lengths.3, ...), custom_call_target="tpu_custom_call" | custom-call | flops 120000004096 | bytes 62914560 | tf_op jit(solution)/shard_map/forward_layer/pallas_call | solution.py:376
  149.5 151.1 %backward_layer.1 = (f32[3,512,512]{2,1,0:T(8,128)}, bf16[2,1,2432,512]{3,2,1,0:T(8,128)(2,1)}, bf16[512,512]{1,0:T(8,128)(2,1)}) custom-call(s32[3]{0:T(128)} %lengths.3, s32[3]{0:T(128)} %pair_ids.3, bf16[3,2048,512]{2,1,0:T(8,128)(2,1)} %get-tuple-element.36.x_seq, bf16[4,384,512]{2,1,0:T(8,128)(2,1)} %get-tuple-element.37.weight, ...), custom_call_target="tpu_custom_call" | custom-call | flops 199999995904 | bytes 62914560 | tf_op jit(solution)/shard_map/backward_layer/pallas_call | solution.py:903
  300.7 9.4 %finish.1 = (f32[2048,512]{1,0:T(8,128)}, f32[512,2048]{1,0:T(8,128)}, f32[8,512]{1,0:T(8,128)}, f32[128,512]{1,0:T(8,128)}, f32[512,384]{1,0:T(8,128)}, /*index...) custom-call(s32[1]{0:T(128)} %bitcast.place_ref, ...), custom_call_target="tpu_custom_call" | custom-call | tf_op jit(solution)/shard_map/finish/pallas_call | solution.py:984
  310.1 0.7 slice_bitcast_fusion
  310.8 0.6 copy.26
  311.4 1.4 fusion
  312.8 1.2 dynamic-slice_bitcast_fusion

commit v6 on v5

--- a/solution.py
+++ b/solution.py
@@ -198,6 +198,7 @@
                 copy.start()
         grads[...] = jnp.zeros_like(grads)
         grad_rows[...] = jnp.zeros_like(grad_rows)
+        x_relay(0).advance(1)
         for copies in across:
             for copy in copies:
                 copy.wait()
@@ -232,22 +233,16 @@
     def hbm_copy(s):
         return pltpu.make_async_copy(x_all.at[s], x_out.at[s], x_copy.at[s])
 
-    for t in range(1, count):
-        @pl.when((seq == 0) & (turn == t))
-        def _():
-            x_relay(0).advance(t)
     for t in range(2, count - 1):
-        @pl.when((seq >= 1) & (turn == t - 1))
+        @pl.when(turn == t - 1)
         def _():
             x_relay(seq).advance(t)
     if count > 2:
-        @pl.when((seq >= 1) & (turn == count - 1))
+        @pl.when(turn == count - 1)
         def _():
             x_relay(seq).advance(count - 1)
 
-    ahead = jnp.where(seq == 0, max(count - 2, 0), max(count - 3, 0))
-
-    @pl.when((turn == ahead) & (seq + 1 < seqs))
+    @pl.when((turn == max(count - 3, 0)) & (seq + 1 < seqs))
     def _():
         x_relay(seq + 1).advance(0)
 
@@ -606,7 +601,7 @@
 def backward_layer(count, data_count, heads_dev, tail_points,
                    lengths, pair_ids, x_seq, weight, q_in, k_in, v_in, att_t, lse, grad_in, mixed_grad, g_in,
                    token_grad, g_out, own_out,
-                   a_buf, a_land, b_buf, b_land, b_parts, own_buf, parts, land, x_acc, dq_acc, delta_all,
+                   a_buf, a_land, b_buf, b_land, b_parts, own_buf, parts, land, both_all, x_acc, dq_acc, delta_all,
                    w_acc, bias_acc, col_acc, table_acc,
                    load_sem, a_send, a_recv, a_free, l_send, l_recv, b_send, b_recv, s_send, s_recv, r_send, r_recv):
     seq, turn = pl.program_id(0), pl.program_id(1)
@@ -701,8 +696,6 @@
     length = lengths[seq]
     at = aligned(chunk * rows, rows, rows)
     own = aligned(place * rows, rows, rows)
-    x_acc[...] = jnp.zeros_like(x_acc)
-
     def pair_step(p, _):
         lanes = aligned(p * PAIR, PAIR, PAIR)
         q_pair = q_in[0, p]
@@ -723,12 +716,14 @@
             dq_acc[p, h] += tn(k_blk, ds)
         dv = dv.astype(BF16)
         both = jnp.concatenate([dk.astype(BF16), dv], axis=1)
-        x_acc[...] += nn(both, weight[p, PAIR:, :])
-        w_acc[p, PAIR:, :] += tn(both, x_seq[0, at, :])
+        both_all[p] = both
         bias_acc[1:2, lanes] += jnp.sum(dv.astype(F32), axis=0, keepdims=True)
         return 0
 
     lax.fori_loop(0, pairs, pair_step, 0, unroll=4)
+    x_acc[...] = sum(nn(both_all[p], weight[p, PAIR:, :]) for p in range(pairs))
+    for p in range(pairs):
+        w_acc[p, PAIR:, :] += tn(both_all[p], x_seq[0, at, :])
 
     @pl.when(turn < count - 1)
     def _():
@@ -904,8 +899,8 @@
         functools.partial(backward_layer, count, data_count, heads_dev, tail_points),
         grid=(seqs, count),
         in_specs=[in_smem, in_smem, seq_block(x_all.shape, CONSTANT), fixed(weight.shape),
-                  seq_block(q.shape, CONSTANT), seq_block(k.shape, CONSTANT),
-                  seq_block(v.shape, CONSTANT), seq_block(att_t.shape, CONSTANT),
+                  seq_block(q.shape, CONSTANT), seq_block(k.shape),
+                  seq_block(v.shape), seq_block(att_t.shape, CONSTANT),
                   seq_block(lse.shape), seq_block(grad.shape), seq_block(mixed_grad.shape), in_hbm],
         out_specs=[fixed((seqs, rows, width)), in_hbm, fixed((slot_rows, width))],
         out_shape=[
@@ -922,6 +917,7 @@
             pltpu.VMEM((slot_rows, width), BF16),
             pltpu.VMEM((seqs, count, rows, width), BF16),
             pltpu.VMEM((seqs, count + 1, rows, width), BF16),
+            pltpu.VMEM((pairs, rows, 2 * PAIR), BF16),
             pltpu.VMEM((rows, width), F32),
             pltpu.VMEM((pairs, 2, PAIR, rows), F32),
             pltpu.VMEM((pairs, 8, rows), F32),
@@ -944,23 +940,27 @@
       g_all.reshape(2, 1, a_rows, width))
 
 
-def finish(place_ref, sums, own, token_in, result_in, last_grad, in_grad, small_sums, out_grad,
-           qkv_grad, q_bias_grad, v_bias_grad, table, token_out, result_out, *, heads_dev, hidden):
-    part = pl.program_id(0)
+def finish(place_ref, last_rows, in_rows, out_strip, vector_rows, own, token_in, result_in,
+           last_grad, in_grad, out_grad, out_bias, in_bias, last_bias,
+           qkv_grad, q_bias_grad, v_bias_grad, table, token_out, result_out, *, heads_dev):
     width = own.shape[1]
     place = place_ref[0]
-    last_grad[...] = sums[pl.ds(pl.multiple_of(part * width, width), width), :].astype(F32)
-    in_grad[...] = sums[pl.ds(pl.multiple_of(hidden + part * width, width), width), :].astype(F32)
+    last_grad[...] = last_rows[...].astype(F32)
+    in_grad[...] = in_rows[...].astype(F32)
     token_out[...] = token_in[...]
     result_out[...] = result_in[...]
 
-    @pl.when(part == 0)
+    @pl.when(pl.program_id(0) == pl.num_programs(0) - 1)
     def _():
         base = heads_dev * 3 * HD
-        out_rows = out_grad.shape[0]
-        out_grad[...] = sums[
-            pl.ds(pl.multiple_of(2 * hidden + place * out_rows, out_rows), out_rows), :].astype(F32)
-        small_sums[...] = sums[2 * hidden + width:2 * hidden + width + 16, :].astype(F32)[:8]
+        bias_len = heads_dev * HD
+        out_grad[...] = out_strip[...].astype(F32)
+        vectors = vector_rows[0:16, :].astype(F32)
+        parts = in_bias.shape[1] // width
+        for c in range(parts):
+            in_bias[:, c * width:(c + 1) * width] = vectors[c:c + 1]
+        last_bias[...] = vectors[parts:parts + 1]
+        out_bias[...] = vectors[parts + 1:parts + 2]
         turned = own[:base, :].astype(F32).T
         parts = []
         for h in range(heads_dev):
@@ -968,38 +968,48 @@
                 lo = (j * heads_dev + h) * HD
                 parts.append(turned[:, lo:lo + HD])
         qkv_grad[...] = jnp.concatenate(parts, axis=1)
-        rows = own[base:base + 16, :].astype(F32)
-        q_bias_grad[...] = rows[0:1]
-        v_bias_grad[...] = rows[1:2]
+        if heads_dev == 2:
+            rows = own[base:base + 16, pl.ds(pl.multiple_of(place * PAIR, PAIR), PAIR)].astype(F32)
+        else:
+            rows = own[base:base + 16, pl.ds(pl.multiple_of((place // 2) * PAIR, PAIR), PAIR)].astype(F32)
+            rows = jnp.where(place % 2 == 0, rows[:, :HD], rows[:, HD:])
+        q_bias_grad[...] = rows[0:1, :bias_len]
+        v_bias_grad[...] = rows[1:2, :bias_len]
         table[...] = own[base + 16:base + 32, :].astype(F32)[:table.shape[0]]
 
 
 def call_finish(place, sums, own, token_grad, result, heads_dev, hidden, table_rows):
     seqs, rows, width = token_grad.shape
-    parts = hidden // width
+    cut = width
+    tail = width // 2
+    parts = hidden // cut
     base = heads_dev * 3 * HD
     out_rows = heads_dev * HD
     shape = jax.ShapeDtypeStruct
     strip = lambda: pl.BlockSpec((seqs, rows // parts, width), lambda i, *_: (0, i, 0))
     return pl.pallas_call(
-        functools.partial(finish, heads_dev=heads_dev, hidden=hidden),
+        functools.partial(finish, heads_dev=heads_dev),
         grid_spec=pltpu.PrefetchScalarGridSpec(
             num_scalar_prefetch=1,
             grid=(parts,),
-            in_specs=[fixed(sums.shape), fixed(own.shape), strip(), strip()],
-            out_specs=[pl.BlockSpec((width, width), lambda i, *_: (i, 0)),
-                       pl.BlockSpec((width, width), lambda i, *_: (0, i)),
-                       fixed((8, width)), fixed((out_rows, width)), fixed((width, base)),
-                       fixed((1, width)), fixed((1, width)), fixed((table_rows, width)),
-                       strip(), strip()],
+            in_specs=[pl.BlockSpec((cut, width), lambda i, *_: (i, 0)),
+                      pl.BlockSpec((cut, width), lambda i, *_: (parts + i, 0)),
+                      pl.BlockSpec((out_rows, width), lambda i, at: (2 * hidden // out_rows + at[0], 0)),
+                      pl.BlockSpec((tail, width), lambda i, *_: ((2 * hidden + width) // tail, 0)),
+                      fixed(own.shape), strip(), strip()],
+            out_specs=[pl.BlockSpec((cut, width), lambda i, *_: (i, 0)),
+                       pl.BlockSpec((cut, width), lambda i, *_: (0, i)),
+                       fixed((out_rows, width)), fixed((1, width)), fixed((1, hidden)), fixed((1, width)),
+                       fixed((width, base)), fixed((1, out_rows)), fixed((1, out_rows)),
+                       fixed((table_rows, width)), strip(), strip()],
         ),
-        out_shape=[shape((hidden, width), F32), shape((width, hidden), F32), shape((8, width), F32),
-                   shape((out_rows, width), F32), shape((width, base), F32), shape((1, width), F32),
-                   shape((1, width), F32), shape((table_rows, width), F32),
-                   shape(token_grad.shape, F32), shape(result.shape, BF16)],
+        out_shape=[shape((hidden, width), F32), shape((width, hidden), F32), shape((out_rows, width), F32),
+                   shape((1, width), F32), shape((1, hidden), F32), shape((1, width), F32),
+                   shape((width, base), F32), shape((1, out_rows), F32), shape((1, out_rows), F32),
+                   shape((table_rows, width), F32), shape(token_grad.shape, F32), shape(result.shape, BF16)],
         compiler_params=pltpu.CompilerParams(vmem_limit_bytes=VMEM_LIMIT),
         name="finish",
-    )(place, sums, own, token_grad, result)
+    )(place, sums, sums, sums, sums, own, token_grad, result)
 
 
 def body(
@@ -1035,24 +1045,22 @@
         att_grad, mixed_grad, g_all)
 
     hidden = ffn_in_weight.shape[1]
-    (g_last_sum, g_in_sum, small, g_out_own, qkv_sum, qb_sum, vb_sum, table_sum, tokens_grad,
-     result) = call_finish(
+    (g_last_sum, g_in_sum, g_out_own, out_bias_sum, in_bias_sum, last_bias_sum, qkv_sum, qb_sum, vb_sum,
+     table_sum, tokens_grad, result) = call_finish(
         place, g_sum.reshape(-1, width), own, tokens_grad, result, heads_dev, hidden, table_rows)
-    at = hidden // width
-    own_bias = lambda v: lax.dynamic_slice_in_dim(v[0], place[0] * bias_len, bias_len)
     return (
         jnp.transpose(result, (1, 0, 2)),
         jnp.transpose(tokens_grad, (1, 0, 2)),
         table_sum,
         qkv_sum,
-        own_bias(qb_sum),
-        own_bias(vb_sum),
+        qb_sum.reshape(-1),
+        vb_sum.reshape(-1),
         g_out_own,
-        small[at + 1],
+        out_bias_sum.reshape(-1),
         g_in_sum,
-        small[:at].reshape(-1),
+        in_bias_sum.reshape(-1),
         g_last_sum,
-        small[at],
+        last_bias_sum.reshape(-1),
     )
 
 

time: 314 us -> 302 us (0.962)
  Pallas kernels: 309 us -> 301 us
  local copies, waits for them, and re-layouts: 3.9 us -> 0 us
    pallas_call x1, Pallas kernels: 149 us -> 142 us  [call_layer(): pl.pallas_call(functools.partial(forward_layer, count, heads_dev), grid=(...]
where the time goes in v6:
time: 302 us
  Pallas kernels  301 us (100%)
    pallas_call x1, Pallas kernels, call_backward(): pl.pallas_call(functools.partial(backward_layer, count, data_count, heads...  150 us
    pallas_call x1, Pallas kernels, call_layer(): pl.pallas_call(functools.partial(forward_layer, count, heads_dev), grid=(...  142 us
    pallas_call x1, Pallas kernels, call_finish(): pl.pallas_call(functools.partial(finish, heads_dev=heads_dev), grid_spec=...  9.27 us

profile of v6, /device:TPU:0, one launch (start us, length us, event | category | flops | bytes accessed | tf_op | source)
XLA Modules:
  0.0 301.9 jit_solution(3445616847425162845)
XLA Ops:
  0.6 141.7 %forward_layer.1 = (bf16[3,2048,512]{2,1,0:T(8,128)(2,1)}, bf16[4,384,512]{2,1,0:T(8,128)(2,1)}, bf16[3,4,512,128]{3,2,1,0:T(8,128)(2,1)}, bf16[3,4,2048,128]{3,...) custom-call(s32[3]{0:T(128)} %lengths.3, ...), custom_call_target="tpu_custom_call" | custom-call | flops 120000004096 | bytes 62914560 | tf_op jit(solution)/shard_map/forward_layer/pallas_call | solution.py:371
  142.3 150.2 %backward_layer.1 = (f32[3,512,512]{2,1,0:T(8,128)}, bf16[2,1,2432,512]{3,2,1,0:T(8,128)(2,1)}, bf16[512,512]{1,0:T(8,128)(2,1)}) custom-call(s32[3]{0:T(128)} %lengths.3, s32[3]{0:T(128)} %pair_ids.3, bf16[3,2048,512]{2,1,0:T(8,128)(2,1)} %get-tuple-element.38.x_seq, bf16[4,384,512]{2,1,0:T(8,128)(2,1)} %get-tuple-element.39.weight, ...), custom_call_target="tpu_custom_call" | custom-call | flops 199999995904 | bytes 62914560 | tf_op jit(solution)/shard_map/backward_layer/pallas_call | solution.py:898
  292.5 9.3 %finish.1 = (f32[2048,512]{1,0:T(8,128)}, f32[512,2048]{1,0:T(8,128)}, f32[128,512]{1,0:T(8,128)}, f32[1,512]{1,0:T(1,128)}, f32[1,2048]{1,0:T(1,128)}, /*index=...) custom-call(s32[1]{0:T(128)} %bitcast.place_ref, ...), custom_call_target="tpu_custom_call" | custom-call | tf_op jit(solution)/shard_map/finish/pallas_call | solution.py:990

commit v7 on v6

--- a/solution.py
+++ b/solution.py
@@ -184,12 +184,17 @@
         for copy in bias_copies():
             copy.start()
         own = pl.ds(pl.multiple_of(place * rows, rows), rows)
-        for s in range(seqs):
+
+        def embed_rows(s):
             row = embed[pl.ds(pair_ids[s], 1), :]
             x_all[s, own, :] = (tok[s].astype(F32) + row).astype(BF16)
+
+        embed_rows(0)
         if count > 2:
             w_relay.advance(1)
         x_relay(0).advance(0)
+        for s in range(1, seqs):
+            embed_rows(s)
         for step in range(2 if count > 2 else 1, count):
             w_relay.advance(step)
         across = [plane(stage) for stage in range(3)]
@@ -803,6 +808,8 @@
         for b in b_sums:
             b.copy(0).start()
         tail_k = [k for k in range(count - 2, 0, -1) if slots[k] >= count]
+        if tail_k:
+            combine(last, tail_k.pop(0))
         for j in range(stages):
             for b in b_sums:
                 b.finish(j)
@@ -828,10 +835,9 @@
             scatter(k).start()
         for k in tail_k:
             combine(last, k)
-        for e in in_tail:
+        for e in in_tail[:-1]:
             for events in a_events:
                 events[e]()
-        store().start()
         for k in range(1, count):
             scatter(k).wait()
         home = b_buf[mine, place % half, aligned(start, strip), :].astype(F32)
@@ -851,6 +857,11 @@
         for j in reversed(range(stages)):
             back(j).start()
             back(j).wait()
+            if j == stages - 1:
+                for e in in_tail[-1:]:
+                    for events in a_events:
+                        events[e]()
+                store().start()
         own_out[...] = own_buf[...]
         conclude(last)
         store().wait()

time: 302 us -> 301 us (level)
  no operation moved by 1% of the time
where the time goes in v7:
time: 301 us
  Pallas kernels  300 us (100%)
    pallas_call x1, Pallas kernels, call_backward(): pl.pallas_call(functools.partial(backward_layer, count, data_count, heads...  149 us
    pallas_call x1, Pallas kernels, call_layer(): pl.pallas_call(functools.partial(forward_layer, count, heads_dev), grid=(...  142 us
    pallas_call x1, Pallas kernels, call_finish(): pl.pallas_call(functools.partial(finish, heads_dev=heads_dev), grid_spec=...  9.27 us

profile of v7, /device:TPU:0, one launch (start us, length us, event | category | flops | bytes accessed | tf_op | source)
XLA Modules:
  0.0 301.2 jit_solution(10783076527880700644)
XLA Ops:
  0.6 141.7 %forward_layer.1 = (bf16[3,2048,512]{2,1,0:T(8,128)(2,1)}, bf16[4,384,512]{2,1,0:T(8,128)(2,1)}, bf16[3,4,512,128]{3,2,1,0:T(8,128)(2,1)}, bf16[3,4,2048,128]{3,...) custom-call(s32[3]{0:T(128)} %lengths.3, ...), custom_call_target="tpu_custom_call" | custom-call | flops 120000004096 | bytes 62914560 | tf_op jit(solution)/shard_map/forward_layer/pallas_call | solution.py:376
  142.3 149.4 %backward_layer.1 = (f32[3,512,512]{2,1,0:T(8,128)}, bf16[2,1,2432,512]{3,2,1,0:T(8,128)(2,1)}, bf16[512,512]{1,0:T(8,128)(2,1)}) custom-call(s32[3]{0:T(128)} %lengths.3, s32[3]{0:T(128)} %pair_ids.3, bf16[3,2048,512]{2,1,0:T(8,128)(2,1)} %get-tuple-element.38.x_seq, bf16[4,384,512]{2,1,0:T(8,128)(2,1)} %get-tuple-element.39.weight, ...), custom_call_target="tpu_custom_call" | custom-call | flops 199999995904 | bytes 62914560 | tf_op jit(solution)/shard_map/backward_layer/pallas_call | solution.py:909
  291.7 9.3 %finish.1 = (f32[2048,512]{1,0:T(8,128)}, f32[512,2048]{1,0:T(8,128)}, f32[128,512]{1,0:T(8,128)}, f32[1,512]{1,0:T(1,128)}, f32[1,2048]{1,0:T(1,128)}, /*index=...) custom-call(s32[1]{0:T(128)} %bitcast.place_ref, ...), custom_call_target="tpu_custom_call" | custom-call | tf_op jit(solution)/shard_map/finish/pallas_call | solution.py:1001
